TPU v7x, 32 devices: a whole 2x2x4 slice. The times are simulated.
32 devices in a mesh: dp: 4 (over y, x), fsdp: 8 (over z, core).
Axes of the slice: x: 2, y: 2, z: 4, core: 2. Of those that a mesh axis runs over, the one named last changes fastest.
Arguments:
- tokens: bfloat16 [16384, 8192], P(('dp', 'fsdp')), may hold values from -6 to 6
- cotangent: bfloat16 [16384, 1024], P(('dp', 'fsdp')), may hold values from -6 to 6
- weight: bfloat16 [8192, 1024], P('fsdp'), may hold values from -0.0625 to 0.0625
- feedback: float32 [4, 8192, 1024], P('dp', 'fsdp'), may hold values from -24 to 24
- q_factor: float32 [1024, 64], replicated, may hold values from -6 to 6
Outputs:
- input_grad: bfloat16 [16384, 8192], P(('dp', 'fsdp'))
- q_next: float32 [1024, 64], replicated
- feedback_next: float32 [4, 8192, 1024], P('dp', 'fsdp')
All inputs are finite; a program needn't handle non-finite values.
Results may differ from a plain program's by a relative error of at most 0.012.
Values may be sent and summed in bfloat16 or wider, within the bound.
No kernel may reach another device: no remote copies, remote signals or barrier semaphores. Data moves between devices by JAX's collectives and lax.ppermute only.
A program may use at most 128 MiB of HBM per device.

v0:
```python
import math

import jax
import jax.numpy as jnp
from jax import lax
from jax.sharding import PartitionSpec as P

highest = lax.Precision.HIGHEST


def exact_dot(left, right):
    return jnp.dot(left, right, precision=highest, preferred_element_type=jnp.float32)


def lower_solve(lower_factor, right_side):
    return lax.linalg.triangular_solve(lower_factor, right_side, left_side=True, lower=True)


def per_device(tokens, cotangent, weight, feedback, q_factor):
    groups = lax.axis_size("dp")
    members = lax.axis_size("fsdp")
    tok_dev = tokens.shape[0]
    grad_scale = 1.0 / math.sqrt(tok_dev * members)
    product = lax.dot_general(
        cotangent,
        lax.all_gather(weight, "fsdp", axis=0, tiled=True),
        (((1,), (1,)), ((), ())),
        preferred_element_type=jnp.float32,
    )
    input_grad = product.astype(jnp.bfloat16)
    grad_rows = (
        lax.psum_scatter(
            lax.dot_general(
                tokens, cotangent, (((0,), (0,)), ((), ())), preferred_element_type=jnp.float32
            ).astype(jnp.bfloat16),
            "fsdp",
            scatter_dimension=0,
            tiled=True,
        ).astype(jnp.float32)
        * grad_scale
    )
    merged = feedback[0] + grad_rows
    p_local = exact_dot(merged, q_factor)
    p_share = (
        lax.psum_scatter(
            p_local.astype(jnp.bfloat16), "dp", scatter_dimension=0, tiled=True
        ).astype(jnp.float32)
        / groups
    )
    gram_sum = lax.psum(exact_dot(p_share.T, p_share), ("dp", "fsdp"))
    lower_factor = jnp.linalg.cholesky(gram_sum)
    hat_share = lower_solve(lower_factor, p_share.T).T
    p_hat = lax.all_gather(hat_share, "dp", axis=0, tiled=True)
    q_next = lax.psum(exact_dot(merged.T, p_hat), ("dp", "fsdp")) / groups
    feedback_next = merged - exact_dot(p_hat, q_next.T)
    return (input_grad, q_next, feedback_next[None])


def solution(mesh):
    placed = (
        P(("dp", "fsdp"), None),
        P(("dp", "fsdp"), None),
        P("fsdp", None),
        P("dp", "fsdp", None),
        P(),
    )
    return jax.shard_map(
        per_device,
        mesh=mesh,
        in_specs=placed,
        out_specs=(P(("dp", "fsdp"), None), P(), P("dp", "fsdp", None)),
        check_vma=False,
    )
```

profile of v0, /device:TPU:0, one launch (start us, length us, event | category | flops | bytes accessed | tf_op | source)
XLA Modules:
  0.0 524.5 jit_solution(1358258118301092593)
XLA Ops:
  7.2 0.0 copy-start
  7.2 0.0 reduce-scatter.3.cloned.1.call-start
  7.2 1.2 copy-done
  8.4 15.9 %convolution_convert_fusion = bf16[8192,1024]{1,0:T(8,128)(2,1)} fusion(bf16[512,8192]{1,0:T(8,128)(2,1)} %param.5, bf16[512,1024]{1,0:T(8,128)(2,1)S(1)} %copy-done), kind=kOutput, calls=%fused_computation | convolution fusion | flops 8598323200 | bytes 26214400 | tf_op jit(solution)/shard_map/dot_general | solution.py:33
  24.3 0.0 copy-start.3
  24.3 0.0 reduce-scatter.3.cloned.1.call-update
  24.3 0.0 reduce-scatter.5.cloned.1.call-start
  24.4 171.1 %reduce-scatter.3.cloned.1.call-done = bf16[1024,1024]{1,0:T(8,128)(2,1)} async-done(((bf16[8192,1024]{1,0:T(8,128)(2,1)}), bf16[1024,1024]{1,0:T(8,128)(2,1)}) %reduce-scatter.3.cloned.1.call-update) | async-done | bytes 2097168 | tf_op jit(solution)/shard_map/reduce_scatter | solution.py:32
  195.4 0.0 copy-done.3
  195.4 0.0 copy-start.1
  195.4 8.2 %convolution_convert_fusion.2 = bf16[1024,64]{0,1:T(8,128)(2,1)} fusion(f32[1024,64]{0,1:T(8,128)S(1)} %copy-done.3, f32[1,1024,1024]{2,1,0:T(8,128)} %param.8, bf16[1024,1024]{1,0:T(8,128)(2,1)} %reduce-scatter.3.cloned.1.call-done), kind=kOutput, calls=%fused_computation.4 | convolution fusion | flops 808517632 | bytes 6684672 | tf_op jit(solution)/shard_map/dot_general | solution.py:12
  203.6 0.0 reduce-scatter.5.cloned.1.call-update
  203.6 0.0 all-gather.2.cloned.1.call-start
  203.7 0.7 all-gather.2.cloned.1.call-update
  204.4 0.0 all-reduce.2.cloned.1.call-start
  204.4 21.5 %reduce-scatter.5.cloned.1.call-done = bf16[256,64]{0,1:T(8,128)(2,1)} async-done(((bf16[1024,64]{0,1:T(8,128)(2,1)}), bf16[256,64]{0,1:T(8,128)(2,1)}) %reduce-scatter.5.cloned.1.call-update) | async-done | bytes 32784 | tf_op jit(solution)/shard_map/reduce_scatter | solution.py:45
  226.0 1.0 fusion.2
  227.0 48.3 %psum.14 = f32[64,64]{0,1:T(8,128)S(1)} all-reduce(f32[64,64]{0,1:T(8,128)S(1)} %fusion.2), channel_id=1, replica_groups=mesh['dp'=4,'fsdp'=8] {'dp','fsdp'}, use_global_device_ids=true, to_apply=%region_2.0 | all-reduce | flops 4096 | bytes 32768 | tf_op jit(solution)/shard_map/psum | solution.py:50
  275.3 0.1 copy.9
  275.4 5.8 %cholesky.16 = f32[64,64]{1,0:T(8,128)S(1)} custom-call(f32[64,64]{1,0:T(8,128)S(1)} %fusion.5), custom_call_target="Cholesky" | custom-call | tf_op jit(solution)/shard_map/jit(cholesky)/cholesky | solution.py:51
  281.2 0.6 compare_reduce_fusion
  281.9 0.7 fusion.3
  282.5 4.9 custom-call.6
  287.4 1.0 fusion.1
  288.5 10.2 %all_gather.7 = f32[1024,64]{0,1:T(8,128)S(1)} all-gather(f32[256,64]{0,1:T(8,128)S(1)} %fusion.1), channel_id=1, replica_groups=mesh['dp'=4,'fsdp'=8] {'dp'}, dimensions={0}, use_global_device_ids=true | all-gather | bytes 327680 | tf_op jit(solution)/shard_map/all_gather | solution.py:53
  298.7 0.0 copy-done.1
  298.7 6.1 %fusion = f32[1024,64]{0,1:T(8,128)} fusion(f32[1024,64]{0,1:T(8,128)S(1)} %all_gather.7, f32[1,1024,1024]{2,1,0:T(8,128)} %param.8, bf16[1024,1024]{1,0:T(8,128)(2,1)S(1)} %copy-done.1), kind=kOutput, calls=%fused_computation.5 | convolution fusion | flops 808452096 | bytes 6815744 | tf_op jit(solution)/shard_map/dot_general | solution.py:12
  304.8 0.0 all-reduce.2.cloned.1.call-update
  304.8 74.9 %all-gather.2.cloned.1.call-done = bf16[8192,1024]{1,0:T(8,128)(2,1)} async-done(((bf16[1024,1024]{1,0:T(8,128)(2,1)}), bf16[8192,1024]{1,0:T(8,128)(2,1)}) %all-gather.2.cloned.1.call-update) | async-done | bytes 16777232 | tf_op jit(solution)/shard_map/all_gather | solution.py:26
  379.7 29.6 %convolution_convert_fusion.1 = bf16[512,8192]{1,0:T(8,128)(2,1)} fusion(bf16[512,1024]{1,0:T(8,128)(2,1)S(1)} %copy-done, bf16[8192,1024]{1,0:T(8,128)(2,1)} %all-gather.2.cloned.1.call-done), kind=kOutput, calls=%fused_computation.1 | convolution fusion | flops 8594128896 | bytes 26214400 | tf_op jit(solution)/shard_map/dot_general | solution.py:24
  409.4 100.6 %all-reduce.2.cloned.1.call-done = f32[1024,64]{0,1:T(8,128)} async-done(((f32[1024,64]{0,1:T(8,128)}), f32[1024,64]{0,1:T(8,128)}) %all-reduce.2.cloned.1.call-update) | async-done | bytes 262160 | tf_op jit(solution)/shard_map/psum | solution.py:54
  510.0 1.0 broadcast_multiply_fusion
  511.0 0.0 copy-start.2
  511.0 7.0 %subtract_bitcast_fusion = f32[1,1024,1024]{2,1,0:T(8,128)} fusion(f32[1024,64]{0,1:T(8,128)S(1)} %all_gather.7, f32[1024,64]{0,1:T(8,128)S(1)} %broadcast_multiply_fusion, bf16[1024,1024]{1,0:T(8,128)(2,1)S(1)} %copy-done.1, f32[1,1024,1024]{2,1,0:T(8,128)} %param.8), kind=kOutput, calls=%fused_computation.3 | convolution fusion | flops 809500672 | bytes 11010048 | tf_op jit(solution)/shard_map/dot_general | solution.py:12
  518.0 0.0 copy-done.2
  (2 shorter events, 0.0 us)
Async XLA Ops:
  7.2 1.2 copy-start
  7.2 188.3 %reduce-scatter.3.cloned.1.call-start = ((), (), s32[]{:S(2)}) async-start(), calls=%async_computation.3 | async-start | bytes 18874368 | tf_op jit(solution)/shard_map/reduce_scatter | solution.py:32
  24.3 171.1 %copy-start.3 = (f32[1024,64]{0,1:T(8,128)S(1)}, f32[1024,64]{0,1:T(8,128)}, u32[]{:S(2)}) copy-start(f32[1024,64]{0,1:T(8,128)} %param.9) | copy-start | bytes 786436
  24.3 201.6 %reduce-scatter.5.cloned.1.call-start = ((), (), s32[]{:S(2)}) async-start(), calls=%async_computation.4 | async-start | bytes 163840 | tf_op jit(solution)/shard_map/reduce_scatter | solution.py:45
  195.4 103.2 %copy-start.1 = (bf16[1024,1024]{1,0:T(8,128)(2,1)S(1)}, bf16[1024,1024]{1,0:T(8,128)(2,1)}, u32[]{:S(2)}) copy-start(bf16[1024,1024]{1,0:T(8,128)(2,1)} %reduce-scatter.3.cloned.1.call-done) | copy-start | bytes 6291460
  203.6 176.1 %all-gather.2.cloned.1.call-start = ((), (), s32[]{:S(2)}) async-start(), calls=%async_computation.2 | async-start | bytes 18874368 | tf_op jit(solution)/shard_map/all_gather | solution.py:26
  204.4 305.6 %all-reduce.2.cloned.1.call-start = ((), (), s32[]{:S(2)}) async-start(), calls=%async_computation.5 | async-start | bytes 524288 | tf_op jit(solution)/shard_map/psum | solution.py:54
  511.0 7.0 %copy-start.2 = (f32[1024,64]{0,1:T(8,128)}, f32[1024,64]{0,1:T(8,128)S(1)}, u32[]{:S(2)}) copy-start(f32[1024,64]{0,1:T(8,128)S(1)} %broadcast_multiply_fusion) | copy-start | bytes 786436
Sparse Core Ops, SparseCore 0:
  24.4 170.9 reduce-scatter.2
  203.8 22.1 reduce-scatter.4
  227.7 152.0 all-gather.1
  386.6 123.3 all-reduce.1
where the time goes:
time: 525 us
  waiting for transfers between devices  369 us (70%)
  matrix products  68.8 us (13%)
  blocking collectives  58.5 us (11%)
  between operations  13.8 us (3%)
  other arithmetic  13 us (2%)
    reduce_scatter x1, waiting for transfers between devices, per_device(): lax.psum_scatter(lax.dot_general(tokens, cotangent, (((0,), (0,)), ((), (...  171 us
    psum x1, waiting for transfers between devices, per_device(): q_next = lax.psum(exact_dot(merged.T, p_hat), ('dp', 'fsdp')) / groups  101 us
    all_gather x1, waiting for transfers between devices, per_device(): lax.all_gather(weight, 'fsdp', axis=0, tiled=True)  74.9 us
    psum x1, blocking collectives, per_device(): gram_sum = lax.psum(exact_dot(p_share.T, p_share), ('dp', 'fsdp'))  48.3 us
    dot_general x1, matrix products, per_device(): lax.dot_general(cotangent, lax.all_gather(weight, 'fsdp', axis=0, tiled=T...  29.6 us
    dot_general x4, matrix products, exact_dot(): jnp.dot(left, right, precision=highest, preferred_element_type=jnp.float32)  22.3 us
    reduce_scatter x1, waiting for transfers between devices, per_device(): lax.psum_scatter(p_local.astype(jnp.bfloat16), 'dp', scatter_dimension=0,...  21.5 us
    dot_general x1, matrix products, per_device(): lax.dot_general(tokens, cotangent, (((0,), (0,)), ((), ())), preferred_el...  15.9 us
  transfers between devices with their start and end apart: 4, of which 4 were waited for; matrix products, arithmetic and copies ran while one was open for 10% of the time, Pallas kernels for 0%

commit v1 on v0

v1 whole, which is shorter than its diff:
```python
import math

import jax
import jax.numpy as jnp
from jax import lax
from jax.experimental import pallas as pl
from jax.experimental.pallas import tpu as pltpu
from jax.sharding import PartitionSpec as P

AXES = ("dp", "fsdp")
f32 = jnp.float32
bf16 = jnp.bfloat16
highest = lax.Precision.HIGHEST
VMEM = 56 << 20


def cost(flops, moved):
    return pl.CostEstimate(flops=flops, bytes_accessed=moved, transcendentals=0)


def dot(left, right, dims, precision=None):
    return lax.dot_general(
        left, right, (dims, ((), ())), precision=precision, preferred_element_type=f32
    )


def crossed(left, right):
    return lax.dot_general(left, right, (((0,), (0,)), ((), ())), preferred_element_type=f32)


def times(left, right):
    return jnp.dot(left, right, preferred_element_type=f32)


def partials(c, start, tall, cot, other_cot, tokens, other, rows):
    tok, width = cot.shape
    chips = tokens.shape[1] // rows // 2
    tile = math.gcd(math.gcd(start, tall), min(512, rows // 2))
    steps = tall // tile

    def kernel(index, cot, other_cot, own, other, result):
        total = crossed(own[...], cot[...]) + crossed(other[...], other_cot[...])
        result[...] = total.astype(result.dtype)

    column = pl.BlockSpec(
        (tok, tile), lambda b, i, index: (0, (2 * b + index[0]) * (rows // tile) + start // tile + i)
    )
    return pl.pallas_call(
        kernel,
        grid_spec=pltpu.PrefetchScalarGridSpec(
            num_scalar_prefetch=1,
            grid=(chips, steps),
            in_specs=[whole(cot.shape), whole(other_cot.shape), column, column],
            out_specs=pl.BlockSpec((tile, width), lambda b, i, index: (b * steps + i, 0)),
        ),
        out_shape=jax.ShapeDtypeStruct((chips * tall, width), bf16),
        compiler_params=params(),
        cost_estimate=cost(4 * tok * width * tall * chips, 4 * chips * tall * (width + tok)),
    )(scalars(c), cot, other_cot, tokens, other)


def remove(feedback, hat, q):
    rows, width = feedback.shape
    rank = hat.shape[1]
    tile = rows // 2

    def kernel(feedback, hat, q, result):
        rank_part = jnp.dot(hat[...], q[...], precision=highest, preferred_element_type=f32)
        result[...] = feedback[...] - rank_part

    row = pl.BlockSpec((tile, width), lambda i: (i, 0))
    return pl.pallas_call(
        kernel,
        grid=(rows // tile,),
        in_specs=[row, pl.BlockSpec((tile, rank), lambda i: (i, 0)), whole(q.shape)],
        out_specs=row,
        out_shape=jax.ShapeDtypeStruct(feedback.shape, f32),
        compiler_params=params(),
        cost_estimate=cost(2 * rows * width * rank, 8 * rows * width),
    )(feedback, hat, q)


def finish(scale, start, gradient, base):
    tall, width = gradient.shape
    tile = math.gcd(start, tall)

    def kernel(gradient, base, result):
        result[...] = base[...] + scale * gradient[...].astype(f32)

    row = pl.BlockSpec((tile, width), lambda i: (start // tile + i, 0))
    return pl.pallas_call(
        kernel,
        grid=(tall // tile,),
        in_specs=[pl.BlockSpec((tile, width), lambda i: (i, 0)), row],
        out_specs=row,
        out_shape=jax.ShapeDtypeStruct(base.shape, f32),
        input_output_aliases={1: 0},
        compiler_params=params(),
        cost_estimate=cost(tall * width, 10 * tall * width),
    )(gradient, base)


def split(value):
    top = value.astype(bf16)
    return top, (value - top.astype(f32)).astype(bf16)


def scalars(*values):
    return jnp.stack([jnp.asarray(value, jnp.int32) for value in values])


def whole(shape):
    return pl.BlockSpec(shape, lambda *_: (0,) * len(shape))


def params():
    return pltpu.CompilerParams(vmem_limit_bytes=VMEM)


def left_part(scale, f, c, q_t, cot, tokens, feedback):
    rank, width = q_t.shape
    tok, depth = tokens.shape
    rows = feedback.shape[0]
    wide = 2 * rows
    half = depth // wide // 2

    def kernel(index, q_t, cot, tokens, feedback, sent, kept, factor):
        stage, j = pl.program_id(0), pl.program_id(1)
        side = jnp.where(stage == 0, 1 - index[1], index[1])

        @pl.when((stage == 0) & (j == 0))
        def _():
            top, low = split(q_t[...])
            nt = (((1,), (1,)), ((), ()))
            both = lax.dot_general(top, cot[...], nt, preferred_element_type=f32)
            both += lax.dot_general(low, cot[...], nt, preferred_element_type=f32)
            top, low = split(both * scale)
            factor[:rank] = top
            factor[rank:] = low

        both = times(factor[...], tokens[...])
        total = both[:rank] + both[rank:]
        mine = side * half + j == index[0] // 2
        column = pl.multiple_of(lax.rem(index[0], 2) * rows, 128)

        def store(ref):
            ref[...] = total.astype(ref.dtype)

            @pl.when(mine)
            def _():
                top, low = split(q_t[...])
                both = lax.dot_general(
                    jnp.concatenate([top, low], axis=0),
                    feedback[...].astype(bf16),
                    (((1,), (1,)), ((), ())),
                    preferred_element_type=f32,
                )
                here = ref[:, pl.ds(column, rows)].astype(f32)
                here += both[:rank] + both[rank:]
                ref[:, pl.ds(column, rows)] = here.astype(ref.dtype)

        @pl.when(stage == 0)
        def _():
            store(sent)

        @pl.when(stage == 1)
        def _():
            store(kept)

    def token_block(stage, j, index):
        return 0, jnp.where(stage == 0, 1 - index[1], index[1]) * half + j

    return pl.pallas_call(
        kernel,
        grid_spec=pltpu.PrefetchScalarGridSpec(
            num_scalar_prefetch=1,
            grid=(2, half),
            in_specs=[
                whole(q_t.shape),
                whole(cot.shape),
                pl.BlockSpec((tok, wide), token_block),
                whole(feedback.shape),
            ],
            out_specs=[
                pl.BlockSpec((rank, wide), lambda s, j, index: (0, jnp.where(s == 0, j, half - 1))),
                pl.BlockSpec((rank, wide), lambda s, j, index: (0, jnp.where(s == 0, 0, j))),
            ],
            scratch_shapes=[pltpu.VMEM((2 * rank, tok), bf16)],
        ),
        out_shape=[
            jax.ShapeDtypeStruct((rank, depth // 2), bf16),
            jax.ShapeDtypeStruct((rank, depth // 2), f32),
        ],
        compiler_params=params(),
        cost_estimate=cost(4 * rank * tok * depth, 2 * tok * depth + 4 * rows * width),
    )(scalars(f, c), q_t, cot, tokens, feedback)


def right_part(scale, f, c, p_all, tokens, cot, feedback):
    rank, depth = p_all.shape
    tok, width = cot.shape
    rows = feedback.shape[0]
    wide = 2 * rows
    steps = depth // wide
    half = width // 2

    def kernel(index, p_all, p_own, tokens, cot, feedback, sent, kept, total):
        step = pl.program_id(0)
        nt = (((1,), (1,)), ((), ()))
        term = lax.dot_general(p_all[...], tokens[...], nt, preferred_element_type=f32)

        @pl.when(step == 0)
        def _():
            total[...] = term

        @pl.when(step > 0)
        def _():
            total[...] += term

        @pl.when(step == steps - 1)
        def _():
            top, low = split(total[...])
            fb_top, fb_low = split(feedback[...])
            value = (times(top, cot[...]) + times(low, cot[...])) * scale
            value += times(p_own[...], fb_top) + times(p_own[...], fb_low)
            first, second = value[:, :half], value[:, half:]
            sent[...] = jnp.where(index[1] == 0, second, first)
            kept[...] = jnp.where(index[1] == 0, first, second)

    return pl.pallas_call(
        kernel,
        grid_spec=pltpu.PrefetchScalarGridSpec(
            num_scalar_prefetch=1,
            grid=(steps,),
            in_specs=[
                pl.BlockSpec((rank, wide), lambda i, index: (0, i)),
                pl.BlockSpec((rank, rows), lambda i, index: (0, index[0])),
                pl.BlockSpec((tok, wide), lambda i, index: (0, i)),
                whole(cot.shape),
                whole(feedback.shape),
            ],
            out_specs=[whole((rank, half))] * 2,
            scratch_shapes=[pltpu.VMEM((rank, tok), f32)],
        ),
        out_shape=[jax.ShapeDtypeStruct((rank, half), f32)] * 2,
        compiler_params=params(),
        cost_estimate=cost(2 * rank * tok * depth, 2 * tok * depth + 4 * rows * width),
    )(scalars(f, c), p_all, p_all, tokens, cot, feedback)


def on_core(function, side, shapes, *operands):
    if min(shape[-1] for shape, _ in shapes) % 128:
        return [x.astype(kind) for x, (_, kind) in zip(function(side, *operands), shapes)]

    def kernel(index, *refs):
        values = function(index[0], *[ref[...] for ref in refs[: len(operands)]])
        for ref, value in zip(refs[len(operands) :], values):
            ref[...] = value.astype(ref.dtype)

    return pl.pallas_call(
        kernel,
        grid_spec=pltpu.PrefetchScalarGridSpec(
            num_scalar_prefetch=1,
            grid=(1,),
            in_specs=[whole(x.shape) for x in operands],
            out_specs=[whole(shape) for shape, _ in shapes],
        ),
        out_shape=[jax.ShapeDtypeStruct(shape, kind) for shape, kind in shapes],
        compiler_params=params(),
        cost_estimate=cost(1, sum(x.size * x.dtype.itemsize for x in operands)),
    )(scalars(side), *operands)


def project_kernel(parts, table, cot, *refs):
    pieces = refs[: sum(parts)]
    result, token, tiles, sems = refs[-4:]
    step, steps = pl.program_id(0), pl.num_programs(0)
    slot = lax.rem(step, 2)
    wide = tiles.shape[3]

    def copy(k, slot, step):
        column = pl.multiple_of(table[step, k] * wide, 128)
        return pltpu.make_async_copy(
            tiles.at[slot, k], result.at[:, pl.ds(column, wide)], sems.at[slot, k]
        )

    @pl.when(step >= 2)
    def _():
        for k in range(len(parts)):
            copy(k, slot, step - 2).wait()

    at = 0
    for k, count in enumerate(parts):
        total, start = None, 0
        for piece in pieces[at : at + count]:
            depth = piece.shape[2]
            term = lax.dot_general(
                cot[:, start : start + depth],
                piece[0],
                (((1,), (1,)), ((), ())),
                preferred_element_type=f32,
            )
            total = term if total is None else total + term
            start += depth
        at += count
        tiles[slot, k] = total.astype(bf16)
        copy(k, slot, step).start()

    @pl.when(step == steps - 1)
    def _():
        token[...] = jnp.zeros(token.shape, token.dtype)
        for k in range(len(parts)):
            copy(k, slot, step).wait()

        @pl.when(steps > 1)
        def _():
            for k in range(len(parts)):
                copy(k, 1 - slot, step - 1).wait()


def project(result, depth, cot, pieces, table):
    count, wide, _ = pieces[0][0].shape
    tok, width = cot.shape
    if wide % 128:
        if result is None:
            result = jnp.zeros((tok, depth), bf16)
        for k, arrays in enumerate(pieces):
            full = jnp.concatenate(arrays, axis=2)
            for i in range(count):
                product = dot(cot, full[i], ((1,), (1,))).astype(bf16)
                result = lax.dynamic_update_slice_in_dim(
                    result, product, table[i, k] * wide, axis=1
                )
        return result, result[:8, :128].astype(f32)
    specs = [pl.BlockSpec((tok, width), lambda i, table: (0, 0))]
    operands = [table.astype(jnp.int32), cot]
    for arrays in pieces:
        for array in arrays:
            specs.append(pl.BlockSpec((1, wide, array.shape[2]), lambda i, table: (i, 0, 0)))
            operands.append(array)
    aliases = {}
    if result is not None:
        specs.append(pl.BlockSpec(memory_space=pl.ANY))
        aliases = {len(operands): 0}
        operands.append(result)
    parts = [len(arrays) for arrays in pieces]
    return pl.pallas_call(
        lambda *refs: project_kernel(parts, *refs),
        grid_spec=pltpu.PrefetchScalarGridSpec(
            num_scalar_prefetch=1,
            grid=(count,),
            in_specs=specs,
            out_specs=[pl.BlockSpec(memory_space=pl.ANY), whole((8, 128))],
            scratch_shapes=[
                pltpu.VMEM((2, len(parts), tok, wide), bf16),
                pltpu.SemaphoreType.DMA((2, len(parts))),
            ],
        ),
        out_shape=[jax.ShapeDtypeStruct((tok, depth), bf16), jax.ShapeDtypeStruct((8, 128), f32)],
        input_output_aliases=aliases,
        compiler_params=params(),
        cost_estimate=cost(2 * tok * width * wide * count * len(pieces), 2 * count * len(pieces) * wide * (width + tok)),
    )(*operands)


def per_device(tokens, cotangent, weight, feedback, q_factor):
    groups = lax.axis_size("dp")
    members = lax.axis_size("fsdp")
    chips = members // 2
    world = groups * members
    tok_dev, depth = tokens.shape
    rows, width = weight.shape
    d = lax.axis_index("dp")
    f = lax.axis_index("fsdp")
    flat = d * members + f
    z, c = f // 2, f % 2
    scale = 1.0 / math.sqrt(tok_dev * members)
    feedback = feedback[0]
    last = [None]

    def after(value):
        if last[0] is not None:
            value, _ = lax.optimization_barrier((value, last[0]))
        last[0] = value
        return value

    def gate(value):
        return lax.optimization_barrier((value, last[0]))[0]

    def swap(value, mask):
        return lax.ppermute(after(value), AXES, [(i, i ^ mask) for i in range(world)])

    def along(value, pairs):
        moves = [
            (g * members + a * 2 + core, g * members + b * 2 + core)
            for g in range(groups)
            for a, b in pairs
            for core in range(2)
        ]
        return lax.ppermute(after(value), AXES, moves)

    def paired(value, moves, odd=0):
        moves = [(a, b) for a, b in moves if (min(a, b) + odd) % 2 == 0]
        return along(value, moves) if moves else None

    results = {}

    def pick(index, parts):
        value = parts[0]
        for k in range(1, len(parts)):
            value = jnp.where(index == k, parts[k], value)
        return value

    def split_sum(sent, kept, kind):
        rank, wide = kept.shape
        got = swap(sent, 1)
        yield
        kept = gate(kept)
        wide //= groups

        def deal(place, kept, got):
            total = kept + got.astype(f32)
            parts = [total[:, k * wide : (k + 1) * wide] for k in range(groups)]
            return [pick(place ^ m, parts) for m in range(groups)]

        shapes = [((rank, wide), f32)] + [((rank, wide), kind)] * (groups - 1)
        kept, *sent = on_core(deal, d, shapes, kept, got)
        got = [swap(one, m * members) for m, one in enumerate(sent, 1)]
        yield
        kept = gate(kept)
        shapes = [((rank, wide), kind)]

        def add(_, kept, *got):
            for one in got:
                kept = kept + one.astype(f32)
            return [kept]

        (value,) = on_core(add, 0, shapes, kept, *got)
        terms = [swap(value, 2 * m) for m in range(1, chips)]
        yield
        terms = [gate(value)] + terms

        def pairs(_, *terms):
            terms = [term.astype(f32) for term in terms]
            while len(terms) > 1:
                terms = [a + b for a, b in zip(terms[::2], terms[1::2])]
            return terms

        return on_core(pairs, 0, shapes, *terms)[0]

    def join(value):
        for place, step, count in ((d, members, groups), (c, 1, 2)):
            others = [swap(value, m * step) for m in range(1, count)]
            yield
            value = gate(value)
            rank, wide = value.shape

            def beside(place, *terms, count=count):
                return [jnp.concatenate([pick(place ^ k, terms) for k in range(count)], axis=1)]

            shapes = [((rank, (count if wide % 128 == 0 else 1) * wide), value.dtype)]
            (value,) = on_core(beside, place, shapes, value, *others)
        return value

    def finish_of(generator):
        value = yield from generator
        return value

    other_cot, other = swap(cotangent, 1), swap(tokens, 1)

    def gradient():
        same_core = [[2 * a + core for a in range(chips)] for core in range(2)]
        parts = [(0, rows // 4), (rows // 4, rows - rows // 4)]
        summed = []
        for start, tall in parts:
            other_cot, other = results["other"]
            both = partials(c, start, tall, gate(cotangent), other_cot, tokens, other, rows)
            both = after(both)
            yield
            summed.append(
                lax.psum_scatter(
                    after(both), "fsdp", scatter_dimension=0, axis_index_groups=same_core, tiled=True
                )
            )
            yield
        result = results["low_rank"]
        for (start, _), part in zip(parts, summed):
            result = finish(scale, start, part, result)
            results["feedback"] = result
            yield

    def low_rank_chain():
        sent, kept = left_part(scale, f, c, q_factor.T, cotangent, tokens, feedback)
        sent = after(sent)
        results["other"] = after(other_cot), after(other)
        yield
        reduction = split_sum(sent, kept, bf16)
        p_sum = yield from reduction
        p_all = yield from join(p_sum)
        p_own = lax.dynamic_slice_in_dim(p_all, f * rows, rows, axis=1)
        z_part = right_part(scale, f, c, p_all, tokens, cotangent, feedback)
        reduction = split_sum(*z_part, f32)
        for _ in range(3):
            next(reduction)
            yield
        p_gated = gate(p_all)
        gram = dot(p_gated, p_gated, ((1,), (1,)))
        lower_factor = jnp.linalg.cholesky(gram)
        inverse = lax.linalg.triangular_solve(
            lower_factor, jnp.eye(gram.shape[0], dtype=f32), left_side=True, lower=True
        )
        inverse = after(inverse)
        yield
        z_sum = yield from finish_of(reduction)
        z_all = yield from join(z_sum)
        hat_own = dot(p_own.astype(f32), inverse, ((0,), (1,)), highest)
        q_next = dot(inverse, z_all, ((1,), (0,)), highest) / groups
        results["q_next"] = q_next.T
        results["low_rank"] = remove(feedback, hat_own, q_next)
        yield

    def weights():
        share = rows // groups
        piece = lax.dynamic_slice_in_dim(weight, d * share, share, axis=0)
        near, across = [piece], [piece]
        for h in range(chips - 1):
            moves = [(a, a + 1) for a in range(h, chips - 1)]
            moves += [(a + 1, a) for a in range(chips - 1 - h)]
            from_near, from_across = near[-1], across[-1]
            near.append(paired(from_across, moves))
            across.append(paired(from_near, moves, 1))
            if h == chips - 2:
                sibling = swap(weight, 1)
            yield
        toward = jnp.where(z % 2 == 0, 1, -1)
        count = jnp.where(z % 2 == 0, chips - 1 - z, z)
        slots, sources = [], []
        for k in range(1, chips):
            slot = near[k]
            for m in range(1, k, 2):
                slot = jnp.where(count == m, across[k - m], slot)
            slots.append(slot)
            sources.append(jnp.where(k <= count, z + toward * k, z - toward * (k - count)))
        slots, far = after(jnp.stack(slots)), jnp.stack(sources)
        yield
        shares, twins = {0: [slots]}, {}
        middle = width // 2
        for m in range(1, groups):
            low_bit = m & -m
            high_bit = 1 << (m.bit_length() - 1)
            if low_bit == high_bit:
                source = shares[m ^ low_bit]
                shares[m] = [swap(x, low_bit * members) for x in source]
                if m == 1:
                    twins[0] = [swap(slots, 1)]
            else:
                first = jnp.concatenate(shares[m ^ low_bit], axis=2)[:, :, :middle]
                second = jnp.concatenate(shares[m ^ high_bit], axis=2)[:, :, middle:]
                yield
                shares[m] = [
                    swap(first, low_bit * members),
                    swap(second, high_bit * members),
                ]
        for m in range(groups):
            if m not in twins and len(shares[m]) == 1:
                twins[m] = [swap(x, 1) for x in shares[m]]
        yield
        pieces = [[weight[None]], [sibling[None]]]
        result, token = project(
            None, depth, gate(cotangent), pieces, jnp.stack([f, f ^ 1])[None]
        )
        after(token)
        yield
        for m in range(groups):
            if m not in twins:
                twins[m] = [swap(x, 1) for x in shares[m]]
        pieces, table = [], []
        for m in range(groups):
            for core, arrays in ((c, shares[m]), (1 - c, twins[m])):
                pieces.append(arrays)
                table.append((far * 2 + core) * groups + (d ^ m))
        result, token = project(result, depth, gate(cotangent), pieces, jnp.stack(table, axis=1))
        results["input_grad"] = result
        after(token)
        yield

    chains = {"R": gradient(), "L": low_rank_chain(), "W": weights()}
    order = "WLWLLWLRWLRLLLRRLWLLWWLLW"
    for name in order:
        next(chains[name], None)
    for name in ("L", "W", "R"):
        for _ in chains[name]:
            pass
    return (results["input_grad"], results["q_next"], results["feedback"][None])


def solution(mesh):
    placed = (
        P(("dp", "fsdp"), None),
        P(("dp", "fsdp"), None),
        P("fsdp", None),
        P("dp", "fsdp", None),
        P(),
    )
    return jax.shard_map(
        per_device,
        mesh=mesh,
        in_specs=placed,
        out_specs=(P(("dp", "fsdp"), None), P(), P("dp", "fsdp", None)),
        check_vma=False,
    )
```

time: 525 us -> 243 us (0.46)
  waiting for transfers between devices: 369 us -> 55.2 us
  Pallas kernels: 0 us -> 92.5 us
  matrix products: 68.8 us -> 3.9 us
  blocking collectives: 58.5 us -> 0 us
  starting transfers between devices: 0.16 us -> 45.2 us
  local copies, waits for them, and re-layouts: 1.27 us -> 14.3 us
    reduce_scatter x2, waiting for transfers between devices: 193 us -> 0.02 us  [gradient(): lax.psum_scatter(after(both), 'fsdp', scatter_dimension=0, axis_index_gro...]
    psum x1 -> x0, waiting for transfers between devices: 101 us -> none  [per_device(): q_next = lax.psum(exact_dot(merged.T, p_hat), ('dp', 'fsdp')) / groups]
    pallas_call x0 -> x19, Pallas kernels: none -> 92.5 us  [the longest x2 20.3 us: project(): pl.pallas_call(lambda *refs: project_kernel(parts, *refs), grid_spec=pltp...]
    all_gather x1 -> x0, waiting for transfers between devices: 74.9 us -> none  [per_device(): lax.all_gather(weight, 'fsdp', axis=0, tiled=True)]
    dot_general x6 -> x3, matrix products: 67.8 us -> 3.69 us  [dot(): lax.dot_general(left, right, (dims, ((), ())), precision=precision, prefe...]
    ppermute x0 -> x39, waiting for transfers between devices: none -> 55.2 us  [the longest x34 46 us: swap(): lax.ppermute(after(value), AXES, [(i, i ^ mask) for i in range(world)])]
    psum x1 -> x0, blocking collectives: 48.3 us -> none  [per_device(): gram_sum = lax.psum(exact_dot(p_share.T, p_share), ('dp', 'fsdp'))]
    ppermute x0 -> x39, starting transfers between devices: none -> 45 us  [the longest x34 35.1 us: swap(): lax.ppermute(after(value), AXES, [(i, i ^ mask) for i in range(world)])]
  transfers between devices with their start and end apart: 4 -> 41, of which waited for: 4 -> 18; matrix products, arithmetic and copies ran while one was open for 10% -> 10% of each run, Pallas kernels for 0% -> 36%
where the time goes in v1:
time: 243 us; the launch traced here: 241 us
  Pallas kernels  92.5 us (38%)
  waiting for transfers between devices  55.2 us (23%)
  starting transfers between devices  45.2 us (19%)
  other arithmetic  15.8 us (7%)
  between operations  14.4 us (6%)
  local copies, waits for them, and re-layouts  14.3 us (6%)
  matrix products  3.9 us (2%)
    ppermute x34, waiting for transfers between devices, swap(): lax.ppermute(after(value), AXES, [(i, i ^ mask) for i in range(world)])  46 us
    ppermute x34, starting transfers between devices, swap(): lax.ppermute(after(value), AXES, [(i, i ^ mask) for i in range(world)])  35.1 us
    pallas_call x2, Pallas kernels, project(): pl.pallas_call(lambda *refs: project_kernel(parts, *refs), grid_spec=pltp...  20.3 us
    pallas_call x2, Pallas kernels, partials(): pl.pallas_call(kernel, grid_spec=pltpu.PrefetchScalarGridSpec(num_scalar_...  20.1 us
    pallas_call x10, Pallas kernels, on_core(): pl.pallas_call(kernel, grid_spec=pltpu.PrefetchScalarGridSpec(num_scalar_...  17.8 us
    pallas_call x1, Pallas kernels, right_part(): pl.pallas_call(kernel, grid_spec=pltpu.PrefetchScalarGridSpec(num_scalar_...  10.2 us
    ppermute x5, starting transfers between devices, along(): return lax.ppermute(after(value), AXES, moves)  9.81 us
    pallas_call x1, Pallas kernels, left_part(): pl.pallas_call(kernel, grid_spec=pltpu.PrefetchScalarGridSpec(num_scalar_...  9.65 us
  transfers between devices with their start and end apart: 41, of which 18 were waited for; matrix products, arithmetic and copies ran while one was open for 10% of the time, Pallas kernels for 36%

profile of v1, /device:TPU:0, one launch (start us, length us, event | category | flops | bytes accessed | tf_op | source)
XLA Modules:
  0.0 241.5 jit_solution(7589181216195144215)
XLA Ops:
  7.8 1.1 constant_dynamic-slice_fusion
  8.9 0.7 collective-permute-start.1
  9.6 5.9 %collective-permute-start = (bf16[256,1024]{1,0:T(8,128)(2,1)S(1)}, bf16[256,1024]{1,0:T(8,128)(2,1)S(1)}, u32[]{:S(2)}, u32[]{:S(2)}) collective-permute-start(bf16[256,1024]{1,0:T(8,128)(2,1)S(1)} %constant_dynamic-slice_fusion), channel_id=1, source_target_pairs={{0,2},{1,3},{4,6},{5,7},{2,0},{3,1},{6,4},{7,5},{8,10},{9,11},{12,... | collective-permute-start | bytes 1572872 | tf_op jit(solution)/shard_map/ppermute | solution.py:400
  16.1 9.6 %shard_map.76 = (bf16[64,4096]{1,0:T(8,128)(2,1)}, f32[64,4096]{1,0:T(8,128)}) custom-call(s32[2]{0:T(128)} %pad_add_fusion.1.index, f32[64,1024]{1,0:T(8,128)} %bitcast.40, bf16[512,1024]{1,0:T(8,128)(2,1)} %refs_1_.1, bf16[512,8192]{1,0:T(8,128)(2,1)} %own.3, f32[1024,1024]{1,0:T(8,128)} %bitcast.34), custom_call_target="tpu_custom_call" | custom-call | flops 1073741824 | bytes 12582912 | tf_op jit(solution)/shard_map/pallas_call | solution.py:173
  25.8 1.6 collective-permute-done
  28.0 1.3 collective-permute-start.4
  29.5 0.8 copy-done.4
  30.3 2.3 shard_map.77
  32.6 1.3 collective-permute-start.7
  33.9 2.5 %collective-permute-start.10 = (bf16[64,1024]{1,0:T(8,128)(2,1)}, bf16[64,1024]{1,0:T(8,128)(2,1)S(1)}, u32[]{:S(2)}, u32[]{:S(2)}) collective-permute-start(bf16[64,1024]{1,0:T(8,128)(2,1)} %get-tuple-element.97), channel_id=1, source_target_pairs={{0,24},{1,25},{2,26},{3,27},{4,28},{5,29},{6,30},{7,31},{8,16},{9,... | collective-permute-start | bytes 393224 | tf_op jit(solution)/shard_map/ppermute | solution.py:391
  37.5 7.7 %collective-permute-done.4 = bf16[256,1024]{1,0:T(8,128)(2,1)} collective-permute-done((bf16[256,1024]{1,0:T(8,128)(2,1)S(1)}, bf16[256,1024]{1,0:T(8,128)(2,1)}, u32[]{:S(2)}, u32[]{:S(2)}) %collective-permute-start.4) | collective-permute-done | bytes 524320 | tf_op jit(solution)/shard_map/ppermute | solution.py:400
  45.1 1.1 select_bitcast_fusion.1
  47.6 1.8 shard_map.78.refs_0_
  49.4 2.5 %collective-permute-start.13 = (bf16[64,1024]{1,0:T(8,128)(2,1)}, bf16[64,1024]{1,0:T(8,128)(2,1)S(1)}, u32[]{:S(2)}, u32[]{:S(2)}) collective-permute-start(bf16[64,1024]{1,0:T(8,128)(2,1)} %shard_map.78.refs_0_), channel_id=1, source_target_pairs={{0,6},{1,7},{2,4},{3,5},{4,2},{5,3},{6,0},{7,1},{8,14},{9,15},{10,... | collective-permute-start | bytes 393224 | tf_op jit(solution)/shard_map/ppermute | solution.py:391
  51.9 8.5 %collective-permute-start.12 = (bf16[64,1024]{1,0:T(8,128)(2,1)}, bf16[64,1024]{1,0:T(8,128)(2,1)S(1)}, u32[]{:S(2)}, u32[]{:S(2)}) collective-permute-start(bf16[64,1024]{1,0:T(8,128)(2,1)} %shard_map.78.refs_0_), channel_id=1, source_target_pairs={{0,4},{1,5},{2,6},{3,7},{4,0},{5,1},{6,2},{7,3},{8,12},{9,13},{10,... | collective-permute-start | bytes 393224 | tf_op jit(solution)/shard_map/ppermute | solution.py:391
  60.4 6.0 %shard_map.79 = bf16[1024,1024]{1,0:T(8,128)(2,1)} custom-call(s32[1]{0:T(128)} %bitcast.5.index, bf16[512,1024]{1,0:T(8,128)(2,1)} %refs_1_.1, bf16[512,1024]{1,0:T(8,128)(2,1)} %copy-done.1, bf16[512,8192]{1,0:T(8,128)(2,1)} %own.3, bf16[512,8192]{1,0:T(8,128)(2,1)} %collective-permute-done.2.other), custom_call_target="tpu_custom_call" | custom-call | flops 2147483648 | bytes 6291456 | tf_op jit(solution)/shard_map/pallas_call | solution.py:48
  66.5 1.2 pad_maximum_fusion.refs_2_
  67.7 1.8 collective-permute-done.12.refs_2_
  70.8 1.8 shard_map.80.refs_0_
  73.5 1.0 collective-permute-start.16
  74.5 2.0 collective-permute-start.15
  77.0 3.4 %collective-permute-done.16.refs_3_ = bf16[64,1024]{1,0:T(8,128)(2,1)S(1)} collective-permute-done((bf16[64,1024]{1,0:T(8,128)(2,1)S(1)}, bf16[64,1024]{1,0:T(8,128)(2,1)S(1)}, u32[]{:S(2)}, u32[]{:S(2)}) %collective-permute-start.16) | collective-permute-done | bytes 131104 | tf_op jit(solution)/shard_map/ppermute | solution.py:391
  80.4 1.3 collective-permute-done.15.refs_2_
  83.1 2.0 shard_map.81.refs_0_
  85.1 2.1 collective-permute-done.17.refs_1_
  87.2 0.8 copy-done.3
  88.0 2.2 shard_map.82.p_all.p_own
  90.2 10.2 %shard_map.83 = (f32[64,512]{1,0:T(8,128)}, f32[64,512]{1,0:T(8,128)}) custom-call(s32[2]{0:T(128)} %pad_add_fusion.1.index, bf16[64,8192]{1,0:T(8,128)(2,1)} %shard_map.82.p_all.p_own, bf16[64,8192]{1,0:T(8,128)(2,1)} %shard_map.82.p_all.p_own, bf16[512,8192]{1,0:T(8,128)(2,1)} %own.3, bf16[512,1024]{1,0:T(8,128)(2,1)} %refs_1_.1, f32[1024,1024]{1,0:T(8,128)} %bitcast.35), custom_call_target="tpu_custom_call" | custom-call | flops 536870912 | bytes 12582912 | tf_op jit(solution)/shard_map/pallas_call | solution.py:230
  100.6 1.4 collective-permute-done.18.refs_1_
  102.6 1.6 shard_map.84
  104.3 14.1 %shard_map.85 = bf16[3072,1024]{1,0:T(8,128)(2,1)} custom-call(s32[1]{0:T(128)} %bitcast.5.index, bf16[512,1024]{1,0:T(8,128)(2,1)} %refs_1_.1, bf16[512,1024]{1,0:T(8,128)(2,1)} %copy-done.1, bf16[512,8192]{1,0:T(8,128)(2,1)} %own.3, bf16[512,8192]{1,0:T(8,128)(2,1)} %collective-permute-done.2.other), custom_call_target="tpu_custom_call" | custom-call | flops 6442450944 | bytes 18874368 | tf_op jit(solution)/shard_map/pallas_call | solution.py:48
  119.1 1.0 collective-permute-start.21
  120.1 1.9 collective-permute-start.20
  122.6 1.3 collective-permute-done.21.refs_3_
  124.3 1.7 collective-permute-done.19.refs_1_
  126.6 1.4 shard_map.86.refs_0_
  128.6 1.5 collective-permute-start.22
  130.2 1.4 collective-permute-start.26
  132.4 5.8 %cholesky.17 = f32[64,64]{1,0:T(8,128)S(1)} custom-call(f32[64,64]{1,0:T(8,128)S(1)} %fusion.5), custom_call_target="Cholesky" | custom-call | tf_op jit(solution)/shard_map/jit(cholesky)/cholesky | solution.py:508
  139.6 4.9 %custom-call.6 = f32[1,64,64]{1,2,0:T(8,128)S(1)} custom-call(f32[1,64,64]{2,1,0:T(8,128)S(1)} %fusion.2), custom_call_target="InvertDiagBlocksLowerTriangular" | custom-call | tf_op jit(solution)/shard_map/triangular_solve | solution.py:509
  144.5 2.7 %collective-permute-start.24 = (f32[64,128]{1,0:T(8,128)S(1)}, f32[64,128]{1,0:T(8,128)S(1)}, u32[]{:S(2)}, u32[]{:S(2)}) collective-permute-start(f32[64,128]{1,0:T(8,128)S(1)} %copy-done.7), channel_id=1, source_target_pairs={{0,2},{1,3},{2,0},{3,1},{4,6},{5,7},{6,4},{7,5},{8,10},{9,11},{10,... | collective-permute-start | bytes 98312 | tf_op jit(solution)/shard_map/ppermute | solution.py:391
  147.5 3.2 %collective-permute-done.24.refs_1_ = f32[64,128]{1,0:T(8,128)S(1)} collective-permute-done((f32[64,128]{1,0:T(8,128)S(1)}, f32[64,128]{1,0:T(8,128)S(1)}, u32[]{:S(2)}, u32[]{:S(2)}) %collective-permute-start.24) | collective-permute-done | bytes 32800 | tf_op jit(solution)/shard_map/ppermute | solution.py:391
  151.4 1.4 shard_map.87.refs_0_
  152.8 10.1 %collective-permute-done.23.refs_6_ = bf16[3,256,1024]{2,1,0:T(8,128)(2,1)} collective-permute-done((bf16[3,256,1024]{2,1,0:T(8,128)(2,1)S(1)}, bf16[3,256,1024]{2,1,0:T(8,128)(2,1)}, u32[]{:S(2)}, u32[]{:S(2)}) %collective-permute-start.23) | collective-permute-done | bytes 1572896 | tf_op jit(solution)/shard_map/ppermute | solution.py:391
  162.9 2.1 slice.19
  165.0 1.3 collective-permute-start.28
  166.3 1.5 collective-permute-start.32
  167.8 1.2 slice.18
  169.0 0.7 collective-permute-start.27
  169.7 1.4 collective-permute-start.31
  171.1 13.8 %collective-permute-done.32.refs_3_ = f32[64,128]{1,0:T(8,128)S(1)} collective-permute-done((f32[64,128]{1,0:T(8,128)}, f32[64,128]{1,0:T(8,128)S(1)}, u32[]{:S(2)}, u32[]{:S(2)}) %collective-permute-start.32) | collective-permute-done | bytes 32800 | tf_op jit(solution)/shard_map/ppermute | solution.py:391
  184.9 2.8 %collective-permute-done.31.refs_2_ = f32[64,128]{1,0:T(8,128)S(1)} collective-permute-done((f32[64,128]{1,0:T(8,128)S(1)}, f32[64,128]{1,0:T(8,128)S(1)}, u32[]{:S(2)}, u32[]{:S(2)}) %collective-permute-start.31) | collective-permute-done | bytes 32800 | tf_op jit(solution)/shard_map/ppermute | solution.py:391
  187.6 1.1 collective-permute-done.30.refs_1_
  190.6 7.2 %shard_map.88 = (bf16[512,8192]{1,0:T(8,128)(2,1)}, f32[8,128]{1,0:T(8,128)}) custom-call(s32[1,2]{1,0:T(1,128)} %add_bitcast_fusion.refs_0_, bf16[512,1024]{1,0:T(8,128)(2,1)} %refs_1_.1, bf16[1,1024,1024]{2,1,0:T(8,128)(2,1)} %bitcast.41, bf16[1,1024,1024]{2,1,0:T(8,128)(2,1)} %bitcast.17.refs_3_), custom_call_target="tpu_custom_call" | custom-call | flops 2147483648 | bytes 6291456 | tf_op jit(solution)/shard_map/pallas_call | solution.py:347
  197.8 1.5 shard_map.89.refs_0_
  199.8 1.2 collective-permute-done.38.refs_1_
  201.3 0.7 stack.68.refs_0_
  202.0 1.3 fusion.hat
  203.3 1.7 shard_map.91
  205.0 2.0 convolution_multiply_fusion.q
  207.0 7.2 %shard_map.92.base = f32[1024,1024]{1,0:T(8,128)} custom-call(f32[1024,1024]{1,0:T(8,128)} %bitcast.36, f32[1024,64]{1,0:T(8,128)} %fusion.hat, f32[64,1024]{1,0:T(8,128)} %convolution_multiply_fusion.q), custom_call_target="tpu_custom_call" | custom-call | flops 134217728 | bytes 8388608 | tf_op jit(solution)/shard_map/pallas_call | solution.py:72
  214.3 13.1 %shard_map.90 = (bf16[512,8192]{1,0:T(8,128)(2,1)}, f32[8,128]{1,0:T(8,128)}) custom-call(s32[3,8]{1,0:T(4,128)} %stack.68.refs_0_, bf16[512,1024]{1,0:T(8,128)(2,1)} %refs_1_.1, bf16[3,256,1024]{2,1,0:T(8,128)(2,1)} %copy-done.2, bf16[3,256,1024]{2,1,0:T(8,128)(2,1)} %collective-permute-done.33.refs_3_, ...), custom_call_target="tpu_custom_call", output_to_operand_aliasing={{0}: (12, {})} | custom-call | flops 6442450944 | bytes 18874368 | tf_op jit(solution)/shard_map/pallas_call | solution.py:347
  227.4 2.5 %shard_map.93.base = f32[1024,1024]{1,0:T(8,128)} custom-call(bf16[256,1024]{1,0:T(8,128)(2,1)} %reduce-scatter.5.cloned.1.call-done.gradient, f32[1024,1024]{1,0:T(8,128)} %shard_map.92.base), custom_call_target="tpu_custom_call", output_to_operand_aliasing={{}: (1, {})} | custom-call | flops 262144 | bytes 2621440 | tf_op jit(solution)/shard_map/pallas_call | solution.py:91
  229.8 4.8 %shard_map.94 = f32[1024,1024]{1,0:T(8,128)} custom-call(bf16[768,1024]{1,0:T(8,128)(2,1)} %reduce-scatter.3.cloned.1.call-done.gradient, f32[1024,1024]{1,0:T(8,128)} %shard_map.93.base), custom_call_target="tpu_custom_call", output_to_operand_aliasing={{}: (1, {})} | custom-call | flops 786432 | bytes 7864320 | tf_op jit(solution)/shard_map/pallas_call | solution.py:91
  (124 shorter events, 18.0 us)
Async XLA Ops:
  7.2 220.2 %reduce-scatter.5.cloned.1.call-start = ((), (), s32[]{:S(2)}) async-start(), calls=%async_computation.3 | async-start | bytes 2621440 | tf_op jit(solution)/shard_map/reduce_scatter | solution.py:481
  7.2 18.5 %collective-permute-start.2 = (bf16[512,8192]{1,0:T(8,128)(2,1)}, bf16[512,8192]{1,0:T(8,128)(2,1)}, u32[]{:S(2)}, u32[]{:S(2)}) collective-permute-start(bf16[512,8192]{1,0:T(8,128)(2,1)} %own.3), channel_id=1, source_target_pairs={{0,1},{1,0},{2,3},{3,2},{4,5},{5,4},{6,7},{7,6},{8,9},{9,8},{10,11... | collective-permute-start | bytes 25165832 | tf_op jit(solution)/shard_map/ppermute | solution.py:391
  7.7 18.0 %collective-permute-start.3 = (bf16[512,1024]{1,0:T(8,128)(2,1)}, bf16[512,1024]{1,0:T(8,128)(2,1)S(1)}, u32[]{:S(2)}, u32[]{:S(2)}) collective-permute-start(bf16[512,1024]{1,0:T(8,128)(2,1)} %refs_1_.1), channel_id=1, source_target_pairs={{0,1},{1,0},{2,3},{3,2},{4,5},{5,4},{6,7},{7,6},{8,9},{9,8},{10,11... | collective-permute-start | bytes 3145736 | tf_op jit(solution)/shard_map/ppermute | solution.py:391
  8.9 16.9 %collective-permute-start.1 = (bf16[256,1024]{1,0:T(8,128)(2,1)S(1)}, bf16[256,1024]{1,0:T(8,128)(2,1)S(1)}, u32[]{:S(2)}, u32[]{:S(2)}) collective-permute-start(bf16[256,1024]{1,0:T(8,128)(2,1)S(1)} %constant_dynamic-slice_fusion), channel_id=1, source_target_pairs={{2,4},{3,5},{4,2},{5,3},{10,12},{11,13},{12,10},{13,11},{18,20},{1... | collective-permute-start | bytes 1572872 | tf_op jit(solution)/shard_map/ppermute | solution.py:400
  9.6 17.7 %collective-permute-start = (bf16[256,1024]{1,0:T(8,128)(2,1)S(1)}, bf16[256,1024]{1,0:T(8,128)(2,1)S(1)}, u32[]{:S(2)}, u32[]{:S(2)}) collective-permute-start(bf16[256,1024]{1,0:T(8,128)(2,1)S(1)} %constant_dynamic-slice_fusion), channel_id=1, source_target_pairs={{0,2},{1,3},{4,6},{5,7},{2,0},{3,1},{6,4},{7,5},{8,10},{9,11},{12,... | collective-permute-start | bytes 1572872 | tf_op jit(solution)/shard_map/ppermute | solution.py:400
  25.7 34.6 %copy-start.1 = (bf16[512,1024]{1,0:T(8,128)(2,1)}, bf16[512,1024]{1,0:T(8,128)(2,1)S(1)}, u32[]{:S(2)}) copy-start(bf16[512,1024]{1,0:T(8,128)(2,1)S(1)} %collective-permute-done.3.other_cot) | copy-start | bytes 3145732
  27.3 5.2 %copy-start.5 = (bf16[256,1024]{1,0:T(8,128)(2,1)}, bf16[256,1024]{1,0:T(8,128)(2,1)S(1)}, u32[]{:S(2)}) copy-start(bf16[256,1024]{1,0:T(8,128)(2,1)S(1)} %collective-permute-done) | copy-start | bytes 1572868
  27.3 2.1 collective-permute-start.6
  27.3 5.2 %collective-permute-start.5 = (bf16[256,1024]{1,0:T(8,128)(2,1)S(1)}, bf16[256,1024]{1,0:T(8,128)(2,1)S(1)}, u32[]{:S(2)}, u32[]{:S(2)}) collective-permute-start(bf16[256,1024]{1,0:T(8,128)(2,1)S(1)} %collective-permute-done), channel_id=1, source_target_pairs={{2,4},{3,5},{4,2},{5,3},{10,12},{11,13},{12,10},{13,11},{18,20},{1... | collective-permute-start | bytes 1572872 | tf_op jit(solution)/shard_map/ppermute | solution.py:400
  28.0 17.1 %collective-permute-start.4 = (bf16[256,1024]{1,0:T(8,128)(2,1)S(1)}, bf16[256,1024]{1,0:T(8,128)(2,1)}, u32[]{:S(2)}, u32[]{:S(2)}) collective-permute-start(bf16[256,1024]{1,0:T(8,128)(2,1)S(1)} %collective-permute-done.1), channel_id=1, source_target_pairs={{4,6},{5,7},{2,0},{3,1},{12,14},{13,15},{10,8},{11,9},{20,22},{21,... | collective-permute-start | bytes 1572872 | tf_op jit(solution)/shard_map/ppermute | solution.py:400
  29.5 0.8 copy-start.4
  32.6 33.8 %collective-permute-start.7 = (bf16[256,1024]{1,0:T(8,128)(2,1)S(1)}, bf16[256,1024]{1,0:T(8,128)(2,1)S(1)}, u32[]{:S(2)}, u32[]{:S(2)}) collective-permute-start(bf16[256,1024]{1,0:T(8,128)(2,1)S(1)} %collective-permute-done.5), channel_id=1, source_target_pairs={{4,6},{5,7},{2,0},{3,1},{12,14},{13,15},{10,8},{11,9},{20,22},{21,... | collective-permute-start | bytes 1572872 | tf_op jit(solution)/shard_map/ppermute | solution.py:400
  33.9 12.3 %collective-permute-start.10 = (bf16[64,1024]{1,0:T(8,128)(2,1)}, bf16[64,1024]{1,0:T(8,128)(2,1)S(1)}, u32[]{:S(2)}, u32[]{:S(2)}) collective-permute-start(bf16[64,1024]{1,0:T(8,128)(2,1)} %get-tuple-element.97), channel_id=1, source_target_pairs={{0,24},{1,25},{2,26},{3,27},{4,28},{5,29},{6,30},{7,31},{8,16},{9,... | collective-permute-start | bytes 393224 | tf_op jit(solution)/shard_map/ppermute | solution.py:391
  36.4 9.8 %collective-permute-start.9 = (bf16[64,1024]{1,0:T(8,128)(2,1)}, bf16[64,1024]{1,0:T(8,128)(2,1)S(1)}, u32[]{:S(2)}, u32[]{:S(2)}) collective-permute-start(bf16[64,1024]{1,0:T(8,128)(2,1)} %get-tuple-element.96), channel_id=1, source_target_pairs={{0,16},{1,17},{2,18},{3,19},{4,20},{5,21},{6,22},{7,23},{8,24},{9,... | collective-permute-start | bytes 393224 | tf_op jit(solution)/shard_map/ppermute | solution.py:391
  36.9 9.3 %collective-permute-start.8 = (bf16[64,1024]{1,0:T(8,128)(2,1)}, bf16[64,1024]{1,0:T(8,128)(2,1)S(1)}, u32[]{:S(2)}, u32[]{:S(2)}) collective-permute-start(bf16[64,1024]{1,0:T(8,128)(2,1)} %get-tuple-element.95), channel_id=1, source_target_pairs={{0,8},{1,9},{2,10},{3,11},{4,12},{5,13},{6,14},{7,15},{8,0},{9,1},... | collective-permute-start | bytes 393224 | tf_op jit(solution)/shard_map/ppermute | solution.py:391
  46.3 0.7 copy-start.13
  49.4 18.3 %collective-permute-start.13 = (bf16[64,1024]{1,0:T(8,128)(2,1)}, bf16[64,1024]{1,0:T(8,128)(2,1)S(1)}, u32[]{:S(2)}, u32[]{:S(2)}) collective-permute-start(bf16[64,1024]{1,0:T(8,128)(2,1)} %shard_map.78.refs_0_), channel_id=1, source_target_pairs={{0,6},{1,7},{2,4},{3,5},{4,2},{5,3},{6,0},{7,1},{8,14},{9,15},{10,... | collective-permute-start | bytes 393224 | tf_op jit(solution)/shard_map/ppermute | solution.py:391
  51.9 17.6 %collective-permute-start.12 = (bf16[64,1024]{1,0:T(8,128)(2,1)}, bf16[64,1024]{1,0:T(8,128)(2,1)S(1)}, u32[]{:S(2)}, u32[]{:S(2)}) collective-permute-start(bf16[64,1024]{1,0:T(8,128)(2,1)} %shard_map.78.refs_0_), channel_id=1, source_target_pairs={{0,4},{1,5},{2,6},{3,7},{4,0},{5,1},{6,2},{7,3},{8,12},{9,13},{10,... | collective-permute-start | bytes 393224 | tf_op jit(solution)/shard_map/ppermute | solution.py:391
  60.4 9.2 %collective-permute-start.11 = (bf16[64,1024]{1,0:T(8,128)(2,1)}, bf16[64,1024]{1,0:T(8,128)(2,1)S(1)}, u32[]{:S(2)}, u32[]{:S(2)}) collective-permute-start(bf16[64,1024]{1,0:T(8,128)(2,1)} %shard_map.78.refs_0_), channel_id=1, source_target_pairs={{0,2},{1,3},{2,0},{3,1},{4,6},{5,7},{6,4},{7,5},{8,10},{9,11},{10,... | collective-permute-start | bytes 393224 | tf_op jit(solution)/shard_map/ppermute | solution.py:391
  67.7 119.9 %copy-start.2 = (bf16[3,256,1024]{2,1,0:T(8,128)(2,1)}, bf16[3,256,1024]{2,1,0:T(8,128)(2,1)S(1)}, u32[]{:S(2)}) copy-start(bf16[3,256,1024]{2,1,0:T(8,128)(2,1)S(1)} %pad_maximum_fusion.refs_2_) | copy-start | bytes 4718596
  67.7 1.8 copy-start.9
  69.5 0.7 copy-start.10
  72.6 0.9 copy-start.6
  72.7 157.2 %reduce-scatter.3.cloned.1.call-start = ((), (), s32[]{:S(2)}) async-start(), calls=%async_computation.2 | async-start | bytes 7864320 | tf_op jit(solution)/shard_map/reduce_scatter | solution.py:481
  73.5 6.9 %collective-permute-start.16 = (bf16[64,1024]{1,0:T(8,128)(2,1)S(1)}, bf16[64,1024]{1,0:T(8,128)(2,1)S(1)}, u32[]{:S(2)}, u32[]{:S(2)}) collective-permute-start(bf16[64,1024]{1,0:T(8,128)(2,1)S(1)} %copy-done.6), channel_id=1, source_target_pairs={{0,24},{1,25},{2,26},{3,27},{4,28},{5,29},{6,30},{7,31},{8,16},{9,... | collective-permute-start | bytes 393224 | tf_op jit(solution)/shard_map/ppermute | solution.py:391
  74.5 7.2 %collective-permute-start.15 = (bf16[64,1024]{1,0:T(8,128)(2,1)S(1)}, bf16[64,1024]{1,0:T(8,128)(2,1)S(1)}, u32[]{:S(2)}, u32[]{:S(2)}) collective-permute-start(bf16[64,1024]{1,0:T(8,128)(2,1)S(1)} %copy-done.6), channel_id=1, source_target_pairs={{0,16},{1,17},{2,18},{3,19},{4,20},{5,21},{6,22},{7,23},{8,24},{9,... | collective-permute-start | bytes 393224 | tf_op jit(solution)/shard_map/ppermute | solution.py:391
  76.5 5.4 %collective-permute-start.14 = (bf16[64,1024]{1,0:T(8,128)(2,1)S(1)}, bf16[64,1024]{1,0:T(8,128)(2,1)S(1)}, u32[]{:S(2)}, u32[]{:S(2)}) collective-permute-start(bf16[64,1024]{1,0:T(8,128)(2,1)S(1)} %copy-done.6), channel_id=1, source_target_pairs={{0,8},{1,9},{2,10},{3,11},{4,12},{5,13},{6,14},{7,15},{8,0},{9,1},... | collective-permute-start | bytes 393224 | tf_op jit(solution)/shard_map/ppermute | solution.py:391
  80.4 1.5 copy-start.16
  81.8 0.7 copy-start.17
  85.1 2.1 collective-permute-start.17
  87.2 0.8 copy-start.3
  100.4 1.6 collective-permute-start.18
  118.4 0.8 copy-start.30
  118.4 1.8 copy-start.29
  118.4 3.7 %copy-start.28 = (f32[64,128]{1,0:T(8,128)S(1)}, f32[64,128]{1,0:T(8,128)}, u32[]{:S(2)}) copy-start(f32[64,128]{1,0:T(8,128)} %get-tuple-element.124) | copy-start | bytes 98308
  118.4 13.5 %copy-start = (bf16[64,8192]{1,0:T(8,128)(2,1)S(1)}, bf16[64,8192]{1,0:T(8,128)(2,1)}, u32[]{:S(2)}) copy-start(bf16[64,8192]{1,0:T(8,128)(2,1)} %shard_map.82.p_all.p_own) | copy-start | bytes 3145732
  118.4 71.0 %collective-permute-start.29 = (bf16[1024,1024]{1,0:T(8,128)(2,1)}, bf16[1024,1024]{1,0:T(8,128)(2,1)}, u32[]{:S(2)}, u32[]{:S(2)}) collective-permute-start(bf16[1024,1024]{1,0:T(8,128)(2,1)} %param.7), channel_id=1, source_target_pairs={{0,1},{1,0},{2,3},{3,2},{4,5},{5,4},{6,7},{7,6},{8,9},{9,8},{10,11... | collective-permute-start | bytes 6291464 | tf_op jit(solution)/shard_map/ppermute | solution.py:391
  119.1 4.8 %collective-permute-start.21 = (f32[64,128]{1,0:T(8,128)S(1)}, f32[64,128]{1,0:T(8,128)S(1)}, u32[]{:S(2)}, u32[]{:S(2)}) collective-permute-start(f32[64,128]{1,0:T(8,128)S(1)} %copy-done.30), channel_id=1, source_target_pairs={{0,24},{1,25},{2,26},{3,27},{4,28},{5,29},{6,30},{7,31},{8,16},{9,... | collective-permute-start | bytes 98312 | tf_op jit(solution)/shard_map/ppermute | solution.py:391
  120.1 4.1 %collective-permute-start.20 = (f32[64,128]{1,0:T(8,128)S(1)}, f32[64,128]{1,0:T(8,128)S(1)}, u32[]{:S(2)}, u32[]{:S(2)}) collective-permute-start(f32[64,128]{1,0:T(8,128)S(1)} %copy-done.29), channel_id=1, source_target_pairs={{0,16},{1,17},{2,18},{3,19},{4,20},{5,21},{6,22},{7,23},{8,24},{9,... | collective-permute-start | bytes 98312 | tf_op jit(solution)/shard_map/ppermute | solution.py:391
  122.1 3.9 %collective-permute-start.19 = (f32[64,128]{1,0:T(8,128)S(1)}, f32[64,128]{1,0:T(8,128)S(1)}, u32[]{:S(2)}, u32[]{:S(2)}) collective-permute-start(f32[64,128]{1,0:T(8,128)S(1)} %copy-done.28), channel_id=1, source_target_pairs={{0,8},{1,9},{2,10},{3,11},{4,12},{5,13},{6,14},{7,15},{8,0},{9,1},... | collective-permute-start | bytes 98312 | tf_op jit(solution)/shard_map/ppermute | solution.py:391
  124.0 2.0 copy-start.21
  124.3 1.7 copy-start.22
  128.0 16.5 %copy-start.7 = (f32[64,128]{1,0:T(8,128)S(1)}, f32[64,128]{1,0:T(8,128)}, u32[]{:S(2)}) copy-start(f32[64,128]{1,0:T(8,128)} %shard_map.86.refs_0_) | copy-start | bytes 98308
  128.0 34.9 %collective-permute-start.23 = (bf16[3,256,1024]{2,1,0:T(8,128)(2,1)S(1)}, bf16[3,256,1024]{2,1,0:T(8,128)(2,1)}, u32[]{:S(2)}, u32[]{:S(2)}) collective-permute-start(bf16[3,256,1024]{2,1,0:T(8,128)(2,1)S(1)} %pad_maximum_fusion.refs_2_), channel_id=1, source_target_pairs={{0,16},{1,17},{2,18},{3,19},{4,20},{5,21},{6,22},{7,23},{8,24},{9,... | collective-permute-start | bytes 4718600 | tf_op jit(solution)/shard_map/ppermute | solution.py:391
  128.6 39.1 %collective-permute-start.22 = (bf16[3,256,1024]{2,1,0:T(8,128)(2,1)S(1)}, bf16[3,256,1024]{2,1,0:T(8,128)(2,1)}, u32[]{:S(2)}, u32[]{:S(2)}) collective-permute-start(bf16[3,256,1024]{2,1,0:T(8,128)(2,1)S(1)} %pad_maximum_fusion.refs_2_), channel_id=1, source_target_pairs={{0,8},{1,9},{2,10},{3,11},{4,12},{5,13},{6,14},{7,15},{8,0},{9,1},... | collective-permute-start | bytes 4718600 | tf_op jit(solution)/shard_map/ppermute | solution.py:391
  130.2 14.3 %collective-permute-start.26 = (f32[64,128]{1,0:T(8,128)}, f32[64,128]{1,0:T(8,128)S(1)}, u32[]{:S(2)}, u32[]{:S(2)}) collective-permute-start(f32[64,128]{1,0:T(8,128)} %shard_map.86.refs_0_), channel_id=1, source_target_pairs={{0,6},{1,7},{2,4},{3,5},{4,2},{5,3},{6,0},{7,1},{8,14},{9,15},{10,... | collective-permute-start | bytes 98312 | tf_op jit(solution)/shard_map/ppermute | solution.py:391
  131.5 16.0 %collective-permute-start.25 = (f32[64,128]{1,0:T(8,128)}, f32[64,128]{1,0:T(8,128)S(1)}, u32[]{:S(2)}, u32[]{:S(2)}) collective-permute-start(f32[64,128]{1,0:T(8,128)} %shard_map.86.refs_0_), channel_id=1, source_target_pairs={{0,4},{1,5},{2,6},{3,7},{4,0},{5,1},{6,2},{7,3},{8,12},{9,13},{10,... | collective-permute-start | bytes 98312 | tf_op jit(solution)/shard_map/ppermute | solution.py:391
  144.5 6.2 %copy-start.19 = (f32[64,128]{1,0:T(8,128)}, f32[64,128]{1,0:T(8,128)S(1)}, u32[]{:S(2)}) copy-start(f32[64,128]{1,0:T(8,128)S(1)} %collective-permute-done.26.refs_3_) | copy-start | bytes 98308
  144.5 6.2 %collective-permute-start.24 = (f32[64,128]{1,0:T(8,128)S(1)}, f32[64,128]{1,0:T(8,128)S(1)}, u32[]{:S(2)}, u32[]{:S(2)}) collective-permute-start(f32[64,128]{1,0:T(8,128)S(1)} %copy-done.7), channel_id=1, source_target_pairs={{0,2},{1,3},{2,0},{3,1},{4,6},{5,7},{6,4},{7,5},{8,10},{9,11},{10,... | collective-permute-start | bytes 98312 | tf_op jit(solution)/shard_map/ppermute | solution.py:391
  147.5 3.3 %copy-start.20 = (f32[64,128]{1,0:T(8,128)}, f32[64,128]{1,0:T(8,128)S(1)}, u32[]{:S(2)}) copy-start(f32[64,128]{1,0:T(8,128)S(1)} %collective-permute-done.25.refs_2_) | copy-start | bytes 98308
  152.8 16.9 %copy-start.15 = (f32[64,128]{1,0:T(8,128)S(1)}, f32[64,128]{1,0:T(8,128)}, u32[]{:S(2)}) copy-start(f32[64,128]{1,0:T(8,128)} %shard_map.87.refs_0_) | copy-start | bytes 98308
  165.0 34.3 %collective-permute-start.28 = (bf16[3,256,512]{2,1,0:T(8,128)(2,1)}, bf16[3,256,512]{2,1,0:T(8,128)(2,1)}, u32[]{:S(2)}, u32[]{:S(2)}) collective-permute-start(bf16[3,256,512]{2,1,0:T(8,128)(2,1)} %slice.19), channel_id=1, source_target_pairs={{0,8},{1,9},{2,10},{3,11},{4,12},{5,13},{6,14},{7,15},{8,0},{9,1},... | collective-permute-start | bytes 2359304 | tf_op jit(solution)/shard_map/ppermute | solution.py:391
  166.3 18.6 %collective-permute-start.32 = (f32[64,128]{1,0:T(8,128)}, f32[64,128]{1,0:T(8,128)S(1)}, u32[]{:S(2)}, u32[]{:S(2)}) collective-permute-start(f32[64,128]{1,0:T(8,128)} %shard_map.87.refs_0_), channel_id=1, source_target_pairs={{0,24},{1,25},{2,26},{3,27},{4,28},{5,29},{6,30},{7,31},{8,16},{9,... | collective-permute-start | bytes 98312 | tf_op jit(solution)/shard_map/ppermute | solution.py:391
  169.0 30.3 %collective-permute-start.27 = (bf16[3,256,512]{2,1,0:T(8,128)(2,1)S(1)}, bf16[3,256,512]{2,1,0:T(8,128)(2,1)}, u32[]{:S(2)}, u32[]{:S(2)}) collective-permute-start(bf16[3,256,512]{2,1,0:T(8,128)(2,1)S(1)} %slice.18), channel_id=1, source_target_pairs={{0,16},{1,17},{2,18},{3,19},{4,20},{5,21},{6,22},{7,23},{8,24},{9,... | collective-permute-start | bytes 2359304 | tf_op jit(solution)/shard_map/ppermute | solution.py:391
  169.7 17.9 %collective-permute-start.31 = (f32[64,128]{1,0:T(8,128)S(1)}, f32[64,128]{1,0:T(8,128)S(1)}, u32[]{:S(2)}, u32[]{:S(2)}) collective-permute-start(f32[64,128]{1,0:T(8,128)S(1)} %copy-done.15), channel_id=1, source_target_pairs={{0,16},{1,17},{2,18},{3,19},{4,20},{5,21},{6,22},{7,23},{8,24},{9,... | collective-permute-start | bytes 98312 | tf_op jit(solution)/shard_map/ppermute | solution.py:391
  184.9 12.9 %copy-start.25 = (f32[64,128]{1,0:T(8,128)}, f32[64,128]{1,0:T(8,128)S(1)}, u32[]{:S(2)}) copy-start(f32[64,128]{1,0:T(8,128)S(1)} %collective-permute-done.32.refs_3_) | copy-start | bytes 98308
  184.9 3.9 %collective-permute-start.30 = (f32[64,128]{1,0:T(8,128)S(1)}, f32[64,128]{1,0:T(8,128)S(1)}, u32[]{:S(2)}, u32[]{:S(2)}) collective-permute-start(f32[64,128]{1,0:T(8,128)S(1)} %copy-done.15), channel_id=1, source_target_pairs={{0,8},{1,9},{2,10},{3,11},{4,12},{5,13},{6,14},{7,15},{8,0},{9,1},... | collective-permute-start | bytes 98312 | tf_op jit(solution)/shard_map/ppermute | solution.py:391
  187.6 10.2 %copy-start.26 = (f32[64,128]{1,0:T(8,128)}, f32[64,128]{1,0:T(8,128)S(1)}, u32[]{:S(2)}) copy-start(f32[64,128]{1,0:T(8,128)S(1)} %collective-permute-done.31.refs_2_) | copy-start | bytes 98308
  187.6 26.6 %collective-permute-start.33 = (bf16[3,256,1024]{2,1,0:T(8,128)(2,1)S(1)}, bf16[3,256,1024]{2,1,0:T(8,128)(2,1)}, u32[]{:S(2)}, u32[]{:S(2)}) collective-permute-start(bf16[3,256,1024]{2,1,0:T(8,128)(2,1)S(1)} %pad_maximum_fusion.refs_2_), channel_id=1, source_target_pairs={{0,1},{1,0},{2,3},{3,2},{4,5},{5,4},{6,7},{7,6},{8,9},{9,8},{10,11... | collective-permute-start | bytes 4718600 | tf_op jit(solution)/shard_map/ppermute | solution.py:391
  189.4 24.8 %collective-permute-start.35 = (bf16[3,256,1024]{2,1,0:T(8,128)(2,1)}, bf16[3,256,1024]{2,1,0:T(8,128)(2,1)}, u32[]{:S(2)}, u32[]{:S(2)}) collective-permute-start(bf16[3,256,1024]{2,1,0:T(8,128)(2,1)} %collective-permute-done.23.refs_6_), channel_id=1, source_target_pairs={{0,1},{1,0},{2,3},{3,2},{4,5},{5,4},{6,7},{7,6},{8,9},{9,8},{10,11... | collective-permute-start | bytes 4718600 | tf_op jit(solution)/shard_map/ppermute | solution.py:391
  189.4 24.8 %collective-permute-start.34 = (bf16[3,256,1024]{2,1,0:T(8,128)(2,1)}, bf16[3,256,1024]{2,1,0:T(8,128)(2,1)}, u32[]{:S(2)}, u32[]{:S(2)}) collective-permute-start(bf16[3,256,1024]{2,1,0:T(8,128)(2,1)} %collective-permute-done.22.refs_4_), channel_id=1, source_target_pairs={{0,1},{1,0},{2,3},{3,2},{4,5},{5,4},{6,7},{7,6},{8,9},{9,8},{10,11... | collective-permute-start | bytes 4718600 | tf_op jit(solution)/shard_map/ppermute | solution.py:391
  199.3 1.7 collective-permute-start.38
  199.3 14.9 %collective-permute-start.36 = (bf16[3,256,512]{2,1,0:T(8,128)(2,1)}, bf16[3,256,512]{2,1,0:T(8,128)(2,1)}, u32[]{:S(2)}, u32[]{:S(2)}) collective-permute-start(bf16[3,256,512]{2,1,0:T(8,128)(2,1)} %collective-permute-done.28.refs_8_), channel_id=1, source_target_pairs={{0,1},{1,0},{2,3},{3,2},{4,5},{5,4},{6,7},{7,6},{8,9},{9,8},{10,11... | collective-permute-start | bytes 2359304 | tf_op jit(solution)/shard_map/ppermute | solution.py:391
  201.0 13.2 %collective-permute-start.37 = (bf16[3,256,512]{2,1,0:T(8,128)(2,1)}, bf16[3,256,512]{2,1,0:T(8,128)(2,1)}, u32[]{:S(2)}, u32[]{:S(2)}) collective-permute-start(bf16[3,256,512]{2,1,0:T(8,128)(2,1)} %collective-permute-done.27.refs_9_), channel_id=1, source_target_pairs={{0,1},{1,0},{2,3},{3,2},{4,5},{5,4},{6,7},{7,6},{8,9},{9,8},{10,11... | collective-permute-start | bytes 2359304 | tf_op jit(solution)/shard_map/ppermute | solution.py:391
  (8 other events, 5.1 us)
Sparse Core Ops, SparseCore 0:
  72.8 41.9 reduce-scatter.4
  118.5 110.9 reduce-scatter.2

commit v2 on v1

--- a/solution.py
+++ b/solution.py
@@ -59,45 +59,41 @@
     )(scalars(c), cot, other_cot, tokens, other)
 
 
-def remove(feedback, hat, q):
-    rows, width = feedback.shape
+def finish(scale, start, gradient, feedback, hat, q, result):
+    tall, width = gradient.shape
     rank = hat.shape[1]
-    tile = rows // 2
-
-    def kernel(feedback, hat, q, result):
-        rank_part = jnp.dot(hat[...], q[...], precision=highest, preferred_element_type=f32)
-        result[...] = feedback[...] - rank_part
-
-    row = pl.BlockSpec((tile, width), lambda i: (i, 0))
-    return pl.pallas_call(
-        kernel,
-        grid=(rows // tile,),
-        in_specs=[row, pl.BlockSpec((tile, rank), lambda i: (i, 0)), whole(q.shape)],
-        out_specs=row,
-        out_shape=jax.ShapeDtypeStruct(feedback.shape, f32),
-        compiler_params=params(),
-        cost_estimate=cost(2 * rows * width * rank, 8 * rows * width),
-    )(feedback, hat, q)
-
-
-def finish(scale, start, gradient, base):
-    tall, width = gradient.shape
     tile = math.gcd(start, tall)
-
-    def kernel(gradient, base, result):
-        result[...] = base[...] + scale * gradient[...].astype(f32)
+    tile = tile // 2 if tile > 512 else tile
+
+    def kernel(gradient, feedback, hat, q, *refs):
+        top, low = split(hat[...])
+        q_top, q_low = split(q[...])
+        rank_part = times(top, q_top) + (times(top, q_low) + times(low, q_top))
+        refs[-1][...] = feedback[...] + (scale * gradient[...].astype(f32) - rank_part)
 
     row = pl.BlockSpec((tile, width), lambda i: (start // tile + i, 0))
+    specs = [
+        pl.BlockSpec((tile, width), lambda i: (i, 0)),
+        row,
+        pl.BlockSpec((tile, rank), lambda i: (start // tile + i, 0)),
+        whole(q.shape),
+    ]
+    operands = [gradient, feedback, hat, q]
+    aliases = {}
+    if result is not None:
+        specs.append(pl.BlockSpec(memory_space=pl.ANY))
+        operands.append(result)
+        aliases = {4: 0}
     return pl.pallas_call(
         kernel,
         grid=(tall // tile,),
-        in_specs=[pl.BlockSpec((tile, width), lambda i: (i, 0)), row],
+        in_specs=specs,
         out_specs=row,
-        out_shape=jax.ShapeDtypeStruct(base.shape, f32),
-        input_output_aliases={1: 0},
+        out_shape=jax.ShapeDtypeStruct(feedback.shape, f32),
+        input_output_aliases=aliases,
         compiler_params=params(),
-        cost_estimate=cost(tall * width, 10 * tall * width),
-    )(gradient, base)
+        cost_estimate=cost(6 * rank * tall * width, 10 * tall * width),
+    )(*operands)
 
 
 def split(value):
@@ -117,18 +113,13 @@
     return pltpu.CompilerParams(vmem_limit_bytes=VMEM)
 
 
-def left_part(scale, f, c, q_t, cot, tokens, feedback):
+def left_factor(scale, core, q_t, cot, tokens, rows, kind):
     rank, width = q_t.shape
     tok, depth = tokens.shape
-    rows = feedback.shape[0]
-    wide = 2 * rows
-    half = depth // wide // 2
-
-    def kernel(index, q_t, cot, tokens, feedback, sent, kept, factor):
-        stage, j = pl.program_id(0), pl.program_id(1)
-        side = jnp.where(stage == 0, 1 - index[1], index[1])
-
-        @pl.when((stage == 0) & (j == 0))
+    steps = depth // rows // 4
+
+    def kernel(index, q_t, cot, first, second, result, factor):
+        @pl.when(pl.program_id(0) == 0)
         def _():
             top, low = split(q_t[...])
             nt = (((1,), (1,)), ((), ()))
@@ -138,15 +129,50 @@
             factor[:rank] = top
             factor[rank:] = low
 
-        both = times(factor[...], tokens[...])
-        total = both[:rank] + both[rank:]
-        mine = side * half + j == index[0] // 2
-        column = pl.multiple_of(lax.rem(index[0], 2) * rows, 128)
-
-        def store(ref):
-            ref[...] = total.astype(ref.dtype)
-
-            @pl.when(mine)
+        for k, block in enumerate((first, second)):
+            both = times(factor[...], block[...])
+            result[:, k * rows : (k + 1) * rows] = (both[:rank] + both[rank:]).astype(kind)
+
+    return pl.pallas_call(
+        kernel,
+        grid_spec=pltpu.PrefetchScalarGridSpec(
+            num_scalar_prefetch=1,
+            grid=(steps,),
+            in_specs=[whole(q_t.shape), whole(cot.shape), *core_blocks(tok, rows)],
+            out_specs=[
+                pl.BlockSpec((rank, 2 * rows), lambda i, index: (0, i)),
+                whole((2 * rank, tok)),
+            ],
+        ),
+        out_shape=[
+            jax.ShapeDtypeStruct((rank, depth // 2), kind),
+            jax.ShapeDtypeStruct((2 * rank, tok), bf16),
+        ],
+        compiler_params=params(),
+        cost_estimate=cost(2 * rank * tok * depth, tok * depth),
+    )(scalars(core), q_t, cot, tokens, tokens)
+
+
+def core_blocks(tok, rows):
+    return [
+        pl.BlockSpec((tok, rows), lambda i, index, k=k: (0, 4 * i + 2 * k + index[0]))
+        for k in range(2)
+    ]
+
+
+def left_kept(core, chip, q_t, factor, tokens, feedback):
+    rank, _ = q_t.shape
+    tok, depth = tokens.shape
+    rows = feedback.shape[0]
+    steps = depth // rows // 4
+
+    def kernel(index, q_t, factor, first, second, feedback, result):
+        for k, block in enumerate((first, second)):
+            both = times(factor[...], block[...])
+            here = slice(k * rows, (k + 1) * rows)
+            result[:, here] = both[:rank] + both[rank:]
+
+            @pl.when(2 * pl.program_id(0) + k == index[1])
             def _():
                 top, low = split(q_t[...])
                 both = lax.dot_general(
@@ -155,59 +181,44 @@
                     (((1,), (1,)), ((), ())),
                     preferred_element_type=f32,
                 )
-                here = ref[:, pl.ds(column, rows)].astype(f32)
-                here += both[:rank] + both[rank:]
-                ref[:, pl.ds(column, rows)] = here.astype(ref.dtype)
-
-        @pl.when(stage == 0)
-        def _():
-            store(sent)
-
-        @pl.when(stage == 1)
-        def _():
-            store(kept)
-
-    def token_block(stage, j, index):
-        return 0, jnp.where(stage == 0, 1 - index[1], index[1]) * half + j
+                result[:, here] += both[:rank] + both[rank:]
 
     return pl.pallas_call(
         kernel,
         grid_spec=pltpu.PrefetchScalarGridSpec(
             num_scalar_prefetch=1,
-            grid=(2, half),
+            grid=(steps,),
             in_specs=[
                 whole(q_t.shape),
-                whole(cot.shape),
-                pl.BlockSpec((tok, wide), token_block),
+                whole(factor.shape),
+                *core_blocks(tok, rows),
                 whole(feedback.shape),
             ],
-            out_specs=[
-                pl.BlockSpec((rank, wide), lambda s, j, index: (0, jnp.where(s == 0, j, half - 1))),
-                pl.BlockSpec((rank, wide), lambda s, j, index: (0, jnp.where(s == 0, 0, j))),
-            ],
-            scratch_shapes=[pltpu.VMEM((2 * rank, tok), bf16)],
+            out_specs=pl.BlockSpec((rank, 2 * rows), lambda i, index: (0, i)),
         ),
-        out_shape=[
-            jax.ShapeDtypeStruct((rank, depth // 2), bf16),
-            jax.ShapeDtypeStruct((rank, depth // 2), f32),
-        ],
+        out_shape=jax.ShapeDtypeStruct((rank, depth // 2), f32),
         compiler_params=params(),
-        cost_estimate=cost(4 * rank * tok * depth, 2 * tok * depth + 4 * rows * width),
-    )(scalars(f, c), q_t, cot, tokens, feedback)
-
-
-def right_part(scale, f, c, p_all, tokens, cot, feedback):
+        cost_estimate=cost(2 * rank * tok * depth, tok * depth + 4 * feedback.size),
+    )(scalars(core, chip), q_t, factor, tokens, tokens, feedback)
+
+
+def right_part(scale, chip, c, p_all, tokens, cot, feedback):
     rank, depth = p_all.shape
     tok, width = cot.shape
     rows = feedback.shape[0]
     wide = 2 * rows
     steps = depth // wide
     half = width // 2
-
-    def kernel(index, p_all, p_own, tokens, cot, feedback, sent, kept, total):
+    half_steps = steps // 2
+
+    def block(i, k):
+        return 4 * lax.rem(i, half_steps) + 2 * k + i // half_steps
+
+    def kernel(index, p_all, p_own, first, second, cot, feedback, sent, kept, total):
         step = pl.program_id(0)
         nt = (((1,), (1,)), ((), ()))
-        term = lax.dot_general(p_all[...], tokens[...], nt, preferred_element_type=f32)
+        term = lax.dot_general(p_all[:, :rows], first[...], nt, preferred_element_type=f32)
+        term += lax.dot_general(p_all[:, rows:], second[...], nt, preferred_element_type=f32)
 
         @pl.when(step == 0)
         def _():
@@ -234,8 +245,11 @@
             grid=(steps,),
             in_specs=[
                 pl.BlockSpec((rank, wide), lambda i, index: (0, i)),
-                pl.BlockSpec((rank, rows), lambda i, index: (0, index[0])),
-                pl.BlockSpec((tok, wide), lambda i, index: (0, i)),
+                pl.BlockSpec((rank, rows), lambda i, index: (0, index[1] * 2 * half_steps + index[0])),
+                *[
+                    pl.BlockSpec((tok, rows), lambda i, index, k=k: (0, block(i, k)))
+                    for k in range(2)
+                ],
                 whole(cot.shape),
                 whole(feedback.shape),
             ],
@@ -245,7 +259,7 @@
         out_shape=[jax.ShapeDtypeStruct((rank, half), f32)] * 2,
         compiler_params=params(),
         cost_estimate=cost(2 * rank * tok * depth, 2 * tok * depth + 4 * rows * width),
-    )(scalars(f, c), p_all, p_all, tokens, cot, feedback)
+    )(scalars(chip, c), p_all, p_all, tokens, tokens, cot, feedback)
 
 
 def on_core(function, side, shapes, *operands):
@@ -331,7 +345,7 @@
                 result = lax.dynamic_update_slice_in_dim(
                     result, product, table[i, k] * wide, axis=1
                 )
-        return result, result[:8, :128].astype(f32)
+        return result, jnp.zeros((8, 128), jnp.int32)
     specs = [pl.BlockSpec((tok, width), lambda i, table: (0, 0))]
     operands = [table.astype(jnp.int32), cot]
     for arrays in pieces:
@@ -356,7 +370,7 @@
                 pltpu.SemaphoreType.DMA((2, len(parts))),
             ],
         ),
-        out_shape=[jax.ShapeDtypeStruct((tok, depth), bf16), jax.ShapeDtypeStruct((8, 128), f32)],
+        out_shape=[jax.ShapeDtypeStruct((tok, depth), bf16), jax.ShapeDtypeStruct((8, 128), jnp.int32)],
         input_output_aliases=aliases,
         compiler_params=params(),
         cost_estimate=cost(2 * tok * width * wide * count * len(pieces), 2 * count * len(pieces) * wide * (width + tok)),
@@ -438,6 +452,8 @@
         (value,) = on_core(add, 0, shapes, kept, *got)
         terms = [swap(value, 2 * m) for m in range(1, chips)]
         yield
+        terms = [after(term) for term in terms]
+        yield
         terms = [gate(value)] + terms
 
         def pairs(_, *terms):
@@ -470,7 +486,7 @@
 
     def gradient():
         same_core = [[2 * a + core for a in range(chips)] for core in range(2)]
-        parts = [(0, rows // 4), (rows // 4, rows - rows // 4)]
+        parts = [(rows - rows // 4, rows // 4), (0, rows - rows // 4)]
         summed = []
         for start, tall in parts:
             other_cot, other = results["other"]
@@ -483,24 +499,28 @@
                 )
             )
             yield
-        result = results["low_rank"]
+        hat, q = results["low_rank"]
+        result = None
         for (start, _), part in zip(parts, summed):
-            result = finish(scale, start, part, result)
+            result = finish(scale, start, part, feedback, hat, q, result)
             results["feedback"] = result
             yield
 
     def low_rank_chain():
-        sent, kept = left_part(scale, f, c, q_factor.T, cotangent, tokens, feedback)
+        q_t = q_factor.T
+        sent, factor = left_factor(scale, 1 - c, q_t, cotangent, tokens, rows, bf16)
         sent = after(sent)
         results["other"] = after(other_cot), after(other)
-        yield
+        results["sibling"] = after(results["sibling"])
+        yield
+        kept = left_kept(c + results["zero"], z, q_t, factor, tokens, feedback)
         reduction = split_sum(sent, kept, bf16)
         p_sum = yield from reduction
         p_all = yield from join(p_sum)
-        p_own = lax.dynamic_slice_in_dim(p_all, f * rows, rows, axis=1)
-        z_part = right_part(scale, f, c, p_all, tokens, cotangent, feedback)
+        p_own = lax.dynamic_slice_in_dim(p_all, (c * chips + z) * rows, rows, axis=1)
+        z_part = right_part(scale, z, c, p_all, tokens, cotangent, feedback)
         reduction = split_sum(*z_part, f32)
-        for _ in range(3):
+        for _ in range(2):
             next(reduction)
             yield
         p_gated = gate(p_all)
@@ -516,7 +536,17 @@
         hat_own = dot(p_own.astype(f32), inverse, ((0,), (1,)), highest)
         q_next = dot(inverse, z_all, ((1,), (0,)), highest) / groups
         results["q_next"] = q_next.T
-        results["low_rank"] = remove(feedback, hat_own, q_next)
+        results["low_rank"] = hat_own, q_next
+        yield
+
+    def own_weights():
+        results["sibling"] = swap(weight, 1)
+        yield
+        pieces = [[weight[None]], [results["sibling"][None]]]
+        results["own"], token = project(
+            None, depth, gate(cotangent), pieces, jnp.stack([f, f ^ 1])[None]
+        )
+        results["zero"] = token[0, 0]
         yield
 
     def weights():
@@ -529,9 +559,10 @@
             from_near, from_across = near[-1], across[-1]
             near.append(paired(from_across, moves))
             across.append(paired(from_near, moves, 1))
-            if h == chips - 2:
-                sibling = swap(weight, 1)
             yield
+            if 0 < h < chips - 2:
+                near[-1], across[-1] = after(near[-1]), after(across[-1])
+                yield
         toward = jnp.where(z % 2 == 0, 1, -1)
         count = jnp.where(z % 2 == 0, chips - 1 - z, z)
         slots, sources = [], []
@@ -565,30 +596,25 @@
             if m not in twins and len(shares[m]) == 1:
                 twins[m] = [swap(x, 1) for x in shares[m]]
         yield
-        pieces = [[weight[None]], [sibling[None]]]
-        result, token = project(
-            None, depth, gate(cotangent), pieces, jnp.stack([f, f ^ 1])[None]
-        )
-        after(token)
-        yield
         for m in range(groups):
             if m not in twins:
                 twins[m] = [swap(x, 1) for x in shares[m]]
+        yield
         pieces, table = [], []
         for m in range(groups):
             for core, arrays in ((c, shares[m]), (1 - c, twins[m])):
                 pieces.append(arrays)
                 table.append((far * 2 + core) * groups + (d ^ m))
-        result, token = project(result, depth, gate(cotangent), pieces, jnp.stack(table, axis=1))
-        results["input_grad"] = result
-        after(token)
-        yield
-
-    chains = {"R": gradient(), "L": low_rank_chain(), "W": weights()}
-    order = "WLWLLWLRWLRLLLRRLWLLWWLLW"
+        results["input_grad"], _ = project(
+            results["own"], depth, gate(cotangent), pieces, jnp.stack(table, axis=1)
+        )
+        yield
+
+    chains = {"R": gradient(), "L": low_rank_chain(), "W": weights(), "O": own_weights()}
+    order = "OWLWROWRLLLWRLWRLLWLLLLWLLWLLW"
     for name in order:
         next(chains[name], None)
-    for name in ("L", "W", "R"):
+    for name in "LWR":
         for _ in chains[name]:
             pass
     return (results["input_grad"], results["q_next"], results["feedback"][None])

time: 243 us -> 235 us (0.967)
  Pallas kernels: 92.5 us -> 87.8 us
  starting transfers between devices: 45.2 us -> 41.4 us
    ppermute x34, waiting for transfers between devices: 46 us -> 38.1 us  [swap(): lax.ppermute(after(value), AXES, [(i, i ^ mask) for i in range(world)])]
    ppermute x5, waiting for transfers between devices: 9.22 us -> 15.8 us  [along(): return lax.ppermute(after(value), AXES, moves)]
    pallas_call x4, Pallas kernels: 24.1 us -> 18.4 us  [the longest x2 7.39 us: finish(): pl.pallas_call(kernel, grid=(tall // tile,), in_specs=specs, out_specs=ro...]
    ppermute x34, starting transfers between devices: 35.1 us -> 31.7 us  [swap(): lax.ppermute(after(value), AXES, [(i, i ^ mask) for i in range(world)])]
    reduce_scatter x2, waiting for transfers between devices: 0.02 us -> 3.4 us  [gradient(): lax.psum_scatter(after(both), 'fsdp', scatter_dimension=0, axis_index_gro...]
    unnamed x62 -> x58, local copies, waits for them, and re-layouts: 9.09 us -> 6.99 us
  transfers between devices with their start and end apart: 41 -> 41, of which waited for: 18 -> 21; matrix products, arithmetic and copies ran while one was open for 10% -> 11% of each run, Pallas kernels for 36% -> 36%
where the time goes in v2:
time: 235 us; the launch traced here: 233 us
  Pallas kernels  87.8 us (37%)
  waiting for transfers between devices  57.3 us (24%)
  starting transfers between devices  41.4 us (18%)
  other arithmetic  15.3 us (7%)
  between operations  15 us (6%)
  local copies, waits for them, and re-layouts  12.5 us (5%)
  matrix products  3.93 us (2%)
    ppermute x34, waiting for transfers between devices, swap(): lax.ppermute(after(value), AXES, [(i, i ^ mask) for i in range(world)])  38.1 us
    ppermute x34, starting transfers between devices, swap(): lax.ppermute(after(value), AXES, [(i, i ^ mask) for i in range(world)])  31.7 us
    pallas_call x2, Pallas kernels, project(): pl.pallas_call(lambda *refs: project_kernel(parts, *refs), grid_spec=pltp...  20.3 us
    pallas_call x2, Pallas kernels, partials(): pl.pallas_call(kernel, grid_spec=pltpu.PrefetchScalarGridSpec(num_scalar_...  20.2 us
    pallas_call x10, Pallas kernels, on_core(): pl.pallas_call(kernel, grid_spec=pltpu.PrefetchScalarGridSpec(num_scalar_...  18.4 us
    ppermute x5, waiting for transfers between devices, along(): return lax.ppermute(after(value), AXES, moves)  15.8 us
    pallas_call x1, Pallas kernels, right_part(): pl.pallas_call(kernel, grid_spec=pltpu.PrefetchScalarGridSpec(num_scalar_...  10.6 us
    ppermute x5, starting transfers between devices, along(): return lax.ppermute(after(value), AXES, moves)  9.63 us
  transfers between devices with their start and end apart: 41, of which 21 were waited for; matrix products, arithmetic and copies ran while one was open for 11% of the time, Pallas kernels for 36%

profile of v2, /device:TPU:0, one launch (start us, length us, event | category | flops | bytes accessed | tf_op | source)
XLA Modules:
  0.0 233.4 jit_solution(1850143449429420562)
XLA Ops:
  8.2 1.1 constant_dynamic-slice_fusion
  10.0 5.5 %collective-permute-start = (bf16[256,1024]{1,0:T(8,128)(2,1)S(1)}, bf16[256,1024]{1,0:T(8,128)(2,1)}, u32[]{:S(2)}, u32[]{:S(2)}) collective-permute-start(bf16[256,1024]{1,0:T(8,128)(2,1)S(1)} %constant_dynamic-slice_fusion), channel_id=1, source_target_pairs={{0,2},{1,3},{4,6},{5,7},{2,0},{3,1},{6,4},{7,5},{8,10},{9,11},{12,... | collective-permute-start | bytes 1572872 | tf_op jit(solution)/shard_map/ppermute | solution.py:414
  15.5 4.4 %shard_map.76 = (bf16[64,4096]{1,0:T(8,128)(2,1)}, bf16[128,512]{1,0:T(8,128)(2,1)}) custom-call(s32[1]{0:T(128)} %bitcast.9.index, f32[64,1024]{1,0:T(8,128)} %bitcast.44, bf16[512,1024]{1,0:T(8,128)(2,1)} %refs_1_.1, bf16[512,8192]{1,0:T(8,128)(2,1)} %second.5, bf16[512,8192]{1,0:T(8,128)(2,1)} %second.5), custom_call_target="tpu_custom_call" | custom-call | flops 536870912 | bytes 4194304 | tf_op jit(solution)/shard_map/pallas_call | solution.py:136
  19.9 2.5 %collective-permute-done.3.other = bf16[512,8192]{1,0:T(8,128)(2,1)} collective-permute-done((bf16[512,8192]{1,0:T(8,128)(2,1)}, bf16[512,8192]{1,0:T(8,128)(2,1)}, u32[]{:S(2)}, u32[]{:S(2)}) %collective-permute-start.3) | collective-permute-done | bytes 8388640 | tf_op jit(solution)/shard_map/ppermute | solution.py:405
  22.4 3.0 %collective-permute-done.2 = bf16[1024,1024]{1,0:T(8,128)(2,1)} collective-permute-done((bf16[1024,1024]{1,0:T(8,128)(2,1)}, bf16[1024,1024]{1,0:T(8,128)(2,1)}, u32[]{:S(2)}, u32[]{:S(2)}) %collective-permute-start.2) | collective-permute-done | bytes 2097184 | tf_op jit(solution)/shard_map/ppermute | solution.py:405
  25.4 1.3 collective-permute-start.6
  26.6 1.2 collective-permute-done
  28.6 6.1 %shard_map.77 = bf16[1024,1024]{1,0:T(8,128)(2,1)} custom-call(s32[1]{0:T(128)} %bitcast.5.index, bf16[512,1024]{1,0:T(8,128)(2,1)} %refs_1_.1, bf16[512,1024]{1,0:T(8,128)(2,1)} %copy-done.1, bf16[512,8192]{1,0:T(8,128)(2,1)} %second.5, bf16[512,8192]{1,0:T(8,128)(2,1)} %collective-permute-done.3.other), custom_call_target="tpu_custom_call" | custom-call | flops 2147483648 | bytes 6291456 | tf_op jit(solution)/shard_map/pallas_call | solution.py:48
  34.6 7.1 %collective-permute-done.6 = bf16[256,1024]{1,0:T(8,128)(2,1)S(1)} collective-permute-done((bf16[256,1024]{1,0:T(8,128)(2,1)S(1)}, bf16[256,1024]{1,0:T(8,128)(2,1)S(1)}, u32[]{:S(2)}, u32[]{:S(2)}) %collective-permute-start.6) | collective-permute-done | bytes 524320 | tf_op jit(solution)/shard_map/ppermute | solution.py:414
  42.7 7.2 %shard_map.78 = (bf16[512,8192]{1,0:T(8,128)(2,1)}, s32[8,128]{1,0:T(8,128)}) custom-call(s32[1,2]{1,0:T(1,128)} %add_bitcast_fusion.refs_0_, bf16[512,1024]{1,0:T(8,128)(2,1)} %refs_1_.1, bf16[1,1024,1024]{2,1,0:T(8,128)(2,1)} %bitcast.46, bf16[1,1024,1024]{2,1,0:T(8,128)(2,1)} %bitcast.12.refs_3_), custom_call_target="tpu_custom_call" | custom-call | flops 2147483648 | bytes 6291456 | tf_op jit(solution)/shard_map/pallas_call | solution.py:361
  49.8 1.2 slice.19
  52.2 6.6 %shard_map.79.refs_0_ = f32[64,4096]{1,0:T(8,128)} custom-call(s32[2]{0:T(128)} %pad_add_fusion.2.index, f32[64,1024]{1,0:T(8,128)} %bitcast.45, bf16[128,512]{1,0:T(8,128)(2,1)} %get-tuple-element.104.factor, bf16[512,8192]{1,0:T(8,128)(2,1)} %second.5, bf16[512,8192]{1,0:T(8,128)(2,1)} %second.5, f32[1024,1024]{1,0:T(8,128)} %bitcast.38), custom_call_target="tpu_custom_call" | custom-call | flops 536870912 | bytes 8388608 | tf_op jit(solution)/shard_map/pallas_call | solution.py:186
  59.6 2.3 shard_map.80
  61.9 2.3 collective-permute-start.8
  64.1 1.5 collective-permute-start.9
  65.7 6.9 %collective-permute-done.10.refs_3_ = bf16[64,1024]{1,0:T(8,128)(2,1)S(1)} collective-permute-done((bf16[64,1024]{1,0:T(8,128)(2,1)}, bf16[64,1024]{1,0:T(8,128)(2,1)S(1)}, u32[]{:S(2)}, u32[]{:S(2)}) %collective-permute-start.10) | collective-permute-done | bytes 131104 | tf_op jit(solution)/shard_map/ppermute | solution.py:405
  74.1 1.8 shard_map.81.refs_0_
  75.9 3.6 %collective-permute-start.12 = (bf16[64,1024]{1,0:T(8,128)(2,1)}, bf16[64,1024]{1,0:T(8,128)(2,1)S(1)}, u32[]{:S(2)}, u32[]{:S(2)}) collective-permute-start(bf16[64,1024]{1,0:T(8,128)(2,1)} %shard_map.81.refs_0_), channel_id=1, source_target_pairs={{0,6},{1,7},{2,4},{3,5},{4,2},{5,3},{6,0},{7,1},{8,14},{9,15},{10,... | collective-permute-start | bytes 393224 | tf_op jit(solution)/shard_map/ppermute | solution.py:405
  79.5 2.8 %collective-permute-start.13 = (bf16[64,1024]{1,0:T(8,128)(2,1)}, bf16[64,1024]{1,0:T(8,128)(2,1)S(1)}, u32[]{:S(2)}, u32[]{:S(2)}) collective-permute-start(bf16[64,1024]{1,0:T(8,128)(2,1)} %shard_map.81.refs_0_), channel_id=1, source_target_pairs={{0,4},{1,5},{2,6},{3,7},{4,0},{5,1},{6,2},{7,3},{8,12},{9,13},{10,... | collective-permute-start | bytes 393224 | tf_op jit(solution)/shard_map/ppermute | solution.py:405
  82.5 1.5 collective-permute-start.11
  84.0 14.1 %shard_map.82 = bf16[3072,1024]{1,0:T(8,128)(2,1)} custom-call(s32[1]{0:T(128)} %bitcast.5.index, bf16[512,1024]{1,0:T(8,128)(2,1)} %refs_1_.1, bf16[512,1024]{1,0:T(8,128)(2,1)} %copy-done.1, bf16[512,8192]{1,0:T(8,128)(2,1)} %second.5, bf16[512,8192]{1,0:T(8,128)(2,1)} %collective-permute-done.3.other), custom_call_target="tpu_custom_call" | custom-call | flops 6442450944 | bytes 18874368 | tf_op jit(solution)/shard_map/pallas_call | solution.py:48
  98.1 2.2 collective-permute-done.13.refs_2_
  100.4 7.4 %collective-permute-done.11 = bf16[256,1024]{1,0:T(8,128)(2,1)S(1)} collective-permute-done((bf16[256,1024]{1,0:T(8,128)(2,1)S(1)}, bf16[256,1024]{1,0:T(8,128)(2,1)S(1)}, u32[]{:S(2)}, u32[]{:S(2)}) %collective-permute-start.11) | collective-permute-done | bytes 524320 | tf_op jit(solution)/shard_map/ppermute | solution.py:414
  107.9 1.2 pad_maximum_fusion.refs_2_
  109.1 2.4 %shard_map.83.refs_0_ = bf16[64,1024]{1,0:T(8,128)(2,1)} custom-call(s32[1]{0:T(128)} %constant.90.clone.1.index, bf16[64,1024]{1,0:T(8,128)(2,1)} %shard_map.81.refs_0_, bf16[64,1024]{1,0:T(8,128)(2,1)} %copy-done.10, bf16[64,1024]{1,0:T(8,128)(2,1)} %copy-done.9, bf16[64,1024]{1,0:T(8,128)(2,1)} %copy-done.8), custom_call_target="tpu_custom_call" | custom-call | flops 1 | bytes 524288 | tf_op jit(solution)/shard_map/pallas_call | solution.py:274
  111.5 2.4 %collective-permute-start.17 = (bf16[64,1024]{1,0:T(8,128)(2,1)}, bf16[64,1024]{1,0:T(8,128)(2,1)S(1)}, u32[]{:S(2)}, u32[]{:S(2)}) collective-permute-start(bf16[64,1024]{1,0:T(8,128)(2,1)} %shard_map.83.refs_0_), channel_id=1, source_target_pairs={{0,24},{1,25},{2,26},{3,27},{4,28},{5,29},{6,30},{7,31},{8,16},{9,... | collective-permute-start | bytes 393224 | tf_op jit(solution)/shard_map/ppermute | solution.py:405
  115.0 3.6 %collective-permute-done.17.refs_3_ = bf16[64,1024]{1,0:T(8,128)(2,1)S(1)} collective-permute-done((bf16[64,1024]{1,0:T(8,128)(2,1)}, bf16[64,1024]{1,0:T(8,128)(2,1)S(1)}, u32[]{:S(2)}, u32[]{:S(2)}) %collective-permute-start.17) | collective-permute-done | bytes 131104 | tf_op jit(solution)/shard_map/ppermute | solution.py:405
  118.6 2.3 %collective-permute-done.16.refs_2_ = bf16[64,1024]{1,0:T(8,128)(2,1)S(1)} collective-permute-done((bf16[64,1024]{1,0:T(8,128)(2,1)}, bf16[64,1024]{1,0:T(8,128)(2,1)S(1)}, u32[]{:S(2)}, u32[]{:S(2)}) %collective-permute-start.16) | collective-permute-done | bytes 131104 | tf_op jit(solution)/shard_map/ppermute | solution.py:405
  122.2 2.0 shard_map.84.refs_0_
  124.3 1.5 collective-permute-start.26
  127.1 0.8 copy-done.3
  127.9 2.3 shard_map.85.p_all.p_own
  130.2 10.6 %shard_map.86 = (f32[64,512]{1,0:T(8,128)}, f32[64,512]{1,0:T(8,128)}) custom-call(s32[2]{0:T(128)} %pad_add_fusion.1.index, bf16[64,8192]{1,0:T(8,128)(2,1)} %shard_map.85.p_all.p_own, bf16[64,8192]{1,0:T(8,128)(2,1)} %shard_map.85.p_all.p_own, bf16[512,8192]{1,0:T(8,128)(2,1)} %second.5, bf16[512,8192]{1,0:T(8,128)(2,1)} %second.5, ...), custom_call_target="tpu_custom_call" | custom-call | flops 536870912 | bytes 12582912 | tf_op jit(solution)/shard_map/pallas_call | solution.py:241
  140.9 1.6 collective-permute-done.19.refs_1_
  143.1 1.6 shard_map.87
  144.7 1.5 collective-permute-start.22
  146.2 1.3 collective-permute-start.21
  148.7 5.8 %cholesky.17 = f32[64,64]{1,0:T(8,128)S(1)} custom-call(f32[64,64]{1,0:T(8,128)S(1)} %fusion.5), custom_call_target="Cholesky" | custom-call | tf_op jit(solution)/shard_map/jit(cholesky)/cholesky | solution.py:528
  155.9 4.9 %custom-call.6 = f32[1,64,64]{1,2,0:T(8,128)S(1)} custom-call(f32[1,64,64]{2,1,0:T(8,128)S(1)} %fusion.2), custom_call_target="InvertDiagBlocksLowerTriangular" | custom-call | tf_op jit(solution)/shard_map/triangular_solve | solution.py:529
  161.0 2.2 collective-permute-done.22.refs_3_
  164.5 1.4 shard_map.88.refs_0_
  165.9 1.2 slice.23
  167.1 1.5 collective-permute-start.29
  168.7 1.2 slice.22
  169.9 0.9 collective-permute-start.28
  170.7 2.7 %collective-permute-start.24 = (f32[64,128]{1,0:T(8,128)S(1)}, f32[64,128]{1,0:T(8,128)S(1)}, u32[]{:S(2)}, u32[]{:S(2)}) collective-permute-start(f32[64,128]{1,0:T(8,128)S(1)} %copy-done.6), channel_id=1, source_target_pairs={{0,4},{1,5},{2,6},{3,7},{4,0},{5,1},{6,2},{7,3},{8,12},{9,13},{10,... | collective-permute-start | bytes 98312 | tf_op jit(solution)/shard_map/ppermute | solution.py:405
  173.5 1.7 collective-permute-start.23
  175.1 1.9 collective-permute-done.25.refs_1_
  177.1 3.0 %collective-permute-done.23.refs_3_ = f32[64,128]{1,0:T(8,128)S(1)} collective-permute-done((f32[64,128]{1,0:T(8,128)S(1)}, f32[64,128]{1,0:T(8,128)S(1)}, u32[]{:S(2)}, u32[]{:S(2)}) %collective-permute-start.23) | collective-permute-done | bytes 32800 | tf_op jit(solution)/shard_map/ppermute | solution.py:405
  180.7 1.4 shard_map.89.refs_0_
  182.1 1.2 collective-permute-start.32
  183.8 3.6 %collective-permute-done.32.refs_3_ = f32[64,128]{1,0:T(8,128)S(1)} collective-permute-done((f32[64,128]{1,0:T(8,128)}, f32[64,128]{1,0:T(8,128)S(1)}, u32[]{:S(2)}, u32[]{:S(2)}) %collective-permute-start.32) | collective-permute-done | bytes 32800 | tf_op jit(solution)/shard_map/ppermute | solution.py:405
  187.3 1.1 collective-permute-start.31
  189.5 2.1 collective-permute-done.31.refs_2_
  191.5 1.4 collective-permute-done.30.refs_1_
  193.5 1.5 shard_map.90.refs_0_
  195.5 1.0 collective-permute-done.38.refs_1_
  197.6 1.3 fusion.hat
  198.9 1.7 shard_map.92
  200.6 2.0 convolution_multiply_fusion.q
  202.6 3.0 %shard_map.93.refs_0_ = f32[1024,1024]{1,0:T(8,128)} custom-call(bf16[256,1024]{1,0:T(8,128)(2,1)} %reduce-scatter.5.cloned.1.call-done.gradient, f32[1024,1024]{1,0:T(8,128)} %bitcast.40, f32[1024,64]{1,0:T(8,128)} %fusion.hat, f32[64,1024]{1,0:T(8,128)} %convolution_multiply_fusion.q), custom_call_target="tpu_custom_call" | custom-call | flops 100663296 | bytes 2621440 | tf_op jit(solution)/shard_map/pallas_call | solution.py:87
  205.6 13.1 %shard_map.91 = (bf16[512,8192]{1,0:T(8,128)(2,1)}, s32[8,128]{1,0:T(8,128)}) custom-call(s32[3,8]{1,0:T(4,128)} %stack.77.refs_0_, bf16[512,1024]{1,0:T(8,128)(2,1)} %refs_1_.1, bf16[3,256,1024]{2,1,0:T(8,128)(2,1)} %copy-done.2, bf16[3,256,1024]{2,1,0:T(8,128)(2,1)} %collective-permute-done.33.refs_3_, ...), custom_call_target="tpu_custom_call", output_to_operand_aliasing={{0}: (12, {})} | custom-call | flops 6442450944 | bytes 18874368 | tf_op jit(solution)/shard_map/pallas_call | solution.py:361
  218.7 3.4 %reduce-scatter.3.cloned.1.call-done.gradient = bf16[768,1024]{1,0:T(8,128)(2,1)} async-done(((bf16[3072,1024]{1,0:T(8,128)(2,1)}), bf16[768,1024]{1,0:T(8,128)(2,1)}) %reduce-scatter.3.cloned.1.call-update) | async-done | bytes 1572880 | tf_op jit(solution)/shard_map/reduce_scatter | solution.py:497
  222.1 4.4 %shard_map.94 = f32[1024,1024]{1,0:T(8,128)} custom-call(bf16[768,1024]{1,0:T(8,128)(2,1)} %reduce-scatter.3.cloned.1.call-done.gradient, f32[1024,1024]{1,0:T(8,128)} %bitcast.41, f32[1024,64]{1,0:T(8,128)} %fusion.hat, f32[64,1024]{1,0:T(8,128)} %convolution_multiply_fusion.q, f32[1024,1024]{1,0:T(8,128)} %shard_map.93.refs_0_), custom_call_target="tpu_custom_call", output_to_operand_aliasing={{}: (4, {})} | custom-call | flops 301989888 | bytes 7864320 | tf_op jit(solution)/shard_map/pallas_call | solution.py:87
  (122 shorter events, 19.2 us)
Async XLA Ops:
  7.2 195.4 %reduce-scatter.5.cloned.1.call-start = ((), (), s32[]{:S(2)}) async-start(), calls=%async_computation.3 | async-start | bytes 2621440 | tf_op jit(solution)/shard_map/reduce_scatter | solution.py:497
  7.2 15.1 %collective-permute-start.3 = (bf16[512,8192]{1,0:T(8,128)(2,1)}, bf16[512,8192]{1,0:T(8,128)(2,1)}, u32[]{:S(2)}, u32[]{:S(2)}) collective-permute-start(bf16[512,8192]{1,0:T(8,128)(2,1)} %second.5), channel_id=1, source_target_pairs={{0,1},{1,0},{2,3},{3,2},{4,5},{5,4},{6,7},{7,6},{8,9},{9,8},{10,11... | collective-permute-start | bytes 25165832 | tf_op jit(solution)/shard_map/ppermute | solution.py:405
  7.7 17.6 %collective-permute-start.2 = (bf16[1024,1024]{1,0:T(8,128)(2,1)}, bf16[1024,1024]{1,0:T(8,128)(2,1)}, u32[]{:S(2)}, u32[]{:S(2)}) collective-permute-start(bf16[1024,1024]{1,0:T(8,128)(2,1)} %param.7), channel_id=1, source_target_pairs={{0,1},{1,0},{2,3},{3,2},{4,5},{5,4},{6,7},{7,6},{8,9},{9,8},{10,11... | collective-permute-start | bytes 6291464 | tf_op jit(solution)/shard_map/ppermute | solution.py:405
  7.8 12.1 %collective-permute-start.4 = (bf16[512,1024]{1,0:T(8,128)(2,1)}, bf16[512,1024]{1,0:T(8,128)(2,1)S(1)}, u32[]{:S(2)}, u32[]{:S(2)}) collective-permute-start(bf16[512,1024]{1,0:T(8,128)(2,1)} %refs_1_.1), channel_id=1, source_target_pairs={{0,1},{1,0},{2,3},{3,2},{4,5},{5,4},{6,7},{7,6},{8,9},{9,8},{10,11... | collective-permute-start | bytes 3145736 | tf_op jit(solution)/shard_map/ppermute | solution.py:405
  9.3 16.0 %collective-permute-start.1 = (bf16[256,1024]{1,0:T(8,128)(2,1)S(1)}, bf16[256,1024]{1,0:T(8,128)(2,1)S(1)}, u32[]{:S(2)}, u32[]{:S(2)}) collective-permute-start(bf16[256,1024]{1,0:T(8,128)(2,1)S(1)} %constant_dynamic-slice_fusion), channel_id=1, source_target_pairs={{2,4},{3,5},{4,2},{5,3},{10,12},{11,13},{12,10},{13,11},{18,20},{1... | collective-permute-start | bytes 1572872 | tf_op jit(solution)/shard_map/ppermute | solution.py:414
  10.0 17.9 %collective-permute-start = (bf16[256,1024]{1,0:T(8,128)(2,1)S(1)}, bf16[256,1024]{1,0:T(8,128)(2,1)}, u32[]{:S(2)}, u32[]{:S(2)}) collective-permute-start(bf16[256,1024]{1,0:T(8,128)(2,1)S(1)} %constant_dynamic-slice_fusion), channel_id=1, source_target_pairs={{0,2},{1,3},{4,6},{5,7},{2,0},{3,1},{6,4},{7,5},{8,10},{9,11},{12,... | collective-permute-start | bytes 1572872 | tf_op jit(solution)/shard_map/ppermute | solution.py:414
  19.9 8.7 %copy-start.1 = (bf16[512,1024]{1,0:T(8,128)(2,1)}, bf16[512,1024]{1,0:T(8,128)(2,1)S(1)}, u32[]{:S(2)}) copy-start(bf16[512,1024]{1,0:T(8,128)(2,1)S(1)} %collective-permute-done.4.other_cot) | copy-start | bytes 3145732
  25.4 16.4 %collective-permute-start.6 = (bf16[256,1024]{1,0:T(8,128)(2,1)S(1)}, bf16[256,1024]{1,0:T(8,128)(2,1)S(1)}, u32[]{:S(2)}, u32[]{:S(2)}) collective-permute-start(bf16[256,1024]{1,0:T(8,128)(2,1)S(1)} %collective-permute-done.1), channel_id=1, source_target_pairs={{4,6},{5,7},{2,0},{3,1},{12,14},{13,15},{10,8},{11,9},{20,22},{21,... | collective-permute-start | bytes 1572872 | tf_op jit(solution)/shard_map/ppermute | solution.py:414
  27.9 13.9 %collective-permute-start.5 = (bf16[256,1024]{1,0:T(8,128)(2,1)}, bf16[256,1024]{1,0:T(8,128)(2,1)S(1)}, u32[]{:S(2)}, u32[]{:S(2)}) collective-permute-start(bf16[256,1024]{1,0:T(8,128)(2,1)} %collective-permute-done), channel_id=1, source_target_pairs={{2,4},{3,5},{4,2},{5,3},{10,12},{11,13},{12,10},{13,11},{18,20},{1... | collective-permute-start | bytes 1572872 | tf_op jit(solution)/shard_map/ppermute | solution.py:414
  34.6 7.2 %copy-start.28 = (bf16[64,4096]{1,0:T(8,128)(2,1)S(1)}, bf16[64,4096]{1,0:T(8,128)(2,1)}, u32[]{:S(2)}) copy-start(bf16[64,4096]{1,0:T(8,128)(2,1)} %get-tuple-element.108) | copy-start | bytes 1572868
  41.8 180.3 %reduce-scatter.3.cloned.1.call-start = ((), (), s32[]{:S(2)}) async-start(), calls=%async_computation.2 | async-start | bytes 7864320 | tf_op jit(solution)/shard_map/reduce_scatter | solution.py:497
  41.9 16.9 %collective-permute-start.7 = (bf16[64,4096]{1,0:T(8,128)(2,1)S(1)}, bf16[64,4096]{1,0:T(8,128)(2,1)S(1)}, u32[]{:S(2)}, u32[]{:S(2)}) collective-permute-start(bf16[64,4096]{1,0:T(8,128)(2,1)S(1)} %copy-done.28), channel_id=1, source_target_pairs={{0,1},{1,0},{2,3},{3,2},{4,5},{5,4},{6,7},{7,6},{8,9},{9,8},{10,11... | collective-permute-start | bytes 1572872 | tf_op jit(solution)/shard_map/ppermute | solution.py:405
  58.8 0.8 copy-start.4
  61.9 10.9 %collective-permute-start.8 = (bf16[64,1024]{1,0:T(8,128)(2,1)}, bf16[64,1024]{1,0:T(8,128)(2,1)S(1)}, u32[]{:S(2)}, u32[]{:S(2)}) collective-permute-start(bf16[64,1024]{1,0:T(8,128)(2,1)} %get-tuple-element.114), channel_id=1, source_target_pairs={{0,8},{1,9},{2,10},{3,11},{4,12},{5,13},{6,14},{7,15},{8,0},{9,1},... | collective-permute-start | bytes 393224 | tf_op jit(solution)/shard_map/ppermute | solution.py:405
  64.1 8.6 %collective-permute-start.9 = (bf16[64,1024]{1,0:T(8,128)(2,1)}, bf16[64,1024]{1,0:T(8,128)(2,1)S(1)}, u32[]{:S(2)}, u32[]{:S(2)}) collective-permute-start(bf16[64,1024]{1,0:T(8,128)(2,1)} %get-tuple-element.115), channel_id=1, source_target_pairs={{0,16},{1,17},{2,18},{3,19},{4,20},{5,21},{6,22},{7,23},{8,24},{9,... | collective-permute-start | bytes 393224 | tf_op jit(solution)/shard_map/ppermute | solution.py:405
  65.7 7.0 %collective-permute-start.10 = (bf16[64,1024]{1,0:T(8,128)(2,1)}, bf16[64,1024]{1,0:T(8,128)(2,1)S(1)}, u32[]{:S(2)}, u32[]{:S(2)}) collective-permute-start(bf16[64,1024]{1,0:T(8,128)(2,1)} %get-tuple-element.116), channel_id=1, source_target_pairs={{0,24},{1,25},{2,26},{3,27},{4,28},{5,29},{6,30},{7,31},{8,16},{9,... | collective-permute-start | bytes 393224 | tf_op jit(solution)/shard_map/ppermute | solution.py:405
  72.8 0.7 copy-start.12
  73.4 0.7 copy-start.11
  75.9 24.4 %collective-permute-start.12 = (bf16[64,1024]{1,0:T(8,128)(2,1)}, bf16[64,1024]{1,0:T(8,128)(2,1)S(1)}, u32[]{:S(2)}, u32[]{:S(2)}) collective-permute-start(bf16[64,1024]{1,0:T(8,128)(2,1)} %shard_map.81.refs_0_), channel_id=1, source_target_pairs={{0,6},{1,7},{2,4},{3,5},{4,2},{5,3},{6,0},{7,1},{8,14},{9,15},{10,... | collective-permute-start | bytes 393224 | tf_op jit(solution)/shard_map/ppermute | solution.py:405
  79.5 20.9 %collective-permute-start.13 = (bf16[64,1024]{1,0:T(8,128)(2,1)}, bf16[64,1024]{1,0:T(8,128)(2,1)S(1)}, u32[]{:S(2)}, u32[]{:S(2)}) collective-permute-start(bf16[64,1024]{1,0:T(8,128)(2,1)} %shard_map.81.refs_0_), channel_id=1, source_target_pairs={{0,4},{1,5},{2,6},{3,7},{4,0},{5,1},{6,2},{7,3},{8,12},{9,13},{10,... | collective-permute-start | bytes 393224 | tf_op jit(solution)/shard_map/ppermute | solution.py:405
  82.3 15.9 %collective-permute-start.14 = (bf16[64,1024]{1,0:T(8,128)(2,1)}, bf16[64,1024]{1,0:T(8,128)(2,1)S(1)}, u32[]{:S(2)}, u32[]{:S(2)}) collective-permute-start(bf16[64,1024]{1,0:T(8,128)(2,1)} %shard_map.81.refs_0_), channel_id=1, source_target_pairs={{0,2},{1,3},{2,0},{3,1},{4,6},{5,7},{6,4},{7,5},{8,10},{9,11},{10,... | collective-permute-start | bytes 393224 | tf_op jit(solution)/shard_map/ppermute | solution.py:405
  82.5 25.3 %collective-permute-start.11 = (bf16[256,1024]{1,0:T(8,128)(2,1)S(1)}, bf16[256,1024]{1,0:T(8,128)(2,1)S(1)}, u32[]{:S(2)}, u32[]{:S(2)}) collective-permute-start(bf16[256,1024]{1,0:T(8,128)(2,1)S(1)} %collective-permute-done.5), channel_id=1, source_target_pairs={{4,6},{5,7},{2,0},{3,1},{12,14},{13,15},{10,8},{11,9},{20,22},{21,... | collective-permute-start | bytes 1572872 | tf_op jit(solution)/shard_map/ppermute | solution.py:414
  98.1 10.9 %copy-start.10 = (bf16[64,1024]{1,0:T(8,128)(2,1)}, bf16[64,1024]{1,0:T(8,128)(2,1)S(1)}, u32[]{:S(2)}) copy-start(bf16[64,1024]{1,0:T(8,128)(2,1)S(1)} %collective-permute-done.14.refs_1_) | copy-start | bytes 393220
  100.3 8.7 %copy-start.9 = (bf16[64,1024]{1,0:T(8,128)(2,1)}, bf16[64,1024]{1,0:T(8,128)(2,1)S(1)}, u32[]{:S(2)}) copy-start(bf16[64,1024]{1,0:T(8,128)(2,1)S(1)} %collective-permute-done.13.refs_2_) | copy-start | bytes 393220
  100.4 8.7 %copy-start.8 = (bf16[64,1024]{1,0:T(8,128)(2,1)}, bf16[64,1024]{1,0:T(8,128)(2,1)S(1)}, u32[]{:S(2)}) copy-start(bf16[64,1024]{1,0:T(8,128)(2,1)S(1)} %collective-permute-done.12.refs_3_) | copy-start | bytes 393220
  109.1 74.1 %copy-start.2 = (bf16[3,256,1024]{2,1,0:T(8,128)(2,1)}, bf16[3,256,1024]{2,1,0:T(8,128)(2,1)S(1)}, u32[]{:S(2)}) copy-start(bf16[3,256,1024]{2,1,0:T(8,128)(2,1)S(1)} %pad_maximum_fusion.refs_2_) | copy-start | bytes 4718596
  111.5 7.0 %collective-permute-start.17 = (bf16[64,1024]{1,0:T(8,128)(2,1)}, bf16[64,1024]{1,0:T(8,128)(2,1)S(1)}, u32[]{:S(2)}, u32[]{:S(2)}) collective-permute-start(bf16[64,1024]{1,0:T(8,128)(2,1)} %shard_map.83.refs_0_), channel_id=1, source_target_pairs={{0,24},{1,25},{2,26},{3,27},{4,28},{5,29},{6,30},{7,31},{8,16},{9,... | collective-permute-start | bytes 393224 | tf_op jit(solution)/shard_map/ppermute | solution.py:405
  113.9 7.0 %collective-permute-start.16 = (bf16[64,1024]{1,0:T(8,128)(2,1)}, bf16[64,1024]{1,0:T(8,128)(2,1)S(1)}, u32[]{:S(2)}, u32[]{:S(2)}) collective-permute-start(bf16[64,1024]{1,0:T(8,128)(2,1)} %shard_map.83.refs_0_), channel_id=1, source_target_pairs={{0,16},{1,17},{2,18},{3,19},{4,20},{5,21},{6,22},{7,23},{8,24},{9,... | collective-permute-start | bytes 393224 | tf_op jit(solution)/shard_map/ppermute | solution.py:405
  114.4 6.5 %collective-permute-start.15 = (bf16[64,1024]{1,0:T(8,128)(2,1)}, bf16[64,1024]{1,0:T(8,128)(2,1)S(1)}, u32[]{:S(2)}, u32[]{:S(2)}) collective-permute-start(bf16[64,1024]{1,0:T(8,128)(2,1)} %shard_map.83.refs_0_), channel_id=1, source_target_pairs={{0,8},{1,9},{2,10},{3,11},{4,12},{5,13},{6,14},{7,15},{8,0},{9,1},... | collective-permute-start | bytes 393224 | tf_op jit(solution)/shard_map/ppermute | solution.py:405
  118.6 2.4 %copy-start.14 = (bf16[64,1024]{1,0:T(8,128)(2,1)}, bf16[64,1024]{1,0:T(8,128)(2,1)S(1)}, u32[]{:S(2)}) copy-start(bf16[64,1024]{1,0:T(8,128)(2,1)S(1)} %collective-permute-done.17.refs_3_) | copy-start | bytes 393220
  120.9 0.7 copy-start.15
  121.5 0.7 copy-start.16
  124.2 2.9 %collective-permute-start.18 = (bf16[64,4096]{1,0:T(8,128)(2,1)}, bf16[64,4096]{1,0:T(8,128)(2,1)S(1)}, u32[]{:S(2)}, u32[]{:S(2)}) collective-permute-start(bf16[64,4096]{1,0:T(8,128)(2,1)} %shard_map.84.refs_0_), channel_id=1, source_target_pairs={{0,1},{1,0},{2,3},{3,2},{4,5},{5,4},{6,7},{7,6},{8,9},{9,8},{10,11... | collective-permute-start | bytes 1572872 | tf_op jit(solution)/shard_map/ppermute | solution.py:405
  124.3 41.6 %collective-permute-start.26 = (bf16[3,256,1024]{2,1,0:T(8,128)(2,1)S(1)}, bf16[3,256,1024]{2,1,0:T(8,128)(2,1)}, u32[]{:S(2)}, u32[]{:S(2)}) collective-permute-start(bf16[3,256,1024]{2,1,0:T(8,128)(2,1)S(1)} %pad_maximum_fusion.refs_2_), channel_id=1, source_target_pairs={{0,16},{1,17},{2,18},{3,19},{4,20},{5,21},{6,22},{7,23},{8,24},{9,... | collective-permute-start | bytes 4718600 | tf_op jit(solution)/shard_map/ppermute | solution.py:405
  125.8 42.9 %collective-permute-start.27 = (bf16[3,256,1024]{2,1,0:T(8,128)(2,1)S(1)}, bf16[3,256,1024]{2,1,0:T(8,128)(2,1)}, u32[]{:S(2)}, u32[]{:S(2)}) collective-permute-start(bf16[3,256,1024]{2,1,0:T(8,128)(2,1)S(1)} %pad_maximum_fusion.refs_2_), channel_id=1, source_target_pairs={{0,8},{1,9},{2,10},{3,11},{4,12},{5,13},{6,14},{7,15},{8,0},{9,1},... | collective-permute-start | bytes 4718600 | tf_op jit(solution)/shard_map/ppermute | solution.py:405
  127.1 0.8 copy-start.3
  130.2 18.0 %copy-start = (bf16[64,8192]{1,0:T(8,128)(2,1)S(1)}, bf16[64,8192]{1,0:T(8,128)(2,1)}, u32[]{:S(2)}) copy-start(bf16[64,8192]{1,0:T(8,128)(2,1)} %shard_map.85.p_all.p_own) | copy-start | bytes 3145732
  140.8 1.6 collective-permute-start.19
  142.4 0.7 copy-start.7
  144.7 18.5 %collective-permute-start.22 = (f32[64,128]{1,0:T(8,128)}, f32[64,128]{1,0:T(8,128)S(1)}, u32[]{:S(2)}, u32[]{:S(2)}) collective-permute-start(f32[64,128]{1,0:T(8,128)} %get-tuple-element.149), channel_id=1, source_target_pairs={{0,24},{1,25},{2,26},{3,27},{4,28},{5,29},{6,30},{7,31},{8,16},{9,... | collective-permute-start | bytes 98312 | tf_op jit(solution)/shard_map/ppermute | solution.py:405
  146.2 17.1 %collective-permute-start.21 = (f32[64,128]{1,0:T(8,128)}, f32[64,128]{1,0:T(8,128)S(1)}, u32[]{:S(2)}, u32[]{:S(2)}) collective-permute-start(f32[64,128]{1,0:T(8,128)} %get-tuple-element.148), channel_id=1, source_target_pairs={{0,16},{1,17},{2,18},{3,19},{4,20},{5,21},{6,22},{7,23},{8,24},{9,... | collective-permute-start | bytes 98312 | tf_op jit(solution)/shard_map/ppermute | solution.py:405
  147.5 16.1 %collective-permute-start.20 = (f32[64,128]{1,0:T(8,128)}, f32[64,128]{1,0:T(8,128)S(1)}, u32[]{:S(2)}, u32[]{:S(2)}) collective-permute-start(f32[64,128]{1,0:T(8,128)} %get-tuple-element.147), channel_id=1, source_target_pairs={{0,8},{1,9},{2,10},{3,11},{4,12},{5,13},{6,14},{7,15},{8,0},{9,1},... | collective-permute-start | bytes 98312 | tf_op jit(solution)/shard_map/ppermute | solution.py:405
  165.9 4.8 %copy-start.6 = (f32[64,128]{1,0:T(8,128)S(1)}, f32[64,128]{1,0:T(8,128)}, u32[]{:S(2)}) copy-start(f32[64,128]{1,0:T(8,128)} %shard_map.88.refs_0_) | copy-start | bytes 98308
  167.1 20.2 %collective-permute-start.29 = (bf16[3,256,512]{2,1,0:T(8,128)(2,1)S(1)}, bf16[3,256,512]{2,1,0:T(8,128)(2,1)S(1)}, u32[]{:S(2)}, u32[]{:S(2)}) collective-permute-start(bf16[3,256,512]{2,1,0:T(8,128)(2,1)S(1)} %slice.23), channel_id=1, source_target_pairs={{0,8},{1,9},{2,10},{3,11},{4,12},{5,13},{6,14},{7,15},{8,0},{9,1},... | collective-permute-start | bytes 2359304 | tf_op jit(solution)/shard_map/ppermute | solution.py:405
  169.9 18.9 %collective-permute-start.28 = (bf16[3,256,512]{2,1,0:T(8,128)(2,1)S(1)}, bf16[3,256,512]{2,1,0:T(8,128)(2,1)S(1)}, u32[]{:S(2)}, u32[]{:S(2)}) collective-permute-start(bf16[3,256,512]{2,1,0:T(8,128)(2,1)S(1)} %slice.22), channel_id=1, source_target_pairs={{0,16},{1,17},{2,18},{3,19},{4,20},{5,21},{6,22},{7,23},{8,24},{9,... | collective-permute-start | bytes 2359304 | tf_op jit(solution)/shard_map/ppermute | solution.py:405
  170.7 6.3 %collective-permute-start.25 = (f32[64,128]{1,0:T(8,128)S(1)}, f32[64,128]{1,0:T(8,128)S(1)}, u32[]{:S(2)}, u32[]{:S(2)}) collective-permute-start(f32[64,128]{1,0:T(8,128)S(1)} %copy-done.6), channel_id=1, source_target_pairs={{0,2},{1,3},{2,0},{3,1},{4,6},{5,7},{6,4},{7,5},{8,10},{9,11},{10,... | collective-permute-start | bytes 98312 | tf_op jit(solution)/shard_map/ppermute | solution.py:405
  170.7 6.3 %collective-permute-start.24 = (f32[64,128]{1,0:T(8,128)S(1)}, f32[64,128]{1,0:T(8,128)S(1)}, u32[]{:S(2)}, u32[]{:S(2)}) collective-permute-start(f32[64,128]{1,0:T(8,128)S(1)} %copy-done.6), channel_id=1, source_target_pairs={{0,4},{1,5},{2,6},{3,7},{4,0},{5,1},{6,2},{7,3},{8,12},{9,13},{10,... | collective-permute-start | bytes 98312 | tf_op jit(solution)/shard_map/ppermute | solution.py:405
  173.5 6.6 %collective-permute-start.23 = (f32[64,128]{1,0:T(8,128)S(1)}, f32[64,128]{1,0:T(8,128)S(1)}, u32[]{:S(2)}, u32[]{:S(2)}) collective-permute-start(f32[64,128]{1,0:T(8,128)S(1)} %copy-done.6), channel_id=1, source_target_pairs={{0,6},{1,7},{2,4},{3,5},{4,2},{5,3},{6,0},{7,1},{8,14},{9,15},{10,... | collective-permute-start | bytes 98312 | tf_op jit(solution)/shard_map/ppermute | solution.py:405
  177.0 3.0 %copy-start.20 = (f32[64,128]{1,0:T(8,128)}, f32[64,128]{1,0:T(8,128)S(1)}, u32[]{:S(2)}) copy-start(f32[64,128]{1,0:T(8,128)S(1)} %collective-permute-done.25.refs_1_) | copy-start | bytes 98308
  177.1 3.0 %copy-start.21 = (f32[64,128]{1,0:T(8,128)}, f32[64,128]{1,0:T(8,128)S(1)}, u32[]{:S(2)}) copy-start(f32[64,128]{1,0:T(8,128)S(1)} %collective-permute-done.24.refs_2_) | copy-start | bytes 98308
  182.1 5.3 %collective-permute-start.32 = (f32[64,128]{1,0:T(8,128)}, f32[64,128]{1,0:T(8,128)S(1)}, u32[]{:S(2)}, u32[]{:S(2)}) collective-permute-start(f32[64,128]{1,0:T(8,128)} %shard_map.89.refs_0_), channel_id=1, source_target_pairs={{0,24},{1,25},{2,26},{3,27},{4,28},{5,29},{6,30},{7,31},{8,16},{9,... | collective-permute-start | bytes 98312 | tf_op jit(solution)/shard_map/ppermute | solution.py:405
  183.3 22.3 %collective-permute-start.33 = (bf16[3,256,1024]{2,1,0:T(8,128)(2,1)S(1)}, bf16[3,256,1024]{2,1,0:T(8,128)(2,1)}, u32[]{:S(2)}, u32[]{:S(2)}) collective-permute-start(bf16[3,256,1024]{2,1,0:T(8,128)(2,1)S(1)} %pad_maximum_fusion.refs_2_), channel_id=1, source_target_pairs={{0,1},{1,0},{2,3},{3,2},{4,5},{5,4},{6,7},{7,6},{8,9},{9,8},{10,11... | collective-permute-start | bytes 4718600 | tf_op jit(solution)/shard_map/ppermute | solution.py:405
  183.3 22.3 %collective-permute-start.35 = (bf16[3,256,1024]{2,1,0:T(8,128)(2,1)}, bf16[3,256,1024]{2,1,0:T(8,128)(2,1)}, u32[]{:S(2)}, u32[]{:S(2)}) collective-permute-start(bf16[3,256,1024]{2,1,0:T(8,128)(2,1)} %collective-permute-done.26.refs_6_), channel_id=1, source_target_pairs={{0,1},{1,0},{2,3},{3,2},{4,5},{5,4},{6,7},{7,6},{8,9},{9,8},{10,11... | collective-permute-start | bytes 4718600 | tf_op jit(solution)/shard_map/ppermute | solution.py:405
  187.3 5.6 %copy-start.23 = (f32[64,128]{1,0:T(8,128)}, f32[64,128]{1,0:T(8,128)S(1)}, u32[]{:S(2)}) copy-start(f32[64,128]{1,0:T(8,128)S(1)} %collective-permute-done.32.refs_3_) | copy-start | bytes 98308
  187.3 18.3 %collective-permute-start.34 = (bf16[3,256,1024]{2,1,0:T(8,128)(2,1)}, bf16[3,256,1024]{2,1,0:T(8,128)(2,1)}, u32[]{:S(2)}, u32[]{:S(2)}) collective-permute-start(bf16[3,256,1024]{2,1,0:T(8,128)(2,1)} %collective-permute-done.27.refs_4_), channel_id=1, source_target_pairs={{0,1},{1,0},{2,3},{3,2},{4,5},{5,4},{6,7},{7,6},{8,9},{9,8},{10,11... | collective-permute-start | bytes 4718600 | tf_op jit(solution)/shard_map/ppermute | solution.py:405
  187.3 7.7 %copy-start.26 = (bf16[3,256,512]{2,1,0:T(8,128)(2,1)}, bf16[3,256,512]{2,1,0:T(8,128)(2,1)S(1)}, u32[]{:S(2)}) copy-start(bf16[3,256,512]{2,1,0:T(8,128)(2,1)S(1)} %collective-permute-done.29.refs_8_) | copy-start | bytes 2359300
  187.3 4.2 %collective-permute-start.31 = (f32[64,128]{1,0:T(8,128)}, f32[64,128]{1,0:T(8,128)S(1)}, u32[]{:S(2)}, u32[]{:S(2)}) collective-permute-start(f32[64,128]{1,0:T(8,128)} %shard_map.89.refs_0_), channel_id=1, source_target_pairs={{0,16},{1,17},{2,18},{3,19},{4,20},{5,21},{6,22},{7,23},{8,24},{9,... | collective-permute-start | bytes 98312 | tf_op jit(solution)/shard_map/ppermute | solution.py:405
  188.8 6.2 %copy-start.27 = (bf16[3,256,512]{2,1,0:T(8,128)(2,1)}, bf16[3,256,512]{2,1,0:T(8,128)(2,1)S(1)}, u32[]{:S(2)}) copy-start(bf16[3,256,512]{2,1,0:T(8,128)(2,1)S(1)} %collective-permute-done.28.refs_9_) | copy-start | bytes 2359300
  188.8 4.1 %collective-permute-start.30 = (f32[64,128]{1,0:T(8,128)}, f32[64,128]{1,0:T(8,128)S(1)}, u32[]{:S(2)}, u32[]{:S(2)}) collective-permute-start(f32[64,128]{1,0:T(8,128)} %shard_map.89.refs_0_), channel_id=1, source_target_pairs={{0,8},{1,9},{2,10},{3,11},{4,12},{5,13},{6,14},{7,15},{8,0},{9,1},... | collective-permute-start | bytes 98312 | tf_op jit(solution)/shard_map/ppermute | solution.py:405
  191.5 1.4 copy-start.24
  195.0 1.6 collective-permute-start.38
  195.1 10.5 %collective-permute-start.36 = (bf16[3,256,512]{2,1,0:T(8,128)(2,1)}, bf16[3,256,512]{2,1,0:T(8,128)(2,1)}, u32[]{:S(2)}, u32[]{:S(2)}) collective-permute-start(bf16[3,256,512]{2,1,0:T(8,128)(2,1)} %copy-done.26), channel_id=1, source_target_pairs={{0,1},{1,0},{2,3},{3,2},{4,5},{5,4},{6,7},{7,6},{8,9},{9,8},{10,11... | collective-permute-start | bytes 2359304 | tf_op jit(solution)/shard_map/ppermute | solution.py:405
  196.6 2.3 copy-start.5
  196.6 9.0 %collective-permute-start.37 = (bf16[3,256,512]{2,1,0:T(8,128)(2,1)}, bf16[3,256,512]{2,1,0:T(8,128)(2,1)}, u32[]{:S(2)}, u32[]{:S(2)}) collective-permute-start(bf16[3,256,512]{2,1,0:T(8,128)(2,1)} %copy-done.27), channel_id=1, source_target_pairs={{0,1},{1,0},{2,3},{3,2},{4,5},{5,4},{6,7},{7,6},{8,9},{9,8},{10,11... | collective-permute-start | bytes 2359304 | tf_op jit(solution)/shard_map/ppermute | solution.py:405
  (6 other events, 3.7 us)
Sparse Core Ops, SparseCore 0:
  41.9 56.4 reduce-scatter.4
  109.3 112.8 reduce-scatter.2

commit v3 on v2

--- a/solution.py
+++ b/solution.py
@@ -55,7 +55,7 @@
         ),
         out_shape=jax.ShapeDtypeStruct((chips * tall, width), bf16),
         compiler_params=params(),
-        cost_estimate=cost(4 * tok * width * tall * chips, 4 * chips * tall * (width + tok)),
+        cost_estimate=cost(1, 1),
     )(scalars(c), cot, other_cot, tokens, other)
 
 
@@ -563,6 +563,8 @@
             if 0 < h < chips - 2:
                 near[-1], across[-1] = after(near[-1]), after(across[-1])
                 yield
+        near[-1] = after(near[-1])
+        yield
         toward = jnp.where(z % 2 == 0, 1, -1)
         count = jnp.where(z % 2 == 0, chips - 1 - z, z)
         slots, sources = [], []
@@ -611,7 +613,7 @@
         yield
 
     chains = {"R": gradient(), "L": low_rank_chain(), "W": weights(), "O": own_weights()}
-    order = "OWLWROWRLLLWRLWRLLWLLLLWLLWLLW"
+    order = "OWLWROWRWLLLRLWRWLLWLLLLWLLWLLW"
     for name in order:
         next(chains[name], None)
     for name in "LWR":

time: 235 us -> 233 us (level)
  waiting for transfers between devices: 57.3 us -> 52.9 us
  starting transfers between devices: 41.4 us -> 44.4 us
    ppermute x5, waiting for transfers between devices: 15.8 us -> 8.39 us  [along(): return lax.ppermute(after(value), AXES, moves)]
    ppermute x34, starting transfers between devices: 31.7 us -> 34.8 us  [swap(): lax.ppermute(after(value), AXES, [(i, i ^ mask) for i in range(world)])]
    unnamed x58 -> x56, local copies, waits for them, and re-layouts: 6.99 us -> 7.91 us
  transfers between devices with their start and end apart: 41 -> 41, of which waited for: 21 -> 20; matrix products, arithmetic and copies ran while one was open for 11% -> 10% of each run, Pallas kernels for 36% -> 36%
where the time goes in v3:
time: 233 us; the launch traced here: 232 us
  Pallas kernels  88.1 us (38%)
  waiting for transfers between devices  52.9 us (23%)
  starting transfers between devices  44.4 us (19%)
  between operations  15 us (6%)
  other arithmetic  14.2 us (6%)
  local copies, waits for them, and re-layouts  13.4 us (6%)
  matrix products  3.94 us (2%)
    ppermute x34, waiting for transfers between devices, swap(): lax.ppermute(after(value), AXES, [(i, i ^ mask) for i in range(world)])  38.8 us
    ppermute x34, starting transfers between devices, swap(): lax.ppermute(after(value), AXES, [(i, i ^ mask) for i in range(world)])  34.8 us
    pallas_call x2, Pallas kernels, project(): pl.pallas_call(lambda *refs: project_kernel(parts, *refs), grid_spec=pltp...  20.2 us
    pallas_call x2, Pallas kernels, partials(): pl.pallas_call(kernel, grid_spec=pltpu.PrefetchScalarGridSpec(num_scalar_...  20.1 us
    pallas_call x10, Pallas kernels, on_core(): pl.pallas_call(kernel, grid_spec=pltpu.PrefetchScalarGridSpec(num_scalar_...  18.5 us
    pallas_call x1, Pallas kernels, right_part(): pl.pallas_call(kernel, grid_spec=pltpu.PrefetchScalarGridSpec(num_scalar_...  10.8 us
    ppermute x5, starting transfers between devices, along(): return lax.ppermute(after(value), AXES, moves)  9.45 us
    ppermute x5, waiting for transfers between devices, along(): return lax.ppermute(after(value), AXES, moves)  8.39 us
  transfers between devices with their start and end apart: 41, of which 20 were waited for; matrix products, arithmetic and copies ran while one was open for 10% of the time, Pallas kernels for 36%

profile of v3, /device:TPU:0, one launch (start us, length us, event | category | flops | bytes accessed | tf_op | source)
XLA Modules:
  0.0 231.9 jit_solution(3038508883260125127)
XLA Ops:
  8.2 1.1 constant_dynamic-slice_fusion
  10.0 5.5 %collective-permute-start = (bf16[256,1024]{1,0:T(8,128)(2,1)S(1)}, bf16[256,1024]{1,0:T(8,128)(2,1)S(1)}, u32[]{:S(2)}, u32[]{:S(2)}) collective-permute-start(bf16[256,1024]{1,0:T(8,128)(2,1)S(1)} %constant_dynamic-slice_fusion), channel_id=1, source_target_pairs={{0,2},{1,3},{4,6},{5,7},{2,0},{3,1},{6,4},{7,5},{8,10},{9,11},{12,... | collective-permute-start | bytes 1572872 | tf_op jit(solution)/shard_map/ppermute | solution.py:414
  15.5 4.4 %shard_map.76 = (bf16[64,4096]{1,0:T(8,128)(2,1)}, bf16[128,512]{1,0:T(8,128)(2,1)}) custom-call(s32[1]{0:T(128)} %bitcast.9.index, f32[64,1024]{1,0:T(8,128)} %bitcast.44, bf16[512,1024]{1,0:T(8,128)(2,1)} %refs_1_.1, bf16[512,8192]{1,0:T(8,128)(2,1)} %second.5, bf16[512,8192]{1,0:T(8,128)(2,1)} %second.5), custom_call_target="tpu_custom_call" | custom-call | flops 536870912 | bytes 4194304 | tf_op jit(solution)/shard_map/pallas_call | solution.py:136
  19.9 2.5 %collective-permute-done.3.other = bf16[512,8192]{1,0:T(8,128)(2,1)} collective-permute-done((bf16[512,8192]{1,0:T(8,128)(2,1)}, bf16[512,8192]{1,0:T(8,128)(2,1)}, u32[]{:S(2)}, u32[]{:S(2)}) %collective-permute-start.3) | collective-permute-done | bytes 8388640 | tf_op jit(solution)/shard_map/ppermute | solution.py:405
  22.4 3.0 %collective-permute-done.2 = bf16[1024,1024]{1,0:T(8,128)(2,1)} collective-permute-done((bf16[1024,1024]{1,0:T(8,128)(2,1)}, bf16[1024,1024]{1,0:T(8,128)(2,1)}, u32[]{:S(2)}, u32[]{:S(2)}) %collective-permute-start.2) | collective-permute-done | bytes 2097184 | tf_op jit(solution)/shard_map/ppermute | solution.py:405
  25.4 1.3 collective-permute-start.6
  26.6 1.1 collective-permute-done
  28.5 6.1 %shard_map.77 = bf16[1024,1024]{1,0:T(8,128)(2,1)} custom-call(s32[1]{0:T(128)} %bitcast.5.index, bf16[512,1024]{1,0:T(8,128)(2,1)} %refs_1_.1, bf16[512,1024]{1,0:T(8,128)(2,1)} %copy-done.1, bf16[512,8192]{1,0:T(8,128)(2,1)} %second.5, bf16[512,8192]{1,0:T(8,128)(2,1)} %collective-permute-done.3.other), custom_call_target="tpu_custom_call" | custom-call | flops 1 | bytes 1 | tf_op jit(solution)/shard_map/pallas_call | solution.py:48
  34.5 7.2 %collective-permute-done.6 = bf16[256,1024]{1,0:T(8,128)(2,1)S(1)} collective-permute-done((bf16[256,1024]{1,0:T(8,128)(2,1)S(1)}, bf16[256,1024]{1,0:T(8,128)(2,1)S(1)}, u32[]{:S(2)}, u32[]{:S(2)}) %collective-permute-start.6) | collective-permute-done | bytes 524320 | tf_op jit(solution)/shard_map/ppermute | solution.py:414
  42.5 1.3 collective-permute-start.11
  43.8 7.2 %shard_map.78 = (bf16[512,8192]{1,0:T(8,128)(2,1)}, s32[8,128]{1,0:T(8,128)}) custom-call(s32[1,2]{1,0:T(1,128)} %add_bitcast_fusion.refs_0_, bf16[512,1024]{1,0:T(8,128)(2,1)} %refs_1_.1, bf16[1,1024,1024]{2,1,0:T(8,128)(2,1)} %bitcast.47, bf16[1,1024,1024]{2,1,0:T(8,128)(2,1)} %bitcast.12.refs_3_), custom_call_target="tpu_custom_call" | custom-call | flops 2147483648 | bytes 6291456 | tf_op jit(solution)/shard_map/pallas_call | solution.py:361
  51.0 1.2 slice.19
  53.4 6.8 %shard_map.79.refs_0_ = f32[64,4096]{1,0:T(8,128)} custom-call(s32[2]{0:T(128)} %pad_add_fusion.2.index, f32[64,1024]{1,0:T(8,128)} %bitcast.45, bf16[128,512]{1,0:T(8,128)(2,1)} %get-tuple-element.105.factor, bf16[512,8192]{1,0:T(8,128)(2,1)} %second.5, bf16[512,8192]{1,0:T(8,128)(2,1)} %second.5, f32[1024,1024]{1,0:T(8,128)} %bitcast.38), custom_call_target="tpu_custom_call" | custom-call | flops 536870912 | bytes 8388608 | tf_op jit(solution)/shard_map/pallas_call | solution.py:186
  60.2 0.8 copy-done.4
  61.0 2.3 shard_map.80
  63.3 3.2 %collective-permute-start.10 = (bf16[64,1024]{1,0:T(8,128)(2,1)}, bf16[64,1024]{1,0:T(8,128)(2,1)S(1)}, u32[]{:S(2)}, u32[]{:S(2)}) collective-permute-start(bf16[64,1024]{1,0:T(8,128)(2,1)} %get-tuple-element.118), channel_id=1, source_target_pairs={{0,24},{1,25},{2,26},{3,27},{4,28},{5,29},{6,30},{7,31},{8,16},{9,... | collective-permute-start | bytes 393224 | tf_op jit(solution)/shard_map/ppermute | solution.py:405
  67.1 3.9 %collective-permute-done.10.refs_3_ = bf16[64,1024]{1,0:T(8,128)(2,1)S(1)} collective-permute-done((bf16[64,1024]{1,0:T(8,128)(2,1)}, bf16[64,1024]{1,0:T(8,128)(2,1)S(1)}, u32[]{:S(2)}, u32[]{:S(2)}) %collective-permute-start.10) | collective-permute-done | bytes 131104 | tf_op jit(solution)/shard_map/ppermute | solution.py:405
  71.0 2.7 %collective-permute-done.9.refs_2_ = bf16[64,1024]{1,0:T(8,128)(2,1)S(1)} collective-permute-done((bf16[64,1024]{1,0:T(8,128)(2,1)}, bf16[64,1024]{1,0:T(8,128)(2,1)S(1)}, u32[]{:S(2)}, u32[]{:S(2)}) %collective-permute-start.9) | collective-permute-done | bytes 131104 | tf_op jit(solution)/shard_map/ppermute | solution.py:405
  75.0 1.8 shard_map.81.refs_0_
  76.8 4.9 %collective-permute-start.14 = (bf16[64,1024]{1,0:T(8,128)(2,1)}, bf16[64,1024]{1,0:T(8,128)(2,1)S(1)}, u32[]{:S(2)}, u32[]{:S(2)}) collective-permute-start(bf16[64,1024]{1,0:T(8,128)(2,1)} %shard_map.81.refs_0_), channel_id=1, source_target_pairs={{0,2},{1,3},{2,0},{3,1},{4,6},{5,7},{6,4},{7,5},{8,10},{9,11},{10,... | collective-permute-start | bytes 393224 | tf_op jit(solution)/shard_map/ppermute | solution.py:405
  81.7 1.2 collective-permute-start.13
  82.9 1.5 collective-permute-start.12
  84.4 14.1 %shard_map.82 = bf16[3072,1024]{1,0:T(8,128)(2,1)} custom-call(s32[1]{0:T(128)} %bitcast.5.index, bf16[512,1024]{1,0:T(8,128)(2,1)} %refs_1_.1, bf16[512,1024]{1,0:T(8,128)(2,1)} %copy-done.1, bf16[512,8192]{1,0:T(8,128)(2,1)} %second.5, bf16[512,8192]{1,0:T(8,128)(2,1)} %collective-permute-done.3.other), custom_call_target="tpu_custom_call" | custom-call | flops 1 | bytes 1 | tf_op jit(solution)/shard_map/pallas_call | solution.py:48
  98.5 4.0 %collective-permute-done.12.refs_3_ = bf16[64,1024]{1,0:T(8,128)(2,1)S(1)} collective-permute-done((bf16[64,1024]{1,0:T(8,128)(2,1)}, bf16[64,1024]{1,0:T(8,128)(2,1)S(1)}, u32[]{:S(2)}, u32[]{:S(2)}) %collective-permute-start.12) | collective-permute-done | bytes 131104 | tf_op jit(solution)/shard_map/ppermute | solution.py:405
  103.4 2.4 %shard_map.83.refs_0_ = bf16[64,1024]{1,0:T(8,128)(2,1)} custom-call(s32[1]{0:T(128)} %constant.90.clone.1.index, bf16[64,1024]{1,0:T(8,128)(2,1)} %shard_map.81.refs_0_, bf16[64,1024]{1,0:T(8,128)(2,1)} %copy-done.8, bf16[64,1024]{1,0:T(8,128)(2,1)} %copy-done.9, bf16[64,1024]{1,0:T(8,128)(2,1)} %copy-done.10), custom_call_target="tpu_custom_call" | custom-call | flops 1 | bytes 524288 | tf_op jit(solution)/shard_map/pallas_call | solution.py:274
  106.5 1.8 collective-permute-start.16
  108.3 1.0 collective-permute-start.15
  109.3 3.9 %collective-permute-done.17.refs_3_ = bf16[64,1024]{1,0:T(8,128)(2,1)S(1)} collective-permute-done((bf16[64,1024]{1,0:T(8,128)(2,1)}, bf16[64,1024]{1,0:T(8,128)(2,1)S(1)}, u32[]{:S(2)}, u32[]{:S(2)}) %collective-permute-start.17) | collective-permute-done | bytes 131104 | tf_op jit(solution)/shard_map/ppermute | solution.py:405
  115.1 2.0 shard_map.84.refs_0_
  117.2 1.5 collective-permute-start.26
  119.7 0.8 copy-done.3
  120.5 2.3 shard_map.85.p_all.p_own
  122.8 10.8 %shard_map.86 = (f32[64,512]{1,0:T(8,128)}, f32[64,512]{1,0:T(8,128)}) custom-call(s32[2]{0:T(128)} %pad_add_fusion.1.index, bf16[64,8192]{1,0:T(8,128)(2,1)} %shard_map.85.p_all.p_own, bf16[64,8192]{1,0:T(8,128)(2,1)} %shard_map.85.p_all.p_own, bf16[512,8192]{1,0:T(8,128)(2,1)} %second.5, bf16[512,8192]{1,0:T(8,128)(2,1)} %second.5, ...), custom_call_target="tpu_custom_call" | custom-call | flops 536870912 | bytes 12582912 | tf_op jit(solution)/shard_map/pallas_call | solution.py:241
  133.5 1.6 collective-permute-done.19.refs_1_
  135.8 1.6 shard_map.87
  137.4 1.5 collective-permute-start.22
  138.9 1.6 collective-permute-start.21
  141.4 5.8 %cholesky.17 = f32[64,64]{1,0:T(8,128)S(1)} custom-call(f32[64,64]{1,0:T(8,128)S(1)} %fusion.5), custom_call_target="Cholesky" | custom-call | tf_op jit(solution)/shard_map/jit(cholesky)/cholesky | solution.py:528
  148.6 4.9 %custom-call.6 = f32[1,64,64]{1,2,0:T(8,128)S(1)} custom-call(f32[1,64,64]{2,1,0:T(8,128)S(1)} %fusion.2), custom_call_target="InvertDiagBlocksLowerTriangular" | custom-call | tf_op jit(solution)/shard_map/triangular_solve | solution.py:529
  153.7 2.5 %collective-permute-done.22.refs_3_ = f32[64,128]{1,0:T(8,128)S(1)} collective-permute-done((f32[64,128]{1,0:T(8,128)}, f32[64,128]{1,0:T(8,128)S(1)}, u32[]{:S(2)}, u32[]{:S(2)}) %collective-permute-start.22) | collective-permute-done | bytes 32800 | tf_op jit(solution)/shard_map/ppermute | solution.py:405
  157.4 1.4 shard_map.88.refs_0_
  158.9 1.2 slice.23
  160.1 1.6 collective-permute-start.29
  161.6 1.2 slice.22
  163.3 2.9 %collective-permute-start.25 = (f32[64,128]{1,0:T(8,128)S(1)}, f32[64,128]{1,0:T(8,128)S(1)}, u32[]{:S(2)}, u32[]{:S(2)}) collective-permute-start(f32[64,128]{1,0:T(8,128)S(1)} %copy-done.6), channel_id=1, source_target_pairs={{0,2},{1,3},{2,0},{3,1},{4,6},{5,7},{6,4},{7,5},{8,10},{9,11},{10,... | collective-permute-start | bytes 98312 | tf_op jit(solution)/shard_map/ppermute | solution.py:405
  166.7 1.9 collective-permute-start.23
  168.6 2.1 collective-permute-done.25.refs_1_
  170.6 5.4 %collective-permute-done.24.refs_2_ = f32[64,128]{1,0:T(8,128)S(1)} collective-permute-done((f32[64,128]{1,0:T(8,128)S(1)}, f32[64,128]{1,0:T(8,128)S(1)}, u32[]{:S(2)}, u32[]{:S(2)}) %collective-permute-start.24) | collective-permute-done | bytes 32800 | tf_op jit(solution)/shard_map/ppermute | solution.py:405
  177.3 1.4 shard_map.89.refs_0_
  178.7 2.2 collective-permute-start.32
  181.4 2.3 %collective-permute-done.32.refs_3_ = f32[64,128]{1,0:T(8,128)S(1)} collective-permute-done((f32[64,128]{1,0:T(8,128)}, f32[64,128]{1,0:T(8,128)S(1)}, u32[]{:S(2)}, u32[]{:S(2)}) %collective-permute-start.32) | collective-permute-done | bytes 32800 | tf_op jit(solution)/shard_map/ppermute | solution.py:405
  183.8 1.3 collective-permute-start.31
  185.0 1.6 collective-permute-start.30
  186.6 1.4 collective-permute-done.31.refs_2_
  187.9 1.2 collective-permute-done.30.refs_1_
  189.7 1.5 shard_map.90.refs_0_
  191.7 1.0 collective-permute-done.38.refs_1_
  193.8 1.3 fusion.hat
  195.1 1.7 shard_map.92
  196.8 2.0 convolution_multiply_fusion.q
  198.8 13.0 %shard_map.91 = (bf16[512,8192]{1,0:T(8,128)(2,1)}, s32[8,128]{1,0:T(8,128)}) custom-call(s32[3,8]{1,0:T(4,128)} %stack.77.refs_0_, bf16[512,1024]{1,0:T(8,128)(2,1)} %refs_1_.1, bf16[3,256,1024]{2,1,0:T(8,128)(2,1)} %copy-done.2, bf16[3,256,1024]{2,1,0:T(8,128)(2,1)} %collective-permute-done.33.refs_3_, ...), custom_call_target="tpu_custom_call", output_to_operand_aliasing={{0}: (12, {})} | custom-call | flops 6442450944 | bytes 18874368 | tf_op jit(solution)/shard_map/pallas_call | solution.py:361
  211.9 3.0 %shard_map.93.refs_0_ = f32[1024,1024]{1,0:T(8,128)} custom-call(bf16[256,1024]{1,0:T(8,128)(2,1)} %reduce-scatter.5.cloned.1.call-done.gradient, f32[1024,1024]{1,0:T(8,128)} %bitcast.40, f32[1024,64]{1,0:T(8,128)} %fusion.hat, f32[64,1024]{1,0:T(8,128)} %convolution_multiply_fusion.q), custom_call_target="tpu_custom_call" | custom-call | flops 100663296 | bytes 2621440 | tf_op jit(solution)/shard_map/pallas_call | solution.py:87
  214.9 5.7 %reduce-scatter.3.cloned.1.call-done.gradient = bf16[768,1024]{1,0:T(8,128)(2,1)} async-done(((bf16[3072,1024]{1,0:T(8,128)(2,1)}), bf16[768,1024]{1,0:T(8,128)(2,1)}) %reduce-scatter.3.cloned.1.call-update) | async-done | bytes 1572880 | tf_op jit(solution)/shard_map/reduce_scatter | solution.py:497
  220.6 4.4 %shard_map.94 = f32[1024,1024]{1,0:T(8,128)} custom-call(bf16[768,1024]{1,0:T(8,128)(2,1)} %reduce-scatter.3.cloned.1.call-done.gradient, f32[1024,1024]{1,0:T(8,128)} %bitcast.41, f32[1024,64]{1,0:T(8,128)} %fusion.hat, f32[64,1024]{1,0:T(8,128)} %convolution_multiply_fusion.q, f32[1024,1024]{1,0:T(8,128)} %shard_map.93.refs_0_), custom_call_target="tpu_custom_call", output_to_operand_aliasing={{}: (4, {})} | custom-call | flops 301989888 | bytes 7864320 | tf_op jit(solution)/shard_map/pallas_call | solution.py:87
  (119 shorter events, 19.3 us)
Async XLA Ops:
  7.2 204.7 %reduce-scatter.5.cloned.1.call-start = ((), (), s32[]{:S(2)}) async-start(), calls=%async_computation.3 | async-start | bytes 2621440 | tf_op jit(solution)/shard_map/reduce_scatter | solution.py:497
  7.2 15.1 %collective-permute-start.3 = (bf16[512,8192]{1,0:T(8,128)(2,1)}, bf16[512,8192]{1,0:T(8,128)(2,1)}, u32[]{:S(2)}, u32[]{:S(2)}) collective-permute-start(bf16[512,8192]{1,0:T(8,128)(2,1)} %second.5), channel_id=1, source_target_pairs={{0,1},{1,0},{2,3},{3,2},{4,5},{5,4},{6,7},{7,6},{8,9},{9,8},{10,11... | collective-permute-start | bytes 25165832 | tf_op jit(solution)/shard_map/ppermute | solution.py:405
  7.7 17.6 %collective-permute-start.2 = (bf16[1024,1024]{1,0:T(8,128)(2,1)}, bf16[1024,1024]{1,0:T(8,128)(2,1)}, u32[]{:S(2)}, u32[]{:S(2)}) collective-permute-start(bf16[1024,1024]{1,0:T(8,128)(2,1)} %param.7), channel_id=1, source_target_pairs={{0,1},{1,0},{2,3},{3,2},{4,5},{5,4},{6,7},{7,6},{8,9},{9,8},{10,11... | collective-permute-start | bytes 6291464 | tf_op jit(solution)/shard_map/ppermute | solution.py:405
  7.8 12.1 %collective-permute-start.4 = (bf16[512,1024]{1,0:T(8,128)(2,1)}, bf16[512,1024]{1,0:T(8,128)(2,1)S(1)}, u32[]{:S(2)}, u32[]{:S(2)}) collective-permute-start(bf16[512,1024]{1,0:T(8,128)(2,1)} %refs_1_.1), channel_id=1, source_target_pairs={{0,1},{1,0},{2,3},{3,2},{4,5},{5,4},{6,7},{7,6},{8,9},{9,8},{10,11... | collective-permute-start | bytes 3145736 | tf_op jit(solution)/shard_map/ppermute | solution.py:405
  9.3 16.0 %collective-permute-start.1 = (bf16[256,1024]{1,0:T(8,128)(2,1)S(1)}, bf16[256,1024]{1,0:T(8,128)(2,1)S(1)}, u32[]{:S(2)}, u32[]{:S(2)}) collective-permute-start(bf16[256,1024]{1,0:T(8,128)(2,1)S(1)} %constant_dynamic-slice_fusion), channel_id=1, source_target_pairs={{2,4},{3,5},{4,2},{5,3},{10,12},{11,13},{12,10},{13,11},{18,20},{1... | collective-permute-start | bytes 1572872 | tf_op jit(solution)/shard_map/ppermute | solution.py:414
  10.0 17.8 %collective-permute-start = (bf16[256,1024]{1,0:T(8,128)(2,1)S(1)}, bf16[256,1024]{1,0:T(8,128)(2,1)S(1)}, u32[]{:S(2)}, u32[]{:S(2)}) collective-permute-start(bf16[256,1024]{1,0:T(8,128)(2,1)S(1)} %constant_dynamic-slice_fusion), channel_id=1, source_target_pairs={{0,2},{1,3},{4,6},{5,7},{2,0},{3,1},{6,4},{7,5},{8,10},{9,11},{12,... | collective-permute-start | bytes 1572872 | tf_op jit(solution)/shard_map/ppermute | solution.py:414
  19.9 8.6 %copy-start.1 = (bf16[512,1024]{1,0:T(8,128)(2,1)}, bf16[512,1024]{1,0:T(8,128)(2,1)S(1)}, u32[]{:S(2)}) copy-start(bf16[512,1024]{1,0:T(8,128)(2,1)S(1)} %collective-permute-done.4.other_cot) | copy-start | bytes 3145732
  25.4 16.4 %collective-permute-start.6 = (bf16[256,1024]{1,0:T(8,128)(2,1)S(1)}, bf16[256,1024]{1,0:T(8,128)(2,1)S(1)}, u32[]{:S(2)}, u32[]{:S(2)}) collective-permute-start(bf16[256,1024]{1,0:T(8,128)(2,1)S(1)} %collective-permute-done.1), channel_id=1, source_target_pairs={{4,6},{5,7},{2,0},{3,1},{12,14},{13,15},{10,8},{11,9},{20,22},{21,... | collective-permute-start | bytes 1572872 | tf_op jit(solution)/shard_map/ppermute | solution.py:414
  27.8 14.0 %collective-permute-start.5 = (bf16[256,1024]{1,0:T(8,128)(2,1)S(1)}, bf16[256,1024]{1,0:T(8,128)(2,1)S(1)}, u32[]{:S(2)}, u32[]{:S(2)}) collective-permute-start(bf16[256,1024]{1,0:T(8,128)(2,1)S(1)} %collective-permute-done), channel_id=1, source_target_pairs={{2,4},{3,5},{4,2},{5,3},{10,12},{11,13},{12,10},{13,11},{18,20},{1... | collective-permute-start | bytes 1572872 | tf_op jit(solution)/shard_map/ppermute | solution.py:414
  41.8 178.8 %reduce-scatter.3.cloned.1.call-start = ((), (), s32[]{:S(2)}) async-start(), calls=%async_computation.2 | async-start | bytes 7864320 | tf_op jit(solution)/shard_map/reduce_scatter | solution.py:497
  41.9 18.3 %collective-permute-start.7 = (bf16[64,4096]{1,0:T(8,128)(2,1)}, bf16[64,4096]{1,0:T(8,128)(2,1)S(1)}, u32[]{:S(2)}, u32[]{:S(2)}) collective-permute-start(bf16[64,4096]{1,0:T(8,128)(2,1)} %get-tuple-element.110), channel_id=1, source_target_pairs={{0,1},{1,0},{2,3},{3,2},{4,5},{5,4},{6,7},{7,6},{8,9},{9,8},{10,11... | collective-permute-start | bytes 1572872 | tf_op jit(solution)/shard_map/ppermute | solution.py:405
  42.5 59.9 %collective-permute-start.11 = (bf16[256,1024]{1,0:T(8,128)(2,1)S(1)}, bf16[256,1024]{1,0:T(8,128)(2,1)S(1)}, u32[]{:S(2)}, u32[]{:S(2)}) collective-permute-start(bf16[256,1024]{1,0:T(8,128)(2,1)S(1)} %collective-permute-done.5), channel_id=1, source_target_pairs={{4,6},{5,7},{2,0},{3,1},{12,14},{13,15},{10,8},{11,9},{20,22},{21,... | collective-permute-start | bytes 1572872 | tf_op jit(solution)/shard_map/ppermute | solution.py:414
  60.2 0.8 copy-start.4
  63.3 7.7 %collective-permute-start.10 = (bf16[64,1024]{1,0:T(8,128)(2,1)}, bf16[64,1024]{1,0:T(8,128)(2,1)S(1)}, u32[]{:S(2)}, u32[]{:S(2)}) collective-permute-start(bf16[64,1024]{1,0:T(8,128)(2,1)} %get-tuple-element.118), channel_id=1, source_target_pairs={{0,24},{1,25},{2,26},{3,27},{4,28},{5,29},{6,30},{7,31},{8,16},{9,... | collective-permute-start | bytes 393224 | tf_op jit(solution)/shard_map/ppermute | solution.py:405
  66.5 7.2 %collective-permute-start.9 = (bf16[64,1024]{1,0:T(8,128)(2,1)}, bf16[64,1024]{1,0:T(8,128)(2,1)S(1)}, u32[]{:S(2)}, u32[]{:S(2)}) collective-permute-start(bf16[64,1024]{1,0:T(8,128)(2,1)} %get-tuple-element.117), channel_id=1, source_target_pairs={{0,16},{1,17},{2,18},{3,19},{4,20},{5,21},{6,22},{7,23},{8,24},{9,... | collective-permute-start | bytes 393224 | tf_op jit(solution)/shard_map/ppermute | solution.py:405
  67.0 6.9 %collective-permute-start.8 = (bf16[64,1024]{1,0:T(8,128)(2,1)}, bf16[64,1024]{1,0:T(8,128)(2,1)S(1)}, u32[]{:S(2)}, u32[]{:S(2)}) collective-permute-start(bf16[64,1024]{1,0:T(8,128)(2,1)} %get-tuple-element.116), channel_id=1, source_target_pairs={{0,8},{1,9},{2,10},{3,11},{4,12},{5,13},{6,14},{7,15},{8,0},{9,1},... | collective-permute-start | bytes 393224 | tf_op jit(solution)/shard_map/ppermute | solution.py:405
  71.0 3.0 %copy-start.11 = (bf16[64,1024]{1,0:T(8,128)(2,1)}, bf16[64,1024]{1,0:T(8,128)(2,1)S(1)}, u32[]{:S(2)}) copy-start(bf16[64,1024]{1,0:T(8,128)(2,1)S(1)} %collective-permute-done.10.refs_3_) | copy-start | bytes 393220
  73.7 0.7 copy-start.12
  74.3 0.7 copy-start.13
  76.8 21.6 %collective-permute-start.14 = (bf16[64,1024]{1,0:T(8,128)(2,1)}, bf16[64,1024]{1,0:T(8,128)(2,1)S(1)}, u32[]{:S(2)}, u32[]{:S(2)}) collective-permute-start(bf16[64,1024]{1,0:T(8,128)(2,1)} %shard_map.81.refs_0_), channel_id=1, source_target_pairs={{0,2},{1,3},{2,0},{3,1},{4,6},{5,7},{6,4},{7,5},{8,10},{9,11},{10,... | collective-permute-start | bytes 393224 | tf_op jit(solution)/shard_map/ppermute | solution.py:405
  81.7 16.7 %collective-permute-start.13 = (bf16[64,1024]{1,0:T(8,128)(2,1)}, bf16[64,1024]{1,0:T(8,128)(2,1)S(1)}, u32[]{:S(2)}, u32[]{:S(2)}) collective-permute-start(bf16[64,1024]{1,0:T(8,128)(2,1)} %shard_map.81.refs_0_), channel_id=1, source_target_pairs={{0,4},{1,5},{2,6},{3,7},{4,0},{5,1},{6,2},{7,3},{8,12},{9,13},{10,... | collective-permute-start | bytes 393224 | tf_op jit(solution)/shard_map/ppermute | solution.py:405
  82.9 19.6 %collective-permute-start.12 = (bf16[64,1024]{1,0:T(8,128)(2,1)}, bf16[64,1024]{1,0:T(8,128)(2,1)S(1)}, u32[]{:S(2)}, u32[]{:S(2)}) collective-permute-start(bf16[64,1024]{1,0:T(8,128)(2,1)} %shard_map.81.refs_0_), channel_id=1, source_target_pairs={{0,6},{1,7},{2,4},{3,5},{4,2},{5,3},{6,0},{7,1},{8,14},{9,15},{10,... | collective-permute-start | bytes 393224 | tf_op jit(solution)/shard_map/ppermute | solution.py:405
  98.4 4.0 %copy-start.8 = (bf16[64,1024]{1,0:T(8,128)(2,1)}, bf16[64,1024]{1,0:T(8,128)(2,1)S(1)}, u32[]{:S(2)}) copy-start(bf16[64,1024]{1,0:T(8,128)(2,1)S(1)} %collective-permute-done.14.refs_1_) | copy-start | bytes 393220
  98.5 4.0 %copy-start.9 = (bf16[64,1024]{1,0:T(8,128)(2,1)}, bf16[64,1024]{1,0:T(8,128)(2,1)S(1)}, u32[]{:S(2)}) copy-start(bf16[64,1024]{1,0:T(8,128)(2,1)S(1)} %collective-permute-done.13.refs_2_) | copy-start | bytes 393220
  102.5 0.7 copy-start.10
  103.4 77.5 %copy-start.2 = (bf16[3,256,1024]{2,1,0:T(8,128)(2,1)}, bf16[3,256,1024]{2,1,0:T(8,128)(2,1)S(1)}, u32[]{:S(2)}) copy-start(bf16[3,256,1024]{2,1,0:T(8,128)(2,1)S(1)} %pad_maximum_fusion.refs_2_) | copy-start | bytes 4718596
  105.8 7.5 %collective-permute-start.17 = (bf16[64,1024]{1,0:T(8,128)(2,1)}, bf16[64,1024]{1,0:T(8,128)(2,1)S(1)}, u32[]{:S(2)}, u32[]{:S(2)}) collective-permute-start(bf16[64,1024]{1,0:T(8,128)(2,1)} %shard_map.83.refs_0_), channel_id=1, source_target_pairs={{0,24},{1,25},{2,26},{3,27},{4,28},{5,29},{6,30},{7,31},{8,16},{9,... | collective-permute-start | bytes 393224 | tf_op jit(solution)/shard_map/ppermute | solution.py:405
  106.5 7.3 %collective-permute-start.16 = (bf16[64,1024]{1,0:T(8,128)(2,1)}, bf16[64,1024]{1,0:T(8,128)(2,1)S(1)}, u32[]{:S(2)}, u32[]{:S(2)}) collective-permute-start(bf16[64,1024]{1,0:T(8,128)(2,1)} %shard_map.83.refs_0_), channel_id=1, source_target_pairs={{0,16},{1,17},{2,18},{3,19},{4,20},{5,21},{6,22},{7,23},{8,24},{9,... | collective-permute-start | bytes 393224 | tf_op jit(solution)/shard_map/ppermute | solution.py:405
  108.3 5.5 %collective-permute-start.15 = (bf16[64,1024]{1,0:T(8,128)(2,1)}, bf16[64,1024]{1,0:T(8,128)(2,1)S(1)}, u32[]{:S(2)}, u32[]{:S(2)}) collective-permute-start(bf16[64,1024]{1,0:T(8,128)(2,1)} %shard_map.83.refs_0_), channel_id=1, source_target_pairs={{0,8},{1,9},{2,10},{3,11},{4,12},{5,13},{6,14},{7,15},{8,0},{9,1},... | collective-permute-start | bytes 393224 | tf_op jit(solution)/shard_map/ppermute | solution.py:405
  113.3 0.7 copy-start.14
  113.8 0.7 copy-start.15
  114.5 0.7 copy-start.16
  117.2 2.5 %collective-permute-start.18 = (bf16[64,4096]{1,0:T(8,128)(2,1)}, bf16[64,4096]{1,0:T(8,128)(2,1)S(1)}, u32[]{:S(2)}, u32[]{:S(2)}) collective-permute-start(bf16[64,4096]{1,0:T(8,128)(2,1)} %shard_map.84.refs_0_), channel_id=1, source_target_pairs={{0,1},{1,0},{2,3},{3,2},{4,5},{5,4},{6,7},{7,6},{8,9},{9,8},{10,11... | collective-permute-start | bytes 1572872 | tf_op jit(solution)/shard_map/ppermute | solution.py:405
  117.2 41.7 %collective-permute-start.26 = (bf16[3,256,1024]{2,1,0:T(8,128)(2,1)S(1)}, bf16[3,256,1024]{2,1,0:T(8,128)(2,1)}, u32[]{:S(2)}, u32[]{:S(2)}) collective-permute-start(bf16[3,256,1024]{2,1,0:T(8,128)(2,1)S(1)} %pad_maximum_fusion.refs_2_), channel_id=1, source_target_pairs={{0,16},{1,17},{2,18},{3,19},{4,20},{5,21},{6,22},{7,23},{8,24},{9,... | collective-permute-start | bytes 4718600 | tf_op jit(solution)/shard_map/ppermute | solution.py:405
  118.7 43.0 %collective-permute-start.27 = (bf16[3,256,1024]{2,1,0:T(8,128)(2,1)S(1)}, bf16[3,256,1024]{2,1,0:T(8,128)(2,1)}, u32[]{:S(2)}, u32[]{:S(2)}) collective-permute-start(bf16[3,256,1024]{2,1,0:T(8,128)(2,1)S(1)} %pad_maximum_fusion.refs_2_), channel_id=1, source_target_pairs={{0,8},{1,9},{2,10},{3,11},{4,12},{5,13},{6,14},{7,15},{8,0},{9,1},... | collective-permute-start | bytes 4718600 | tf_op jit(solution)/shard_map/ppermute | solution.py:405
  119.7 0.8 copy-start.3
  122.8 18.1 %copy-start = (bf16[64,8192]{1,0:T(8,128)(2,1)S(1)}, bf16[64,8192]{1,0:T(8,128)(2,1)}, u32[]{:S(2)}) copy-start(bf16[64,8192]{1,0:T(8,128)(2,1)} %shard_map.85.p_all.p_own) | copy-start | bytes 3145732
  133.5 1.6 collective-permute-start.19
  135.1 0.7 copy-start.7
  137.4 18.8 %collective-permute-start.22 = (f32[64,128]{1,0:T(8,128)}, f32[64,128]{1,0:T(8,128)S(1)}, u32[]{:S(2)}, u32[]{:S(2)}) collective-permute-start(f32[64,128]{1,0:T(8,128)} %get-tuple-element.151), channel_id=1, source_target_pairs={{0,24},{1,25},{2,26},{3,27},{4,28},{5,29},{6,30},{7,31},{8,16},{9,... | collective-permute-start | bytes 98312 | tf_op jit(solution)/shard_map/ppermute | solution.py:405
  138.9 17.3 %collective-permute-start.21 = (f32[64,128]{1,0:T(8,128)}, f32[64,128]{1,0:T(8,128)S(1)}, u32[]{:S(2)}, u32[]{:S(2)}) collective-permute-start(f32[64,128]{1,0:T(8,128)} %get-tuple-element.150), channel_id=1, source_target_pairs={{0,16},{1,17},{2,18},{3,19},{4,20},{5,21},{6,22},{7,23},{8,24},{9,... | collective-permute-start | bytes 98312 | tf_op jit(solution)/shard_map/ppermute | solution.py:405
  140.5 16.1 %collective-permute-start.20 = (f32[64,128]{1,0:T(8,128)}, f32[64,128]{1,0:T(8,128)S(1)}, u32[]{:S(2)}, u32[]{:S(2)}) collective-permute-start(f32[64,128]{1,0:T(8,128)} %get-tuple-element.149), channel_id=1, source_target_pairs={{0,8},{1,9},{2,10},{3,11},{4,12},{5,13},{6,14},{7,15},{8,0},{9,1},... | collective-permute-start | bytes 98312 | tf_op jit(solution)/shard_map/ppermute | solution.py:405
  156.8 0.6 copy-start.19
  158.9 4.5 %copy-start.6 = (f32[64,128]{1,0:T(8,128)S(1)}, f32[64,128]{1,0:T(8,128)}, u32[]{:S(2)}) copy-start(f32[64,128]{1,0:T(8,128)} %shard_map.88.refs_0_) | copy-start | bytes 98308
  160.1 23.7 %collective-permute-start.29 = (bf16[3,256,512]{2,1,0:T(8,128)(2,1)S(1)}, bf16[3,256,512]{2,1,0:T(8,128)(2,1)S(1)}, u32[]{:S(2)}, u32[]{:S(2)}) collective-permute-start(bf16[3,256,512]{2,1,0:T(8,128)(2,1)S(1)} %slice.23), channel_id=1, source_target_pairs={{0,8},{1,9},{2,10},{3,11},{4,12},{5,13},{6,14},{7,15},{8,0},{9,1},... | collective-permute-start | bytes 2359304 | tf_op jit(solution)/shard_map/ppermute | solution.py:405
  162.8 22.2 %collective-permute-start.28 = (bf16[3,256,512]{2,1,0:T(8,128)(2,1)S(1)}, bf16[3,256,512]{2,1,0:T(8,128)(2,1)S(1)}, u32[]{:S(2)}, u32[]{:S(2)}) collective-permute-start(bf16[3,256,512]{2,1,0:T(8,128)(2,1)S(1)} %slice.22), channel_id=1, source_target_pairs={{0,16},{1,17},{2,18},{3,19},{4,20},{5,21},{6,22},{7,23},{8,24},{9,... | collective-permute-start | bytes 2359304 | tf_op jit(solution)/shard_map/ppermute | solution.py:405
  163.3 7.3 %collective-permute-start.25 = (f32[64,128]{1,0:T(8,128)S(1)}, f32[64,128]{1,0:T(8,128)S(1)}, u32[]{:S(2)}, u32[]{:S(2)}) collective-permute-start(f32[64,128]{1,0:T(8,128)S(1)} %copy-done.6), channel_id=1, source_target_pairs={{0,2},{1,3},{2,0},{3,1},{4,6},{5,7},{6,4},{7,5},{8,10},{9,11},{10,... | collective-permute-start | bytes 98312 | tf_op jit(solution)/shard_map/ppermute | solution.py:405
  166.2 9.9 %collective-permute-start.24 = (f32[64,128]{1,0:T(8,128)S(1)}, f32[64,128]{1,0:T(8,128)S(1)}, u32[]{:S(2)}, u32[]{:S(2)}) collective-permute-start(f32[64,128]{1,0:T(8,128)S(1)} %copy-done.6), channel_id=1, source_target_pairs={{0,4},{1,5},{2,6},{3,7},{4,0},{5,1},{6,2},{7,3},{8,12},{9,13},{10,... | collective-permute-start | bytes 98312 | tf_op jit(solution)/shard_map/ppermute | solution.py:405
  166.7 9.4 %collective-permute-start.23 = (f32[64,128]{1,0:T(8,128)S(1)}, f32[64,128]{1,0:T(8,128)S(1)}, u32[]{:S(2)}, u32[]{:S(2)}) collective-permute-start(f32[64,128]{1,0:T(8,128)S(1)} %copy-done.6), channel_id=1, source_target_pairs={{0,6},{1,7},{2,4},{3,5},{4,2},{5,3},{6,0},{7,1},{8,14},{9,15},{10,... | collective-permute-start | bytes 98312 | tf_op jit(solution)/shard_map/ppermute | solution.py:405
  170.6 5.5 %copy-start.20 = (f32[64,128]{1,0:T(8,128)}, f32[64,128]{1,0:T(8,128)S(1)}, u32[]{:S(2)}) copy-start(f32[64,128]{1,0:T(8,128)S(1)} %collective-permute-done.25.refs_1_) | copy-start | bytes 98308
  178.7 5.0 %collective-permute-start.32 = (f32[64,128]{1,0:T(8,128)}, f32[64,128]{1,0:T(8,128)S(1)}, u32[]{:S(2)}, u32[]{:S(2)}) collective-permute-start(f32[64,128]{1,0:T(8,128)} %shard_map.89.refs_0_), channel_id=1, source_target_pairs={{0,24},{1,25},{2,26},{3,27},{4,28},{5,29},{6,30},{7,31},{8,16},{9,... | collective-permute-start | bytes 98312 | tf_op jit(solution)/shard_map/ppermute | solution.py:405
  180.9 17.9 %collective-permute-start.33 = (bf16[3,256,1024]{2,1,0:T(8,128)(2,1)S(1)}, bf16[3,256,1024]{2,1,0:T(8,128)(2,1)}, u32[]{:S(2)}, u32[]{:S(2)}) collective-permute-start(bf16[3,256,1024]{2,1,0:T(8,128)(2,1)S(1)} %pad_maximum_fusion.refs_2_), channel_id=1, source_target_pairs={{0,1},{1,0},{2,3},{3,2},{4,5},{5,4},{6,7},{7,6},{8,9},{9,8},{10,11... | collective-permute-start | bytes 4718600 | tf_op jit(solution)/shard_map/ppermute | solution.py:405
  180.9 17.9 %collective-permute-start.35 = (bf16[3,256,1024]{2,1,0:T(8,128)(2,1)}, bf16[3,256,1024]{2,1,0:T(8,128)(2,1)}, u32[]{:S(2)}, u32[]{:S(2)}) collective-permute-start(bf16[3,256,1024]{2,1,0:T(8,128)(2,1)} %collective-permute-done.26.refs_6_), channel_id=1, source_target_pairs={{0,1},{1,0},{2,3},{3,2},{4,5},{5,4},{6,7},{7,6},{8,9},{9,8},{10,11... | collective-permute-start | bytes 4718600 | tf_op jit(solution)/shard_map/ppermute | solution.py:405
  183.7 5.4 %copy-start.23 = (f32[64,128]{1,0:T(8,128)}, f32[64,128]{1,0:T(8,128)S(1)}, u32[]{:S(2)}) copy-start(f32[64,128]{1,0:T(8,128)S(1)} %collective-permute-done.32.refs_3_) | copy-start | bytes 98308
  183.7 15.1 %collective-permute-start.34 = (bf16[3,256,1024]{2,1,0:T(8,128)(2,1)}, bf16[3,256,1024]{2,1,0:T(8,128)(2,1)}, u32[]{:S(2)}, u32[]{:S(2)}) collective-permute-start(bf16[3,256,1024]{2,1,0:T(8,128)(2,1)} %collective-permute-done.27.refs_4_), channel_id=1, source_target_pairs={{0,1},{1,0},{2,3},{3,2},{4,5},{5,4},{6,7},{7,6},{8,9},{9,8},{10,11... | collective-permute-start | bytes 4718600 | tf_op jit(solution)/shard_map/ppermute | solution.py:405
  183.7 7.5 %copy-start.26 = (bf16[3,256,512]{2,1,0:T(8,128)(2,1)}, bf16[3,256,512]{2,1,0:T(8,128)(2,1)S(1)}, u32[]{:S(2)}) copy-start(bf16[3,256,512]{2,1,0:T(8,128)(2,1)S(1)} %collective-permute-done.29.refs_8_) | copy-start | bytes 2359300
  183.8 4.2 %collective-permute-start.31 = (f32[64,128]{1,0:T(8,128)}, f32[64,128]{1,0:T(8,128)S(1)}, u32[]{:S(2)}, u32[]{:S(2)}) collective-permute-start(f32[64,128]{1,0:T(8,128)} %shard_map.89.refs_0_), channel_id=1, source_target_pairs={{0,16},{1,17},{2,18},{3,19},{4,20},{5,21},{6,22},{7,23},{8,24},{9,... | collective-permute-start | bytes 98312 | tf_op jit(solution)/shard_map/ppermute | solution.py:405
  185.0 6.2 %copy-start.27 = (bf16[3,256,512]{2,1,0:T(8,128)(2,1)}, bf16[3,256,512]{2,1,0:T(8,128)(2,1)S(1)}, u32[]{:S(2)}) copy-start(bf16[3,256,512]{2,1,0:T(8,128)(2,1)S(1)} %collective-permute-done.28.refs_9_) | copy-start | bytes 2359300
  185.0 4.1 %collective-permute-start.30 = (f32[64,128]{1,0:T(8,128)}, f32[64,128]{1,0:T(8,128)S(1)}, u32[]{:S(2)}, u32[]{:S(2)}) collective-permute-start(f32[64,128]{1,0:T(8,128)} %shard_map.89.refs_0_), channel_id=1, source_target_pairs={{0,8},{1,9},{2,10},{3,11},{4,12},{5,13},{6,14},{7,15},{8,0},{9,1},... | collective-permute-start | bytes 98312 | tf_op jit(solution)/shard_map/ppermute | solution.py:405
  187.9 1.2 copy-start.24
  191.2 1.6 collective-permute-start.38
  191.3 7.5 %collective-permute-start.36 = (bf16[3,256,512]{2,1,0:T(8,128)(2,1)}, bf16[3,256,512]{2,1,0:T(8,128)(2,1)}, u32[]{:S(2)}, u32[]{:S(2)}) collective-permute-start(bf16[3,256,512]{2,1,0:T(8,128)(2,1)} %copy-done.26), channel_id=1, source_target_pairs={{0,1},{1,0},{2,3},{3,2},{4,5},{5,4},{6,7},{7,6},{8,9},{9,8},{10,11... | collective-permute-start | bytes 2359304 | tf_op jit(solution)/shard_map/ppermute | solution.py:405
  192.8 2.3 copy-start.5
  192.8 6.0 %collective-permute-start.37 = (bf16[3,256,512]{2,1,0:T(8,128)(2,1)}, bf16[3,256,512]{2,1,0:T(8,128)(2,1)}, u32[]{:S(2)}, u32[]{:S(2)}) collective-permute-start(bf16[3,256,512]{2,1,0:T(8,128)(2,1)} %copy-done.27), channel_id=1, source_target_pairs={{0,1},{1,0},{2,3},{3,2},{4,5},{5,4},{6,7},{7,6},{8,9},{9,8},{10,11... | collective-permute-start | bytes 2359304 | tf_op jit(solution)/shard_map/ppermute | solution.py:405
  (5 other events, 3.0 us)
Sparse Core Ops, SparseCore 0:
  41.9 63.0 reduce-scatter.4
  107.5 113.1 reduce-scatter.2

commit v4 on v3

--- a/solution.py
+++ b/solution.py
@@ -59,41 +59,59 @@
     )(scalars(c), cot, other_cot, tokens, other)
 
 
-def finish(scale, start, gradient, feedback, hat, q, result):
+def begin(scale, start, gradient, feedback, hat, q):
     tall, width = gradient.shape
-    rank = hat.shape[1]
+    rows, rank = hat.shape
     tile = math.gcd(start, tall)
-    tile = tile // 2 if tile > 512 else tile
-
-    def kernel(gradient, feedback, hat, q, *refs):
+    first, count = start // tile, tall // tile
+
+    def kernel(gradient, feedback, hat, q, result):
         top, low = split(hat[...])
         q_top, q_low = split(q[...])
         rank_part = times(top, q_top) + (times(top, q_low) + times(low, q_top))
-        refs[-1][...] = feedback[...] + (scale * gradient[...].astype(f32) - rank_part)
+        result[...] = feedback[...] - rank_part
+        step = pl.program_id(0)
+
+        @pl.when((step >= first) & (step < first + count))
+        def _():
+            result[...] += scale * gradient[...].astype(f32)
+
+    row = pl.BlockSpec((tile, width), lambda i: (i, 0))
+    return pl.pallas_call(
+        kernel,
+        grid=(rows // tile,),
+        in_specs=[
+            pl.BlockSpec((tile, width), lambda i: (jnp.clip(i - first, 0, count - 1), 0)),
+            row,
+            pl.BlockSpec((tile, rank), lambda i: (i, 0)),
+            whole(q.shape),
+        ],
+        out_specs=row,
+        out_shape=jax.ShapeDtypeStruct(feedback.shape, f32),
+        compiler_params=params(),
+        cost_estimate=cost(6 * rank * rows * width, 8 * rows * width),
+    )(gradient, feedback, hat, q)
+
+
+def finish(scale, start, gradient, base):
+    tall, width = gradient.shape
+    tile = math.gcd(start, tall)
+    tile = tile // 2 if tile > 512 else tile
+
+    def kernel(gradient, base, result):
+        result[...] = base[...] + scale * gradient[...].astype(f32)
 
     row = pl.BlockSpec((tile, width), lambda i: (start // tile + i, 0))
-    specs = [
-        pl.BlockSpec((tile, width), lambda i: (i, 0)),
-        row,
-        pl.BlockSpec((tile, rank), lambda i: (start // tile + i, 0)),
-        whole(q.shape),
-    ]
-    operands = [gradient, feedback, hat, q]
-    aliases = {}
-    if result is not None:
-        specs.append(pl.BlockSpec(memory_space=pl.ANY))
-        operands.append(result)
-        aliases = {4: 0}
     return pl.pallas_call(
         kernel,
         grid=(tall // tile,),
-        in_specs=specs,
+        in_specs=[pl.BlockSpec((tile, width), lambda i: (i, 0)), row],
         out_specs=row,
-        out_shape=jax.ShapeDtypeStruct(feedback.shape, f32),
-        input_output_aliases=aliases,
-        compiler_params=params(),
-        cost_estimate=cost(6 * rank * tall * width, 10 * tall * width),
-    )(*operands)
+        out_shape=jax.ShapeDtypeStruct(base.shape, f32),
+        input_output_aliases={1: 0},
+        compiler_params=params(),
+        cost_estimate=cost(tall * width, 10 * tall * width),
+    )(gradient, base)
 
 
 def split(value):
@@ -502,7 +520,10 @@
         hat, q = results["low_rank"]
         result = None
         for (start, _), part in zip(parts, summed):
-            result = finish(scale, start, part, feedback, hat, q, result)
+            if result is None:
+                result = begin(scale, start, part, feedback, hat, q)
+            else:
+                result = finish(scale, start, part, result)
             results["feedback"] = result
             yield
 

time: 233 us -> 232 us (level)
  waiting for transfers between devices: 52.9 us -> 49.3 us
  Pallas kernels: 88.1 us -> 90.9 us
    reduce_scatter x2, waiting for transfers between devices: 5.7 us -> 2.16 us  [gradient(): lax.psum_scatter(after(both), 'fsdp', scatter_dimension=0, axis_index_gro...]
    pallas_call x2, Pallas kernels: 7.44 us -> 10.2 us  [the longest x1 6.58 us: begin(): pl.pallas_call(kernel, grid=(rows // tile,), in_specs=[pl.BlockSpec((tile...]
  transfers between devices with their start and end apart: 41 -> 41, of which waited for: 20 -> 20; matrix products, arithmetic and copies ran while one was open for 10% -> 10% of each run, Pallas kernels for 36% -> 38%
where the time goes in v4:
time: 232 us; the launch traced here: 231 us
  Pallas kernels  90.9 us (39%)
  waiting for transfers between devices  49.3 us (21%)
  starting transfers between devices  44.4 us (19%)
  between operations  15 us (6%)
  other arithmetic  14.2 us (6%)
  local copies, waits for them, and re-layouts  13.4 us (6%)
  matrix products  3.94 us (2%)
    ppermute x34, waiting for transfers between devices, swap(): lax.ppermute(after(value), AXES, [(i, i ^ mask) for i in range(world)])  38.8 us
    ppermute x34, starting transfers between devices, swap(): lax.ppermute(after(value), AXES, [(i, i ^ mask) for i in range(world)])  34.8 us
    pallas_call x2, Pallas kernels, project(): pl.pallas_call(lambda *refs: project_kernel(parts, *refs), grid_spec=pltp...  20.2 us
    pallas_call x2, Pallas kernels, partials(): pl.pallas_call(kernel, grid_spec=pltpu.PrefetchScalarGridSpec(num_scalar_...  20.1 us
    pallas_call x10, Pallas kernels, on_core(): pl.pallas_call(kernel, grid_spec=pltpu.PrefetchScalarGridSpec(num_scalar_...  18.5 us
    pallas_call x1, Pallas kernels, right_part(): pl.pallas_call(kernel, grid_spec=pltpu.PrefetchScalarGridSpec(num_scalar_...  10.8 us
    ppermute x5, starting transfers between devices, along(): return lax.ppermute(after(value), AXES, moves)  9.45 us
    ppermute x5, waiting for transfers between devices, along(): return lax.ppermute(after(value), AXES, moves)  8.39 us
  transfers between devices with their start and end apart: 41, of which 20 were waited for; matrix products, arithmetic and copies ran while one was open for 10% of the time, Pallas kernels for 38%

profile of v4, /device:TPU:0, one launch (start us, length us, event | category | flops | bytes accessed | tf_op | source)
XLA Modules:
  0.0 231.1 jit_solution(4250745703324301836)
XLA Ops:
  8.2 1.1 constant_dynamic-slice_fusion
  10.0 5.5 %collective-permute-start = (bf16[256,1024]{1,0:T(8,128)(2,1)S(1)}, bf16[256,1024]{1,0:T(8,128)(2,1)S(1)}, u32[]{:S(2)}, u32[]{:S(2)}) collective-permute-start(bf16[256,1024]{1,0:T(8,128)(2,1)S(1)} %constant_dynamic-slice_fusion), channel_id=1, source_target_pairs={{0,2},{1,3},{4,6},{5,7},{2,0},{3,1},{6,4},{7,5},{8,10},{9,11},{12,... | collective-permute-start | bytes 1572872 | tf_op jit(solution)/shard_map/ppermute | solution.py:432
  15.5 4.4 %shard_map.76 = (bf16[64,4096]{1,0:T(8,128)(2,1)}, bf16[128,512]{1,0:T(8,128)(2,1)}) custom-call(s32[1]{0:T(128)} %bitcast.9.index, f32[64,1024]{1,0:T(8,128)} %bitcast.42, bf16[512,1024]{1,0:T(8,128)(2,1)} %refs_1_.1, bf16[512,8192]{1,0:T(8,128)(2,1)} %second.5, bf16[512,8192]{1,0:T(8,128)(2,1)} %second.5), custom_call_target="tpu_custom_call" | custom-call | flops 536870912 | bytes 4194304 | tf_op jit(solution)/shard_map/pallas_call | solution.py:154
  19.9 2.5 %collective-permute-done.3.other = bf16[512,8192]{1,0:T(8,128)(2,1)} collective-permute-done((bf16[512,8192]{1,0:T(8,128)(2,1)}, bf16[512,8192]{1,0:T(8,128)(2,1)}, u32[]{:S(2)}, u32[]{:S(2)}) %collective-permute-start.3) | collective-permute-done | bytes 8388640 | tf_op jit(solution)/shard_map/ppermute | solution.py:423
  22.4 3.0 %collective-permute-done.2 = bf16[1024,1024]{1,0:T(8,128)(2,1)} collective-permute-done((bf16[1024,1024]{1,0:T(8,128)(2,1)}, bf16[1024,1024]{1,0:T(8,128)(2,1)}, u32[]{:S(2)}, u32[]{:S(2)}) %collective-permute-start.2) | collective-permute-done | bytes 2097184 | tf_op jit(solution)/shard_map/ppermute | solution.py:423
  25.4 1.3 collective-permute-start.6
  26.6 1.1 collective-permute-done
  28.5 6.1 %shard_map.77 = bf16[1024,1024]{1,0:T(8,128)(2,1)} custom-call(s32[1]{0:T(128)} %bitcast.5.index, bf16[512,1024]{1,0:T(8,128)(2,1)} %refs_1_.1, bf16[512,1024]{1,0:T(8,128)(2,1)} %copy-done.1, bf16[512,8192]{1,0:T(8,128)(2,1)} %second.5, bf16[512,8192]{1,0:T(8,128)(2,1)} %collective-permute-done.3.other), custom_call_target="tpu_custom_call" | custom-call | flops 1 | bytes 1 | tf_op jit(solution)/shard_map/pallas_call | solution.py:48
  34.5 7.2 %collective-permute-done.6 = bf16[256,1024]{1,0:T(8,128)(2,1)S(1)} collective-permute-done((bf16[256,1024]{1,0:T(8,128)(2,1)S(1)}, bf16[256,1024]{1,0:T(8,128)(2,1)S(1)}, u32[]{:S(2)}, u32[]{:S(2)}) %collective-permute-start.6) | collective-permute-done | bytes 524320 | tf_op jit(solution)/shard_map/ppermute | solution.py:432
  42.5 1.3 collective-permute-start.11
  43.8 7.2 %shard_map.78 = (bf16[512,8192]{1,0:T(8,128)(2,1)}, s32[8,128]{1,0:T(8,128)}) custom-call(s32[1,2]{1,0:T(1,128)} %add_bitcast_fusion.refs_0_, bf16[512,1024]{1,0:T(8,128)(2,1)} %refs_1_.1, bf16[1,1024,1024]{2,1,0:T(8,128)(2,1)} %bitcast.46, bf16[1,1024,1024]{2,1,0:T(8,128)(2,1)} %bitcast.12.refs_3_), custom_call_target="tpu_custom_call" | custom-call | flops 2147483648 | bytes 6291456 | tf_op jit(solution)/shard_map/pallas_call | solution.py:379
  51.0 1.2 slice.19
  53.4 6.8 %shard_map.79.refs_0_ = f32[64,4096]{1,0:T(8,128)} custom-call(s32[2]{0:T(128)} %pad_add_fusion.2.index, f32[64,1024]{1,0:T(8,128)} %bitcast.43, bf16[128,512]{1,0:T(8,128)(2,1)} %get-tuple-element.105.factor, bf16[512,8192]{1,0:T(8,128)(2,1)} %second.5, bf16[512,8192]{1,0:T(8,128)(2,1)} %second.5, f32[1024,1024]{1,0:T(8,128)} %bitcast.38), custom_call_target="tpu_custom_call" | custom-call | flops 536870912 | bytes 8388608 | tf_op jit(solution)/shard_map/pallas_call | solution.py:204
  60.2 0.8 copy-done.4
  61.0 2.3 shard_map.80
  63.3 3.2 %collective-permute-start.10 = (bf16[64,1024]{1,0:T(8,128)(2,1)}, bf16[64,1024]{1,0:T(8,128)(2,1)S(1)}, u32[]{:S(2)}, u32[]{:S(2)}) collective-permute-start(bf16[64,1024]{1,0:T(8,128)(2,1)} %get-tuple-element.118), channel_id=1, source_target_pairs={{0,24},{1,25},{2,26},{3,27},{4,28},{5,29},{6,30},{7,31},{8,16},{9,... | collective-permute-start | bytes 393224 | tf_op jit(solution)/shard_map/ppermute | solution.py:423
  67.1 3.9 %collective-permute-done.10.refs_3_ = bf16[64,1024]{1,0:T(8,128)(2,1)S(1)} collective-permute-done((bf16[64,1024]{1,0:T(8,128)(2,1)}, bf16[64,1024]{1,0:T(8,128)(2,1)S(1)}, u32[]{:S(2)}, u32[]{:S(2)}) %collective-permute-start.10) | collective-permute-done | bytes 131104 | tf_op jit(solution)/shard_map/ppermute | solution.py:423
  71.0 2.7 %collective-permute-done.9.refs_2_ = bf16[64,1024]{1,0:T(8,128)(2,1)S(1)} collective-permute-done((bf16[64,1024]{1,0:T(8,128)(2,1)}, bf16[64,1024]{1,0:T(8,128)(2,1)S(1)}, u32[]{:S(2)}, u32[]{:S(2)}) %collective-permute-start.9) | collective-permute-done | bytes 131104 | tf_op jit(solution)/shard_map/ppermute | solution.py:423
  75.0 1.8 shard_map.81.refs_0_
  76.8 4.9 %collective-permute-start.14 = (bf16[64,1024]{1,0:T(8,128)(2,1)}, bf16[64,1024]{1,0:T(8,128)(2,1)S(1)}, u32[]{:S(2)}, u32[]{:S(2)}) collective-permute-start(bf16[64,1024]{1,0:T(8,128)(2,1)} %shard_map.81.refs_0_), channel_id=1, source_target_pairs={{0,2},{1,3},{2,0},{3,1},{4,6},{5,7},{6,4},{7,5},{8,10},{9,11},{10,... | collective-permute-start | bytes 393224 | tf_op jit(solution)/shard_map/ppermute | solution.py:423
  81.7 1.2 collective-permute-start.13
  82.9 1.5 collective-permute-start.12
  84.4 14.1 %shard_map.82 = bf16[3072,1024]{1,0:T(8,128)(2,1)} custom-call(s32[1]{0:T(128)} %bitcast.5.index, bf16[512,1024]{1,0:T(8,128)(2,1)} %refs_1_.1, bf16[512,1024]{1,0:T(8,128)(2,1)} %copy-done.1, bf16[512,8192]{1,0:T(8,128)(2,1)} %second.5, bf16[512,8192]{1,0:T(8,128)(2,1)} %collective-permute-done.3.other), custom_call_target="tpu_custom_call" | custom-call | flops 1 | bytes 1 | tf_op jit(solution)/shard_map/pallas_call | solution.py:48
  98.5 4.0 %collective-permute-done.12.refs_3_ = bf16[64,1024]{1,0:T(8,128)(2,1)S(1)} collective-permute-done((bf16[64,1024]{1,0:T(8,128)(2,1)}, bf16[64,1024]{1,0:T(8,128)(2,1)S(1)}, u32[]{:S(2)}, u32[]{:S(2)}) %collective-permute-start.12) | collective-permute-done | bytes 131104 | tf_op jit(solution)/shard_map/ppermute | solution.py:423
  103.4 2.4 %shard_map.83.refs_0_ = bf16[64,1024]{1,0:T(8,128)(2,1)} custom-call(s32[1]{0:T(128)} %constant.90.clone.1.index, bf16[64,1024]{1,0:T(8,128)(2,1)} %shard_map.81.refs_0_, bf16[64,1024]{1,0:T(8,128)(2,1)} %copy-done.8, bf16[64,1024]{1,0:T(8,128)(2,1)} %copy-done.9, bf16[64,1024]{1,0:T(8,128)(2,1)} %copy-done.10), custom_call_target="tpu_custom_call" | custom-call | flops 1 | bytes 524288 | tf_op jit(solution)/shard_map/pallas_call | solution.py:292
  106.5 1.8 collective-permute-start.16
  108.3 1.0 collective-permute-start.15
  109.3 3.9 %collective-permute-done.17.refs_3_ = bf16[64,1024]{1,0:T(8,128)(2,1)S(1)} collective-permute-done((bf16[64,1024]{1,0:T(8,128)(2,1)}, bf16[64,1024]{1,0:T(8,128)(2,1)S(1)}, u32[]{:S(2)}, u32[]{:S(2)}) %collective-permute-start.17) | collective-permute-done | bytes 131104 | tf_op jit(solution)/shard_map/ppermute | solution.py:423
  115.1 2.0 shard_map.84.refs_0_
  117.2 1.5 collective-permute-start.26
  119.7 0.8 copy-done.3
  120.5 2.3 shard_map.85.p_all.p_own
  122.8 10.8 %shard_map.86 = (f32[64,512]{1,0:T(8,128)}, f32[64,512]{1,0:T(8,128)}) custom-call(s32[2]{0:T(128)} %pad_add_fusion.1.index, bf16[64,8192]{1,0:T(8,128)(2,1)} %shard_map.85.p_all.p_own, bf16[64,8192]{1,0:T(8,128)(2,1)} %shard_map.85.p_all.p_own, bf16[512,8192]{1,0:T(8,128)(2,1)} %second.5, bf16[512,8192]{1,0:T(8,128)(2,1)} %second.5, ...), custom_call_target="tpu_custom_call" | custom-call | flops 536870912 | bytes 12582912 | tf_op jit(solution)/shard_map/pallas_call | solution.py:259
  133.5 1.6 collective-permute-done.19.refs_1_
  135.8 1.6 shard_map.87
  137.4 1.5 collective-permute-start.22
  138.9 1.6 collective-permute-start.21
  141.4 5.8 %cholesky.17 = f32[64,64]{1,0:T(8,128)S(1)} custom-call(f32[64,64]{1,0:T(8,128)S(1)} %fusion.5), custom_call_target="Cholesky" | custom-call | tf_op jit(solution)/shard_map/jit(cholesky)/cholesky | solution.py:549
  148.6 4.9 %custom-call.6 = f32[1,64,64]{1,2,0:T(8,128)S(1)} custom-call(f32[1,64,64]{2,1,0:T(8,128)S(1)} %fusion.2), custom_call_target="InvertDiagBlocksLowerTriangular" | custom-call | tf_op jit(solution)/shard_map/triangular_solve | solution.py:550
  153.7 2.5 %collective-permute-done.22.refs_3_ = f32[64,128]{1,0:T(8,128)S(1)} collective-permute-done((f32[64,128]{1,0:T(8,128)}, f32[64,128]{1,0:T(8,128)S(1)}, u32[]{:S(2)}, u32[]{:S(2)}) %collective-permute-start.22) | collective-permute-done | bytes 32800 | tf_op jit(solution)/shard_map/ppermute | solution.py:423
  157.4 1.4 shard_map.88.refs_0_
  158.9 1.2 slice.23
  160.1 1.6 collective-permute-start.29
  161.6 1.2 slice.22
  163.3 2.9 %collective-permute-start.25 = (f32[64,128]{1,0:T(8,128)S(1)}, f32[64,128]{1,0:T(8,128)S(1)}, u32[]{:S(2)}, u32[]{:S(2)}) collective-permute-start(f32[64,128]{1,0:T(8,128)S(1)} %copy-done.6), channel_id=1, source_target_pairs={{0,2},{1,3},{2,0},{3,1},{4,6},{5,7},{6,4},{7,5},{8,10},{9,11},{10,... | collective-permute-start | bytes 98312 | tf_op jit(solution)/shard_map/ppermute | solution.py:423
  166.7 1.9 collective-permute-start.23
  168.6 2.1 collective-permute-done.25.refs_1_
  170.6 5.4 %collective-permute-done.24.refs_2_ = f32[64,128]{1,0:T(8,128)S(1)} collective-permute-done((f32[64,128]{1,0:T(8,128)S(1)}, f32[64,128]{1,0:T(8,128)S(1)}, u32[]{:S(2)}, u32[]{:S(2)}) %collective-permute-start.24) | collective-permute-done | bytes 32800 | tf_op jit(solution)/shard_map/ppermute | solution.py:423
  177.3 1.4 shard_map.89.refs_0_
  178.7 2.2 collective-permute-start.32
  181.4 2.3 %collective-permute-done.32.refs_3_ = f32[64,128]{1,0:T(8,128)S(1)} collective-permute-done((f32[64,128]{1,0:T(8,128)}, f32[64,128]{1,0:T(8,128)S(1)}, u32[]{:S(2)}, u32[]{:S(2)}) %collective-permute-start.32) | collective-permute-done | bytes 32800 | tf_op jit(solution)/shard_map/ppermute | solution.py:423
  183.8 1.3 collective-permute-start.31
  185.0 1.6 collective-permute-start.30
  186.6 1.4 collective-permute-done.31.refs_2_
  187.9 1.2 collective-permute-done.30.refs_1_
  189.7 1.5 shard_map.90.refs_0_
  191.7 1.0 collective-permute-done.38.refs_1_
  193.8 1.3 fusion.hat
  195.1 1.7 shard_map.92
  196.8 2.0 convolution_multiply_fusion.q
  198.8 13.0 %shard_map.91 = (bf16[512,8192]{1,0:T(8,128)(2,1)}, s32[8,128]{1,0:T(8,128)}) custom-call(s32[3,8]{1,0:T(4,128)} %stack.77.refs_0_, bf16[512,1024]{1,0:T(8,128)(2,1)} %refs_1_.1, bf16[3,256,1024]{2,1,0:T(8,128)(2,1)} %copy-done.2, bf16[3,256,1024]{2,1,0:T(8,128)(2,1)} %collective-permute-done.33.refs_3_, ...), custom_call_target="tpu_custom_call", output_to_operand_aliasing={{0}: (12, {})} | custom-call | flops 6442450944 | bytes 18874368 | tf_op jit(solution)/shard_map/pallas_call | solution.py:379
  211.9 6.6 %shard_map.93.base = f32[1024,1024]{1,0:T(8,128)} custom-call(bf16[256,1024]{1,0:T(8,128)(2,1)} %reduce-scatter.5.cloned.1.call-done.gradient, f32[1024,1024]{1,0:T(8,128)} %bitcast.40, f32[1024,64]{1,0:T(8,128)} %fusion.hat, f32[64,1024]{1,0:T(8,128)} %convolution_multiply_fusion.q), custom_call_target="tpu_custom_call" | custom-call | flops 402653184 | bytes 8388608 | tf_op jit(solution)/shard_map/pallas_call | solution.py:80
  218.5 2.1 reduce-scatter.3.cloned.1.call-done.gradient
  220.6 3.7 %shard_map.94 = f32[1024,1024]{1,0:T(8,128)} custom-call(bf16[768,1024]{1,0:T(8,128)(2,1)} %reduce-scatter.3.cloned.1.call-done.gradient, f32[1024,1024]{1,0:T(8,128)} %shard_map.93.base), custom_call_target="tpu_custom_call", output_to_operand_aliasing={{}: (1, {})} | custom-call | flops 786432 | bytes 7864320 | tf_op jit(solution)/shard_map/pallas_call | solution.py:105
  (119 shorter events, 19.3 us)
Async XLA Ops:
  7.2 204.7 %reduce-scatter.5.cloned.1.call-start = ((), (), s32[]{:S(2)}) async-start(), calls=%async_computation.3 | async-start | bytes 2621440 | tf_op jit(solution)/shard_map/reduce_scatter | solution.py:515
  7.2 15.1 %collective-permute-start.3 = (bf16[512,8192]{1,0:T(8,128)(2,1)}, bf16[512,8192]{1,0:T(8,128)(2,1)}, u32[]{:S(2)}, u32[]{:S(2)}) collective-permute-start(bf16[512,8192]{1,0:T(8,128)(2,1)} %second.5), channel_id=1, source_target_pairs={{0,1},{1,0},{2,3},{3,2},{4,5},{5,4},{6,7},{7,6},{8,9},{9,8},{10,11... | collective-permute-start | bytes 25165832 | tf_op jit(solution)/shard_map/ppermute | solution.py:423
  7.7 17.6 %collective-permute-start.2 = (bf16[1024,1024]{1,0:T(8,128)(2,1)}, bf16[1024,1024]{1,0:T(8,128)(2,1)}, u32[]{:S(2)}, u32[]{:S(2)}) collective-permute-start(bf16[1024,1024]{1,0:T(8,128)(2,1)} %param.7), channel_id=1, source_target_pairs={{0,1},{1,0},{2,3},{3,2},{4,5},{5,4},{6,7},{7,6},{8,9},{9,8},{10,11... | collective-permute-start | bytes 6291464 | tf_op jit(solution)/shard_map/ppermute | solution.py:423
  7.8 12.1 %collective-permute-start.4 = (bf16[512,1024]{1,0:T(8,128)(2,1)}, bf16[512,1024]{1,0:T(8,128)(2,1)S(1)}, u32[]{:S(2)}, u32[]{:S(2)}) collective-permute-start(bf16[512,1024]{1,0:T(8,128)(2,1)} %refs_1_.1), channel_id=1, source_target_pairs={{0,1},{1,0},{2,3},{3,2},{4,5},{5,4},{6,7},{7,6},{8,9},{9,8},{10,11... | collective-permute-start | bytes 3145736 | tf_op jit(solution)/shard_map/ppermute | solution.py:423
  9.3 16.0 %collective-permute-start.1 = (bf16[256,1024]{1,0:T(8,128)(2,1)S(1)}, bf16[256,1024]{1,0:T(8,128)(2,1)S(1)}, u32[]{:S(2)}, u32[]{:S(2)}) collective-permute-start(bf16[256,1024]{1,0:T(8,128)(2,1)S(1)} %constant_dynamic-slice_fusion), channel_id=1, source_target_pairs={{2,4},{3,5},{4,2},{5,3},{10,12},{11,13},{12,10},{13,11},{18,20},{1... | collective-permute-start | bytes 1572872 | tf_op jit(solution)/shard_map/ppermute | solution.py:432
  10.0 17.8 %collective-permute-start = (bf16[256,1024]{1,0:T(8,128)(2,1)S(1)}, bf16[256,1024]{1,0:T(8,128)(2,1)S(1)}, u32[]{:S(2)}, u32[]{:S(2)}) collective-permute-start(bf16[256,1024]{1,0:T(8,128)(2,1)S(1)} %constant_dynamic-slice_fusion), channel_id=1, source_target_pairs={{0,2},{1,3},{4,6},{5,7},{2,0},{3,1},{6,4},{7,5},{8,10},{9,11},{12,... | collective-permute-start | bytes 1572872 | tf_op jit(solution)/shard_map/ppermute | solution.py:432
  19.9 8.6 %copy-start.1 = (bf16[512,1024]{1,0:T(8,128)(2,1)}, bf16[512,1024]{1,0:T(8,128)(2,1)S(1)}, u32[]{:S(2)}) copy-start(bf16[512,1024]{1,0:T(8,128)(2,1)S(1)} %collective-permute-done.4.other_cot) | copy-start | bytes 3145732
  25.4 16.4 %collective-permute-start.6 = (bf16[256,1024]{1,0:T(8,128)(2,1)S(1)}, bf16[256,1024]{1,0:T(8,128)(2,1)S(1)}, u32[]{:S(2)}, u32[]{:S(2)}) collective-permute-start(bf16[256,1024]{1,0:T(8,128)(2,1)S(1)} %collective-permute-done.1), channel_id=1, source_target_pairs={{4,6},{5,7},{2,0},{3,1},{12,14},{13,15},{10,8},{11,9},{20,22},{21,... | collective-permute-start | bytes 1572872 | tf_op jit(solution)/shard_map/ppermute | solution.py:432
  27.8 14.0 %collective-permute-start.5 = (bf16[256,1024]{1,0:T(8,128)(2,1)S(1)}, bf16[256,1024]{1,0:T(8,128)(2,1)S(1)}, u32[]{:S(2)}, u32[]{:S(2)}) collective-permute-start(bf16[256,1024]{1,0:T(8,128)(2,1)S(1)} %collective-permute-done), channel_id=1, source_target_pairs={{2,4},{3,5},{4,2},{5,3},{10,12},{11,13},{12,10},{13,11},{18,20},{1... | collective-permute-start | bytes 1572872 | tf_op jit(solution)/shard_map/ppermute | solution.py:432
  41.8 178.8 %reduce-scatter.3.cloned.1.call-start = ((), (), s32[]{:S(2)}) async-start(), calls=%async_computation.2 | async-start | bytes 7864320 | tf_op jit(solution)/shard_map/reduce_scatter | solution.py:515
  41.9 18.3 %collective-permute-start.7 = (bf16[64,4096]{1,0:T(8,128)(2,1)}, bf16[64,4096]{1,0:T(8,128)(2,1)S(1)}, u32[]{:S(2)}, u32[]{:S(2)}) collective-permute-start(bf16[64,4096]{1,0:T(8,128)(2,1)} %get-tuple-element.110), channel_id=1, source_target_pairs={{0,1},{1,0},{2,3},{3,2},{4,5},{5,4},{6,7},{7,6},{8,9},{9,8},{10,11... | collective-permute-start | bytes 1572872 | tf_op jit(solution)/shard_map/ppermute | solution.py:423
  42.5 59.9 %collective-permute-start.11 = (bf16[256,1024]{1,0:T(8,128)(2,1)S(1)}, bf16[256,1024]{1,0:T(8,128)(2,1)S(1)}, u32[]{:S(2)}, u32[]{:S(2)}) collective-permute-start(bf16[256,1024]{1,0:T(8,128)(2,1)S(1)} %collective-permute-done.5), channel_id=1, source_target_pairs={{4,6},{5,7},{2,0},{3,1},{12,14},{13,15},{10,8},{11,9},{20,22},{21,... | collective-permute-start | bytes 1572872 | tf_op jit(solution)/shard_map/ppermute | solution.py:432
  60.2 0.8 copy-start.4
  63.3 7.7 %collective-permute-start.10 = (bf16[64,1024]{1,0:T(8,128)(2,1)}, bf16[64,1024]{1,0:T(8,128)(2,1)S(1)}, u32[]{:S(2)}, u32[]{:S(2)}) collective-permute-start(bf16[64,1024]{1,0:T(8,128)(2,1)} %get-tuple-element.118), channel_id=1, source_target_pairs={{0,24},{1,25},{2,26},{3,27},{4,28},{5,29},{6,30},{7,31},{8,16},{9,... | collective-permute-start | bytes 393224 | tf_op jit(solution)/shard_map/ppermute | solution.py:423
  66.5 7.2 %collective-permute-start.9 = (bf16[64,1024]{1,0:T(8,128)(2,1)}, bf16[64,1024]{1,0:T(8,128)(2,1)S(1)}, u32[]{:S(2)}, u32[]{:S(2)}) collective-permute-start(bf16[64,1024]{1,0:T(8,128)(2,1)} %get-tuple-element.117), channel_id=1, source_target_pairs={{0,16},{1,17},{2,18},{3,19},{4,20},{5,21},{6,22},{7,23},{8,24},{9,... | collective-permute-start | bytes 393224 | tf_op jit(solution)/shard_map/ppermute | solution.py:423
  67.0 6.9 %collective-permute-start.8 = (bf16[64,1024]{1,0:T(8,128)(2,1)}, bf16[64,1024]{1,0:T(8,128)(2,1)S(1)}, u32[]{:S(2)}, u32[]{:S(2)}) collective-permute-start(bf16[64,1024]{1,0:T(8,128)(2,1)} %get-tuple-element.116), channel_id=1, source_target_pairs={{0,8},{1,9},{2,10},{3,11},{4,12},{5,13},{6,14},{7,15},{8,0},{9,1},... | collective-permute-start | bytes 393224 | tf_op jit(solution)/shard_map/ppermute | solution.py:423
  71.0 3.0 %copy-start.11 = (bf16[64,1024]{1,0:T(8,128)(2,1)}, bf16[64,1024]{1,0:T(8,128)(2,1)S(1)}, u32[]{:S(2)}) copy-start(bf16[64,1024]{1,0:T(8,128)(2,1)S(1)} %collective-permute-done.10.refs_3_) | copy-start | bytes 393220
  73.7 0.7 copy-start.12
  74.3 0.7 copy-start.13
  76.8 21.6 %collective-permute-start.14 = (bf16[64,1024]{1,0:T(8,128)(2,1)}, bf16[64,1024]{1,0:T(8,128)(2,1)S(1)}, u32[]{:S(2)}, u32[]{:S(2)}) collective-permute-start(bf16[64,1024]{1,0:T(8,128)(2,1)} %shard_map.81.refs_0_), channel_id=1, source_target_pairs={{0,2},{1,3},{2,0},{3,1},{4,6},{5,7},{6,4},{7,5},{8,10},{9,11},{10,... | collective-permute-start | bytes 393224 | tf_op jit(solution)/shard_map/ppermute | solution.py:423
  81.7 16.7 %collective-permute-start.13 = (bf16[64,1024]{1,0:T(8,128)(2,1)}, bf16[64,1024]{1,0:T(8,128)(2,1)S(1)}, u32[]{:S(2)}, u32[]{:S(2)}) collective-permute-start(bf16[64,1024]{1,0:T(8,128)(2,1)} %shard_map.81.refs_0_), channel_id=1, source_target_pairs={{0,4},{1,5},{2,6},{3,7},{4,0},{5,1},{6,2},{7,3},{8,12},{9,13},{10,... | collective-permute-start | bytes 393224 | tf_op jit(solution)/shard_map/ppermute | solution.py:423
  82.9 19.6 %collective-permute-start.12 = (bf16[64,1024]{1,0:T(8,128)(2,1)}, bf16[64,1024]{1,0:T(8,128)(2,1)S(1)}, u32[]{:S(2)}, u32[]{:S(2)}) collective-permute-start(bf16[64,1024]{1,0:T(8,128)(2,1)} %shard_map.81.refs_0_), channel_id=1, source_target_pairs={{0,6},{1,7},{2,4},{3,5},{4,2},{5,3},{6,0},{7,1},{8,14},{9,15},{10,... | collective-permute-start | bytes 393224 | tf_op jit(solution)/shard_map/ppermute | solution.py:423
  98.4 4.0 %copy-start.8 = (bf16[64,1024]{1,0:T(8,128)(2,1)}, bf16[64,1024]{1,0:T(8,128)(2,1)S(1)}, u32[]{:S(2)}) copy-start(bf16[64,1024]{1,0:T(8,128)(2,1)S(1)} %collective-permute-done.14.refs_1_) | copy-start | bytes 393220
  98.5 4.0 %copy-start.9 = (bf16[64,1024]{1,0:T(8,128)(2,1)}, bf16[64,1024]{1,0:T(8,128)(2,1)S(1)}, u32[]{:S(2)}) copy-start(bf16[64,1024]{1,0:T(8,128)(2,1)S(1)} %collective-permute-done.13.refs_2_) | copy-start | bytes 393220
  102.5 0.7 copy-start.10
  103.4 77.5 %copy-start.2 = (bf16[3,256,1024]{2,1,0:T(8,128)(2,1)}, bf16[3,256,1024]{2,1,0:T(8,128)(2,1)S(1)}, u32[]{:S(2)}) copy-start(bf16[3,256,1024]{2,1,0:T(8,128)(2,1)S(1)} %pad_maximum_fusion.refs_2_) | copy-start | bytes 4718596
  105.8 7.5 %collective-permute-start.17 = (bf16[64,1024]{1,0:T(8,128)(2,1)}, bf16[64,1024]{1,0:T(8,128)(2,1)S(1)}, u32[]{:S(2)}, u32[]{:S(2)}) collective-permute-start(bf16[64,1024]{1,0:T(8,128)(2,1)} %shard_map.83.refs_0_), channel_id=1, source_target_pairs={{0,24},{1,25},{2,26},{3,27},{4,28},{5,29},{6,30},{7,31},{8,16},{9,... | collective-permute-start | bytes 393224 | tf_op jit(solution)/shard_map/ppermute | solution.py:423
  106.5 7.3 %collective-permute-start.16 = (bf16[64,1024]{1,0:T(8,128)(2,1)}, bf16[64,1024]{1,0:T(8,128)(2,1)S(1)}, u32[]{:S(2)}, u32[]{:S(2)}) collective-permute-start(bf16[64,1024]{1,0:T(8,128)(2,1)} %shard_map.83.refs_0_), channel_id=1, source_target_pairs={{0,16},{1,17},{2,18},{3,19},{4,20},{5,21},{6,22},{7,23},{8,24},{9,... | collective-permute-start | bytes 393224 | tf_op jit(solution)/shard_map/ppermute | solution.py:423
  108.3 5.5 %collective-permute-start.15 = (bf16[64,1024]{1,0:T(8,128)(2,1)}, bf16[64,1024]{1,0:T(8,128)(2,1)S(1)}, u32[]{:S(2)}, u32[]{:S(2)}) collective-permute-start(bf16[64,1024]{1,0:T(8,128)(2,1)} %shard_map.83.refs_0_), channel_id=1, source_target_pairs={{0,8},{1,9},{2,10},{3,11},{4,12},{5,13},{6,14},{7,15},{8,0},{9,1},... | collective-permute-start | bytes 393224 | tf_op jit(solution)/shard_map/ppermute | solution.py:423
  113.3 0.7 copy-start.14
  113.8 0.7 copy-start.15
  114.5 0.7 copy-start.16
  117.2 2.5 %collective-permute-start.18 = (bf16[64,4096]{1,0:T(8,128)(2,1)}, bf16[64,4096]{1,0:T(8,128)(2,1)S(1)}, u32[]{:S(2)}, u32[]{:S(2)}) collective-permute-start(bf16[64,4096]{1,0:T(8,128)(2,1)} %shard_map.84.refs_0_), channel_id=1, source_target_pairs={{0,1},{1,0},{2,3},{3,2},{4,5},{5,4},{6,7},{7,6},{8,9},{9,8},{10,11... | collective-permute-start | bytes 1572872 | tf_op jit(solution)/shard_map/ppermute | solution.py:423
  117.2 41.7 %collective-permute-start.26 = (bf16[3,256,1024]{2,1,0:T(8,128)(2,1)S(1)}, bf16[3,256,1024]{2,1,0:T(8,128)(2,1)}, u32[]{:S(2)}, u32[]{:S(2)}) collective-permute-start(bf16[3,256,1024]{2,1,0:T(8,128)(2,1)S(1)} %pad_maximum_fusion.refs_2_), channel_id=1, source_target_pairs={{0,16},{1,17},{2,18},{3,19},{4,20},{5,21},{6,22},{7,23},{8,24},{9,... | collective-permute-start | bytes 4718600 | tf_op jit(solution)/shard_map/ppermute | solution.py:423
  118.7 43.0 %collective-permute-start.27 = (bf16[3,256,1024]{2,1,0:T(8,128)(2,1)S(1)}, bf16[3,256,1024]{2,1,0:T(8,128)(2,1)}, u32[]{:S(2)}, u32[]{:S(2)}) collective-permute-start(bf16[3,256,1024]{2,1,0:T(8,128)(2,1)S(1)} %pad_maximum_fusion.refs_2_), channel_id=1, source_target_pairs={{0,8},{1,9},{2,10},{3,11},{4,12},{5,13},{6,14},{7,15},{8,0},{9,1},... | collective-permute-start | bytes 4718600 | tf_op jit(solution)/shard_map/ppermute | solution.py:423
  119.7 0.8 copy-start.3
  122.8 18.1 %copy-start = (bf16[64,8192]{1,0:T(8,128)(2,1)S(1)}, bf16[64,8192]{1,0:T(8,128)(2,1)}, u32[]{:S(2)}) copy-start(bf16[64,8192]{1,0:T(8,128)(2,1)} %shard_map.85.p_all.p_own) | copy-start | bytes 3145732
  133.5 1.6 collective-permute-start.19
  135.1 0.7 copy-start.7
  137.4 18.8 %collective-permute-start.22 = (f32[64,128]{1,0:T(8,128)}, f32[64,128]{1,0:T(8,128)S(1)}, u32[]{:S(2)}, u32[]{:S(2)}) collective-permute-start(f32[64,128]{1,0:T(8,128)} %get-tuple-element.151), channel_id=1, source_target_pairs={{0,24},{1,25},{2,26},{3,27},{4,28},{5,29},{6,30},{7,31},{8,16},{9,... | collective-permute-start | bytes 98312 | tf_op jit(solution)/shard_map/ppermute | solution.py:423
  138.9 17.3 %collective-permute-start.21 = (f32[64,128]{1,0:T(8,128)}, f32[64,128]{1,0:T(8,128)S(1)}, u32[]{:S(2)}, u32[]{:S(2)}) collective-permute-start(f32[64,128]{1,0:T(8,128)} %get-tuple-element.150), channel_id=1, source_target_pairs={{0,16},{1,17},{2,18},{3,19},{4,20},{5,21},{6,22},{7,23},{8,24},{9,... | collective-permute-start | bytes 98312 | tf_op jit(solution)/shard_map/ppermute | solution.py:423
  140.5 16.1 %collective-permute-start.20 = (f32[64,128]{1,0:T(8,128)}, f32[64,128]{1,0:T(8,128)S(1)}, u32[]{:S(2)}, u32[]{:S(2)}) collective-permute-start(f32[64,128]{1,0:T(8,128)} %get-tuple-element.149), channel_id=1, source_target_pairs={{0,8},{1,9},{2,10},{3,11},{4,12},{5,13},{6,14},{7,15},{8,0},{9,1},... | collective-permute-start | bytes 98312 | tf_op jit(solution)/shard_map/ppermute | solution.py:423
  156.8 0.6 copy-start.19
  158.9 4.5 %copy-start.6 = (f32[64,128]{1,0:T(8,128)S(1)}, f32[64,128]{1,0:T(8,128)}, u32[]{:S(2)}) copy-start(f32[64,128]{1,0:T(8,128)} %shard_map.88.refs_0_) | copy-start | bytes 98308
  160.1 23.7 %collective-permute-start.29 = (bf16[3,256,512]{2,1,0:T(8,128)(2,1)S(1)}, bf16[3,256,512]{2,1,0:T(8,128)(2,1)S(1)}, u32[]{:S(2)}, u32[]{:S(2)}) collective-permute-start(bf16[3,256,512]{2,1,0:T(8,128)(2,1)S(1)} %slice.23), channel_id=1, source_target_pairs={{0,8},{1,9},{2,10},{3,11},{4,12},{5,13},{6,14},{7,15},{8,0},{9,1},... | collective-permute-start | bytes 2359304 | tf_op jit(solution)/shard_map/ppermute | solution.py:423
  162.8 22.2 %collective-permute-start.28 = (bf16[3,256,512]{2,1,0:T(8,128)(2,1)S(1)}, bf16[3,256,512]{2,1,0:T(8,128)(2,1)S(1)}, u32[]{:S(2)}, u32[]{:S(2)}) collective-permute-start(bf16[3,256,512]{2,1,0:T(8,128)(2,1)S(1)} %slice.22), channel_id=1, source_target_pairs={{0,16},{1,17},{2,18},{3,19},{4,20},{5,21},{6,22},{7,23},{8,24},{9,... | collective-permute-start | bytes 2359304 | tf_op jit(solution)/shard_map/ppermute | solution.py:423
  163.3 7.3 %collective-permute-start.25 = (f32[64,128]{1,0:T(8,128)S(1)}, f32[64,128]{1,0:T(8,128)S(1)}, u32[]{:S(2)}, u32[]{:S(2)}) collective-permute-start(f32[64,128]{1,0:T(8,128)S(1)} %copy-done.6), channel_id=1, source_target_pairs={{0,2},{1,3},{2,0},{3,1},{4,6},{5,7},{6,4},{7,5},{8,10},{9,11},{10,... | collective-permute-start | bytes 98312 | tf_op jit(solution)/shard_map/ppermute | solution.py:423
  166.2 9.9 %collective-permute-start.24 = (f32[64,128]{1,0:T(8,128)S(1)}, f32[64,128]{1,0:T(8,128)S(1)}, u32[]{:S(2)}, u32[]{:S(2)}) collective-permute-start(f32[64,128]{1,0:T(8,128)S(1)} %copy-done.6), channel_id=1, source_target_pairs={{0,4},{1,5},{2,6},{3,7},{4,0},{5,1},{6,2},{7,3},{8,12},{9,13},{10,... | collective-permute-start | bytes 98312 | tf_op jit(solution)/shard_map/ppermute | solution.py:423
  166.7 9.4 %collective-permute-start.23 = (f32[64,128]{1,0:T(8,128)S(1)}, f32[64,128]{1,0:T(8,128)S(1)}, u32[]{:S(2)}, u32[]{:S(2)}) collective-permute-start(f32[64,128]{1,0:T(8,128)S(1)} %copy-done.6), channel_id=1, source_target_pairs={{0,6},{1,7},{2,4},{3,5},{4,2},{5,3},{6,0},{7,1},{8,14},{9,15},{10,... | collective-permute-start | bytes 98312 | tf_op jit(solution)/shard_map/ppermute | solution.py:423
  170.6 5.5 %copy-start.20 = (f32[64,128]{1,0:T(8,128)}, f32[64,128]{1,0:T(8,128)S(1)}, u32[]{:S(2)}) copy-start(f32[64,128]{1,0:T(8,128)S(1)} %collective-permute-done.25.refs_1_) | copy-start | bytes 98308
  178.7 5.0 %collective-permute-start.32 = (f32[64,128]{1,0:T(8,128)}, f32[64,128]{1,0:T(8,128)S(1)}, u32[]{:S(2)}, u32[]{:S(2)}) collective-permute-start(f32[64,128]{1,0:T(8,128)} %shard_map.89.refs_0_), channel_id=1, source_target_pairs={{0,24},{1,25},{2,26},{3,27},{4,28},{5,29},{6,30},{7,31},{8,16},{9,... | collective-permute-start | bytes 98312 | tf_op jit(solution)/shard_map/ppermute | solution.py:423
  180.9 17.9 %collective-permute-start.33 = (bf16[3,256,1024]{2,1,0:T(8,128)(2,1)S(1)}, bf16[3,256,1024]{2,1,0:T(8,128)(2,1)}, u32[]{:S(2)}, u32[]{:S(2)}) collective-permute-start(bf16[3,256,1024]{2,1,0:T(8,128)(2,1)S(1)} %pad_maximum_fusion.refs_2_), channel_id=1, source_target_pairs={{0,1},{1,0},{2,3},{3,2},{4,5},{5,4},{6,7},{7,6},{8,9},{9,8},{10,11... | collective-permute-start | bytes 4718600 | tf_op jit(solution)/shard_map/ppermute | solution.py:423
  180.9 17.9 %collective-permute-start.35 = (bf16[3,256,1024]{2,1,0:T(8,128)(2,1)}, bf16[3,256,1024]{2,1,0:T(8,128)(2,1)}, u32[]{:S(2)}, u32[]{:S(2)}) collective-permute-start(bf16[3,256,1024]{2,1,0:T(8,128)(2,1)} %collective-permute-done.26.refs_6_), channel_id=1, source_target_pairs={{0,1},{1,0},{2,3},{3,2},{4,5},{5,4},{6,7},{7,6},{8,9},{9,8},{10,11... | collective-permute-start | bytes 4718600 | tf_op jit(solution)/shard_map/ppermute | solution.py:423
  183.7 5.4 %copy-start.23 = (f32[64,128]{1,0:T(8,128)}, f32[64,128]{1,0:T(8,128)S(1)}, u32[]{:S(2)}) copy-start(f32[64,128]{1,0:T(8,128)S(1)} %collective-permute-done.32.refs_3_) | copy-start | bytes 98308
  183.7 15.1 %collective-permute-start.34 = (bf16[3,256,1024]{2,1,0:T(8,128)(2,1)}, bf16[3,256,1024]{2,1,0:T(8,128)(2,1)}, u32[]{:S(2)}, u32[]{:S(2)}) collective-permute-start(bf16[3,256,1024]{2,1,0:T(8,128)(2,1)} %collective-permute-done.27.refs_4_), channel_id=1, source_target_pairs={{0,1},{1,0},{2,3},{3,2},{4,5},{5,4},{6,7},{7,6},{8,9},{9,8},{10,11... | collective-permute-start | bytes 4718600 | tf_op jit(solution)/shard_map/ppermute | solution.py:423
  183.7 7.5 %copy-start.26 = (bf16[3,256,512]{2,1,0:T(8,128)(2,1)}, bf16[3,256,512]{2,1,0:T(8,128)(2,1)S(1)}, u32[]{:S(2)}) copy-start(bf16[3,256,512]{2,1,0:T(8,128)(2,1)S(1)} %collective-permute-done.29.refs_8_) | copy-start | bytes 2359300
  183.8 4.2 %collective-permute-start.31 = (f32[64,128]{1,0:T(8,128)}, f32[64,128]{1,0:T(8,128)S(1)}, u32[]{:S(2)}, u32[]{:S(2)}) collective-permute-start(f32[64,128]{1,0:T(8,128)} %shard_map.89.refs_0_), channel_id=1, source_target_pairs={{0,16},{1,17},{2,18},{3,19},{4,20},{5,21},{6,22},{7,23},{8,24},{9,... | collective-permute-start | bytes 98312 | tf_op jit(solution)/shard_map/ppermute | solution.py:423
  185.0 6.2 %copy-start.27 = (bf16[3,256,512]{2,1,0:T(8,128)(2,1)}, bf16[3,256,512]{2,1,0:T(8,128)(2,1)S(1)}, u32[]{:S(2)}) copy-start(bf16[3,256,512]{2,1,0:T(8,128)(2,1)S(1)} %collective-permute-done.28.refs_9_) | copy-start | bytes 2359300
  185.0 4.1 %collective-permute-start.30 = (f32[64,128]{1,0:T(8,128)}, f32[64,128]{1,0:T(8,128)S(1)}, u32[]{:S(2)}, u32[]{:S(2)}) collective-permute-start(f32[64,128]{1,0:T(8,128)} %shard_map.89.refs_0_), channel_id=1, source_target_pairs={{0,8},{1,9},{2,10},{3,11},{4,12},{5,13},{6,14},{7,15},{8,0},{9,1},... | collective-permute-start | bytes 98312 | tf_op jit(solution)/shard_map/ppermute | solution.py:423
  187.9 1.2 copy-start.24
  191.2 1.6 collective-permute-start.38
  191.3 7.5 %collective-permute-start.36 = (bf16[3,256,512]{2,1,0:T(8,128)(2,1)}, bf16[3,256,512]{2,1,0:T(8,128)(2,1)}, u32[]{:S(2)}, u32[]{:S(2)}) collective-permute-start(bf16[3,256,512]{2,1,0:T(8,128)(2,1)} %copy-done.26), channel_id=1, source_target_pairs={{0,1},{1,0},{2,3},{3,2},{4,5},{5,4},{6,7},{7,6},{8,9},{9,8},{10,11... | collective-permute-start | bytes 2359304 | tf_op jit(solution)/shard_map/ppermute | solution.py:423
  192.8 2.3 copy-start.5
  192.8 6.0 %collective-permute-start.37 = (bf16[3,256,512]{2,1,0:T(8,128)(2,1)}, bf16[3,256,512]{2,1,0:T(8,128)(2,1)}, u32[]{:S(2)}, u32[]{:S(2)}) collective-permute-start(bf16[3,256,512]{2,1,0:T(8,128)(2,1)} %copy-done.27), channel_id=1, source_target_pairs={{0,1},{1,0},{2,3},{3,2},{4,5},{5,4},{6,7},{7,6},{8,9},{9,8},{10,11... | collective-permute-start | bytes 2359304 | tf_op jit(solution)/shard_map/ppermute | solution.py:423
  (5 other events, 3.0 us)
Sparse Core Ops, SparseCore 0:
  41.9 63.0 reduce-scatter.4
  107.5 113.1 reduce-scatter.2
